TPU v7x, 32 devices: a whole 2x2x4 slice. The times are simulated.
32 devices in a mesh: dp: 16 (over z, x, core), tensor: 2 (over y).
Axes of the slice: x: 2, y: 2, z: 4, core: 2. Of those that a mesh axis runs over, the one named last changes fastest.
Arguments:
- tokens: bfloat16 [87680, 1024], P(('dp', 'tensor')), may hold values from -6 to 6
- cotangent: bfloat16 [87680, 1024], P(('dp', 'tensor')), may hold values from -12 to 12
- attention_gain: bfloat16 [1024], P('dp'), may hold values from 0.5 to 1.5
- attention_shift: bfloat16 [1024], P('dp'), may hold values from -1.75 to 1.75
- triple_weight: bfloat16 [1024, 3, 1024], P('dp', None, 'tensor'), may hold values from -0.25 to 0.25
- query_bias: bfloat16 [1024], P('dp'), may hold values from -3 to 3
- value_bias: bfloat16 [1024], P('dp'), may hold values from -3 to 3
- merge_weight: bfloat16 [1024, 1024], P('dp', 'tensor'), may hold values from -0.75 to 0.75
- merge_bias: bfloat16 [1024], P('dp'), may hold values from -1.75 to 1.75
- attention_scale: bfloat16 [1024], P('dp'), may hold values from 0.25 to 1.75
- forward_gain: bfloat16 [1024], P('dp'), may hold values from 0.5 to 1.5
- forward_shift: bfloat16 [1024], P('dp'), may hold values from -1.75 to 1.75
- expand_weight: bfloat16 [1024, 4096], P('dp', 'tensor'), may hold values from -0.1875 to 0.1875
- expand_bias: bfloat16 [4096], P('dp'), may hold values from -3 to 3
- reduce_weight: bfloat16 [1024, 4096], P('dp', 'tensor'), may hold values from -0.1875 to 0.1875
- reduce_bias: bfloat16 [1024], P('dp'), may hold values from -1.75 to 1.75
- forward_scale: bfloat16 [1024], P('dp'), may hold values from 0.25 to 1.75
Outputs:
- result: bfloat16 [87680, 1024], P(('dp', 'tensor'))
- tokens_gradient: bfloat16 [87680, 1024], P(('dp', 'tensor'))
- attention_gain_gradient: float32 [1024], P('dp')
- attention_shift_gradient: float32 [1024], P('dp')
- triple_weight_gradient: float32 [1024, 3, 1024], P('dp', None, 'tensor')
- query_bias_gradient: float32 [1024], P('dp')
- value_bias_gradient: float32 [1024], P('dp')
- merge_weight_gradient: float32 [1024, 1024], P('dp', 'tensor')
- merge_bias_gradient: float32 [1024], P('dp')
- attention_scale_gradient: float32 [1024], P('dp')
- forward_gain_gradient: float32 [1024], P('dp')
- forward_shift_gradient: float32 [1024], P('dp')
- expand_weight_gradient: float32 [1024, 4096], P('dp', 'tensor')
- expand_bias_gradient: float32 [4096], P('dp')
- reduce_weight_gradient: float32 [1024, 4096], P('dp', 'tensor')
- reduce_bias_gradient: float32 [1024], P('dp')
- forward_scale_gradient: float32 [1024], P('dp')
All inputs are finite; a program needn't handle non-finite values.
Results may differ from a plain program's by a relative error of at most 0.022.
Values may be sent and summed in bfloat16 or wider, within the bound.
No kernel may reach another device: no remote copies, remote signals or barrier semaphores. Data moves between devices by JAX's collectives and lax.ppermute only.
A program may use at most 448 MiB of HBM per device.

v0:
```python
import jax
import jax.numpy as jnp
from jax import lax
from jax.sharding import PartitionSpec as P

HD = 64
SEQ = 1370


def layer_norm(values, gain, shift):
    centre = jnp.mean(values, axis=-1, keepdims=True)
    centred = values - centre
    spread = jnp.mean(centred * centred, axis=-1, keepdims=True)
    return centred * lax.rsqrt(spread + 1e-06) * gain + shift


def smooth_gate(values):
    return jax.nn.gelu(values, approximate=False)


def attend_forward(block):
    queries, keys, values = block
    scores = jnp.einsum("qhd,khd->hqk", queries, keys, preferred_element_type=jnp.float32) * HD ** (
        -0.5
    )
    peak = jnp.max(scores, axis=-1, keepdims=True)
    weights = jnp.exp(scores - peak)
    total = jnp.sum(weights, axis=-1, keepdims=True)
    probs = (weights / total).astype(jnp.bfloat16)
    mixed = jnp.einsum("hqk,khd->qhd", probs, values, preferred_element_type=jnp.float32)
    return (mixed.astype(jnp.bfloat16), (peak + jnp.log(total))[..., 0])


def attend_backward(block):
    queries, keys, values, mixed_grad, logsum = block
    factor = HD ** (-0.5)
    scores = jnp.einsum("qhd,khd->hqk", queries, keys, preferred_element_type=jnp.float32) * factor
    probs = jnp.exp(scores - logsum[..., None])
    value_grad = jnp.einsum(
        "hqk,qhd->khd", probs.astype(jnp.bfloat16), mixed_grad, preferred_element_type=jnp.float32
    )
    prob_grad = jnp.einsum("qhd,khd->hqk", mixed_grad, values, preferred_element_type=jnp.float32)
    row_term = jnp.sum(prob_grad * probs, axis=-1, keepdims=True)
    score_grad = (probs * (prob_grad - row_term)).astype(jnp.bfloat16)
    query_grad = (
        jnp.einsum("hqk,khd->qhd", score_grad, keys, preferred_element_type=jnp.float32) * factor
    )
    key_grad = (
        jnp.einsum("hqk,qhd->khd", score_grad, queries, preferred_element_type=jnp.float32) * factor
    )
    return jnp.stack([query_grad, key_grad, value_grad], axis=1).astype(jnp.bfloat16)


def body(
    tokens,
    cotangent,
    attention_gain,
    attention_shift,
    triple_weight,
    query_bias,
    value_bias,
    merge_weight,
    merge_bias,
    attention_scale,
    forward_gain,
    forward_shift,
    expand_weight,
    expand_bias,
    reduce_weight,
    reduce_bias,
    forward_scale,
):
    stacked = jnp.stack(
        [
            attention_gain,
            attention_shift,
            query_bias,
            value_bias,
            merge_bias,
            attention_scale,
            forward_gain,
            forward_shift,
            reduce_bias,
            forward_scale,
        ]
    )
    triple_full, merge_full, stacked_full = (
        lax.all_gather(triple_weight, "dp", axis=0, tiled=True),
        lax.all_gather(merge_weight, "dp", axis=0, tiled=True),
        lax.all_gather(stacked, "dp", axis=1, tiled=True),
    )
    vectors = stacked_full.astype(jnp.float32)
    (
        gain_one,
        shift_one,
        query_shift,
        value_shift,
        merge_shift,
        scale_one,
        gain_two,
        shift_two,
        reduce_shift,
        scale_two,
    ) = [vectors[index] for index in range(10)]
    rank = lax.axis_index("tensor")
    local_width = triple_full.shape[2]
    offset = rank * local_width
    bias_rows = jnp.stack(
        [
            lax.dynamic_slice_in_dim(query_shift, offset, local_width),
            jnp.zeros((local_width,), jnp.float32),
            lax.dynamic_slice_in_dim(value_shift, offset, local_width),
        ]
    )
    inputs = tokens.astype(jnp.float32)
    normed_one, pull_one = jax.vjp(layer_norm, inputs, gain_one, shift_one)
    rows_one = lax.all_gather(normed_one.astype(jnp.bfloat16), "tensor", axis=0, tiled=True)
    group = rows_one.shape[0]
    images = group // SEQ
    heads = local_width // HD
    triple = (
        jnp.einsum("rd,dcf->rcf", rows_one, triple_full, preferred_element_type=jnp.float32)
        + bias_rows
    )
    shaped = triple.astype(jnp.bfloat16).reshape(images, SEQ, 3, heads, HD)
    queries = shaped[:, :, 0]
    keys = shaped[:, :, 1]
    values = shaped[:, :, 2]
    mixed, logsum = lax.map(attend_forward, (queries, keys, values))
    mixed_rows = mixed.reshape(group, local_width)
    merge_terms_all = jnp.einsum(
        "rf,of->ro", mixed_rows, merge_full, preferred_element_type=jnp.float32
    )
    attention_out = lax.psum_scatter(merge_terms_all, "tensor", scatter_dimension=0, tiled=True)
    expand_part, reduce_part, expand_shift = (
        lax.all_gather(expand_weight, "dp", axis=0, tiled=True),
        lax.all_gather(reduce_weight, "dp", axis=0, tiled=True),
        lax.all_gather(expand_bias, "dp", axis=0, tiled=True),
    )
    expand_shift = expand_shift.astype(jnp.float32)
    branch_one = attention_out + merge_shift
    middle = inputs + scale_one * branch_one
    normed_two, pull_two = jax.vjp(layer_norm, middle, gain_two, shift_two)
    sent_two = normed_two.astype(jnp.bfloat16)
    upstream = cotangent.astype(jnp.float32)
    back_two = (upstream * scale_two).astype(jnp.bfloat16)
    hidden_width = expand_part.shape[1]
    hidden_start = rank * hidden_width
    rows_two = lax.all_gather(sent_two, "tensor", axis=0, tiled=True)
    gate_input = jnp.dot(
        rows_two, expand_part, preferred_element_type=jnp.float32
    ) + lax.dynamic_slice_in_dim(expand_shift, hidden_start, hidden_width)
    activated, pull_gate = jax.vjp(smooth_gate, gate_input)
    activated = activated.astype(jnp.bfloat16)
    reduce_terms_all = jnp.einsum(
        "rf,of->ro", activated, reduce_part, preferred_element_type=jnp.float32
    )
    branch_two = (
        lax.psum_scatter(
            reduce_terms_all.astype(jnp.bfloat16), "tensor", scatter_dimension=0, tiled=True
        ).astype(jnp.float32)
        + reduce_shift
    )
    back_rows = lax.all_gather(back_two, "tensor", axis=0, tiled=True)
    back_hidden = jnp.einsum(
        "ro,of->rf", back_rows, reduce_part, preferred_element_type=jnp.float32
    )
    gate_grad = pull_gate(back_hidden)[0].astype(jnp.bfloat16)
    reduce_grad = jnp.einsum("ro,rf->of", back_rows, activated, preferred_element_type=jnp.float32)
    expand_grad = jnp.einsum("rd,rf->df", rows_two, gate_grad, preferred_element_type=jnp.float32)
    expand_shift_grad = lax.dynamic_update_slice_in_dim(
        jnp.zeros(expand_shift.shape, jnp.float32),
        jnp.sum(gate_grad, axis=0, dtype=jnp.float32),
        hidden_start,
        0,
    )
    expand_terms_all = jnp.einsum(
        "rf,df->rd", gate_grad, expand_part, preferred_element_type=jnp.float32
    )
    normed_two_grad = lax.psum_scatter(
        expand_terms_all.astype(jnp.bfloat16), "tensor", scatter_dimension=0, tiled=True
    ).astype(jnp.float32)
    result = (middle + scale_two * branch_two).astype(jnp.bfloat16)
    reduce_shift_grad = jnp.sum(upstream * scale_two, axis=0)
    scale_two_grad = jnp.sum(upstream * branch_two, axis=0)
    middle_part, gain_two_grad, shift_two_grad = pull_two(normed_two_grad)
    middle_grad = upstream + middle_part
    merge_shift_grad = jnp.sum(middle_grad * scale_one, axis=0)
    scale_one_grad = jnp.sum(middle_grad * branch_one, axis=0)
    back_one = (middle_grad * scale_one).astype(jnp.bfloat16)
    back_rows_one = lax.all_gather(back_one, "tensor", axis=0, tiled=True)
    mixed_grad = jnp.einsum(
        "ro,of->rf", back_rows_one, merge_full, preferred_element_type=jnp.float32
    ).astype(jnp.bfloat16)
    merge_grad = jnp.einsum(
        "ro,rf->of", back_rows_one, mixed_rows, preferred_element_type=jnp.float32
    )
    triple_grad = lax.map(
        attend_backward, (queries, keys, values, mixed_grad.reshape(images, SEQ, heads, HD), logsum)
    )
    triple_grad = triple_grad.reshape(group, 3, local_width)
    triple_weight_grad = jnp.einsum(
        "rd,rcf->dcf", rows_one, triple_grad, preferred_element_type=jnp.float32
    )
    bias_sums = jnp.sum(triple_grad, axis=0, dtype=jnp.float32)
    empty_row = jnp.zeros(query_shift.shape, jnp.float32)
    query_shift_grad = lax.dynamic_update_slice_in_dim(empty_row, bias_sums[0], offset, 0)
    value_shift_grad = lax.dynamic_update_slice_in_dim(empty_row, bias_sums[2], offset, 0)
    triple_terms_all = jnp.einsum(
        "rcf,dcf->rd", triple_grad, triple_full, preferred_element_type=jnp.float32
    )
    normed_one_grad = lax.psum_scatter(
        triple_terms_all.astype(jnp.bfloat16), "tensor", scatter_dimension=0, tiled=True
    ).astype(jnp.float32)
    input_part, gain_one_grad, shift_one_grad = pull_one(normed_one_grad)
    tokens_grad = (middle_grad + input_part).astype(jnp.bfloat16)
    vector_grads = jnp.stack(
        [
            gain_one_grad,
            shift_one_grad,
            query_shift_grad,
            value_shift_grad,
            merge_shift_grad,
            scale_one_grad,
            gain_two_grad,
            shift_two_grad,
            reduce_shift_grad,
            scale_two_grad,
        ]
    )
    vector_grads, expand_shift_grad = (
        lax.psum(vector_grads.astype(jnp.bfloat16), "tensor").astype(jnp.float32),
        lax.psum(expand_shift_grad.astype(jnp.bfloat16), "tensor").astype(jnp.float32),
    )
    triple_total, merge_total, expand_total, reduce_total, vector_total, expand_shift_total = (
        lax.psum_scatter(
            triple_weight_grad.astype(jnp.bfloat16), "dp", scatter_dimension=0, tiled=True
        ).astype(jnp.float32),
        lax.psum_scatter(
            merge_grad.astype(jnp.bfloat16), "dp", scatter_dimension=0, tiled=True
        ).astype(jnp.float32),
        lax.psum_scatter(
            expand_grad.astype(jnp.bfloat16), "dp", scatter_dimension=0, tiled=True
        ).astype(jnp.float32),
        lax.psum_scatter(
            reduce_grad.astype(jnp.bfloat16), "dp", scatter_dimension=0, tiled=True
        ).astype(jnp.float32),
        lax.psum_scatter(
            vector_grads.astype(jnp.bfloat16), "dp", scatter_dimension=1, tiled=True
        ).astype(jnp.float32),
        lax.psum_scatter(
            expand_shift_grad.astype(jnp.bfloat16), "dp", scatter_dimension=0, tiled=True
        ).astype(jnp.float32),
    )
    return (
        result,
        tokens_grad,
        vector_total[0],
        vector_total[1],
        triple_total,
        vector_total[2],
        vector_total[3],
        merge_total,
        vector_total[4],
        vector_total[5],
        vector_total[6],
        vector_total[7],
        expand_total,
        expand_shift_total,
        reduce_total,
        vector_total[8],
        vector_total[9],
    )


def solution(mesh):
    placed = (
        P(("dp", "tensor"), None),
        P(("dp", "tensor"), None),
        P("dp"),
        P("dp"),
        P("dp", None, "tensor"),
        P("dp"),
        P("dp"),
        P("dp", "tensor"),
        P("dp"),
        P("dp"),
        P("dp"),
        P("dp"),
        P("dp", "tensor"),
        P("dp"),
        P("dp", "tensor"),
        P("dp"),
        P("dp"),
    )
    return jax.shard_map(
        body,
        mesh=mesh,
        in_specs=placed,
        out_specs=(
            P(("dp", "tensor"), None),
            P(("dp", "tensor"), None),
            P("dp"),
            P("dp"),
            P("dp", None, "tensor"),
            P("dp"),
            P("dp"),
            P("dp", "tensor"),
            P("dp"),
            P("dp"),
            P("dp"),
            P("dp"),
            P("dp", "tensor"),
            P("dp"),
            P("dp", "tensor"),
            P("dp"),
            P("dp"),
        ),
        check_vma=False,
    )
```

profile of v0, /device:TPU:0, one launch (start us, length us, event | category | flops | bytes accessed | tf_op | source)
XLA Modules:
  0.0 3099.0 jit_solution(8816175876715363574)
XLA Ops:
  56.8 125.2 %all-gather.23.cloned.1.call-done = bf16[2,2740,1024]{2,1,0:T(8,128)(2,1)} async-done(((bf16[1,2740,1024]{2,1,0:T(8,128)(2,1)}), bf16[2,2740,1024]{2,1,0:T(8,128)(2,1)}) %all-gather.23.cloned.1.call-update) | async-done | bytes 11223056 | tf_op jit(solution)/shard_map/all_gather | solution.py:117
  192.5 36.9 %all-gather.15.cloned.1.call-done = bf16[1024,3,512]{2,0,1:T(8,128)(2,1)} async-done(((bf16[64,3,512]{2,0,1:T(8,128)(2,1)}), bf16[1024,3,512]{2,0,1:T(8,128)(2,1)}) %all-gather.15.cloned.1.call-update) | async-done | bytes 3145744 | tf_op jit(solution)/shard_map/all_gather | solution.py:88
  229.4 25.2 add_convert_fusion.1
  276.2 31.8 %reshape.205 = bf16[4,1370,3,8,64]{1,0,4,3,2:T(4,128)(2,1)} reshape(bf16[5480,3,512]{0,2,1:T(8,128)(2,1)} %copy.83) | data formatting | bytes 33669120 | tf_op jit(solution)/shard_map/reshape | solution.py:125
  329.4 271.8 %while.22 = (s32[]{:T(128)}, bf16[4,1370,8,64]{1,3,2,0:T(8,128)(2,1)}, f32[4,8,1370]{2,1,0:T(8,128)}, bf16[4,1370,8,64]{1,3,2,0:T(8,128)(2,1)}, bf16[4,1370,8,64...) while((s32[]{:T(128)}, bf16[4,1370,8,64]{1,3,2,0:T(8,128)(2,1)}, ...), condition=%wide.region_5.6_spmd, body=%wide.region_2.5_spmd.sunk | while | flops 3949688064 | bytes 188239888 | solution.py:129
  329.8 24.1 fusion.125
  373.5 23.5 fusion.127
  397.6 24.1 fusion.125
  465.5 24.1 fusion.125
  509.1 23.6 fusion.127
  533.3 24.1 fusion.125
  577.0 23.6 fusion.127
  635.3 263.2 %fusion = f32[2752,1024]{1,0:T(8,128)} fusion(f32[5480,1024]{1,0:T(8,128)} %fusion.82), kind=kCustom, calls=%all-reduce-scatter | all-reduce-scatter fusion | flops 5636097 | bytes 33718784
  904.7 29.3 concatenate.8
  989.3 106.1 %all-gather.25.cloned.1.call-done = bf16[2,2740,1024]{2,1,0:T(8,128)(2,1)} async-done(((bf16[1,2740,1024]{2,1,0:T(8,128)(2,1)}), bf16[2,2740,1024]{2,1,0:T(8,128)(2,1)}) %all-gather.25.cloned.1.call-update) | async-done | bytes 11223056 | tf_op jit(solution)/shard_map/all_gather | solution.py:149
  1105.8 42.3 %all-gather.19.cloned.1.call-done = bf16[1024,2048]{1,0:T(8,128)(2,1)} async-done(((bf16[64,2048]{1,0:T(8,128)(2,1)}), bf16[1024,2048]{1,0:T(8,128)(2,1)}) %all-gather.19.cloned.1.call-update) | async-done | bytes 4194320 | tf_op jit(solution)/shard_map/all_gather | solution.py:136
  1148.1 122.5 %multiply_convert_fusion.1 = (bf16[5480,2048]{1,0:T(8,128)(2,1)}, f32[5480,2048]{1,0:T(8,128)}, f32[5480,2048]{1,0:T(8,128)}) fusion(f32[2048]{0:T(1024)S(1)} %dynamic_slice.37, bf16[5480,1024]{1,0:T(8,128)(2,1)} %reshape.218, bf16[1024,2048]{1,0:T(8,128)(2,1)} %all-gather.19.cloned.1.call-done), kind=kOutput, calls=%fused_computation.57 | convolution fusion | flops 23725506560 | bytes 127655936 | tf_op jit(solution)/shard_map/dot_general | solution.py:150
  1270.6 49.9 %convert_reduce_fusion = (bf16[2048]{0:T(1024)(128)(2,1)}, bf16[5480,2048]{1,0:T(8,128)(2,1)}) fusion(f32[5480,2048]{1,0:T(8,128)} %get-tuple-element.174, bf16[5480,1024]{1,0:T(8,128)(2,1)} %reshape.222, bf16[1024,2048]{1,0:T(8,128)(2,1)} %all-gather.21.cloned.1.call-done, f32[5480,2048]{1,0:T(8,128)} %get-tuple-element.209, f32[2048]{0:T(1024)S(1)} %dynamic_slice.37), kind=kOutput, calls=%fused_computation.55 | convolution fusion | flops 23175575552 | bytes 127660032 | tf_op jit(solution)/shard_map/ro,of->rf/dot_general | solution.py:165
  1320.5 29.6 convolution_convert_fusion
  1350.1 133.1 %fusion.2 = bf16[2752,1024]{1,0:T(8,128)(2,1)} fusion(bf16[5480,1024]{1,0:T(8,128)(2,1)} %convolution_convert_fusion), kind=kCustom, calls=%all-reduce-scatter.2 | all-reduce-scatter fusion | flops 5636097 | bytes 16859648
  1486.4 29.8 convolution_convert_fusion.1
  1516.2 130.8 %fusion.1 = bf16[2752,1024]{1,0:T(8,128)(2,1)} fusion(bf16[5480,1024]{1,0:T(8,128)(2,1)} %convolution_convert_fusion.1), kind=kCustom, calls=%all-reduce-scatter.1 | all-reduce-scatter fusion | flops 5636097 | bytes 16859648
  1651.4 27.7 concatenate.10
  1698.5 27.6 concatenate.9
  1757.3 35.9 %convolution_convert_fusion.3 = bf16[1024,2048]{1,0:T(8,128)(2,1)} fusion(bf16[5480,1024]{1,0:T(8,128)(2,1)} %reshape.222, bf16[5480,2048]{1,0:T(8,128)(2,1)} %get-tuple-element.173), kind=kOutput, calls=%fused_computation.124 | convolution fusion | flops 22986883072 | bytes 37863424 | tf_op jit(solution)/shard_map/ro,rf->of/dot_general | solution.py:169
  1793.2 34.9 %convolution_convert_fusion.4 = bf16[1024,2048]{1,0:T(8,128)(2,1)} fusion(bf16[5480,1024]{1,0:T(8,128)(2,1)} %reshape.218, bf16[5480,2048]{1,0:T(8,128)(2,1)} %get-tuple-element.211), kind=kOutput, calls=%fused_computation.125 | convolution fusion | flops 22986883072 | bytes 37863424 | tf_op jit(solution)/shard_map/rd,rf->df/dot_general | solution.py:170
  1835.9 56.9 %all-gather.29.cloned.1.call-done = bf16[2,2740,1024]{2,1,0:T(8,128)(2,1)} async-done(((bf16[1,2740,1024]{2,1,0:T(8,128)(2,1)}), bf16[2,2740,1024]{2,1,0:T(8,128)(2,1)}) %all-gather.29.cloned.1.call-update) | async-done | bytes 11223056 | tf_op jit(solution)/shard_map/all_gather | solution.py:191
  1940.9 698.3 %while.23 = (s32[]{:T(128)}, bf16[4,1370,3,8,64]{1,4,3,2,0:T(8,128)(2,1)}, bf16[4,1370,8,64]{1,3,2,0:T(8,128)(2,1)}, bf16[4,1370,8,64]{1,3,2,0:T(8,128)(2,1)}, f...) while((s32[]{:T(128)}, ...), condition=%wide.region_15.16_spmd, body=%wide.region_13.15_spmd.sunk | while | flops 9745971200 | bytes 479360224 | solution.py:198
  1941.9 24.6 fusion.135
  1966.5 24.6 fusion.136
  1991.0 42.8 %multiply_reduce_fusion.5 = (f32[8,1370]{1,0:T(8,128)S(1)}, f32[8,1370,1370]{1,2,0:T(8,128)}) fusion(f32[8,1370,1370]{1,2,0:T(8,128)} %fusion.135, bf16[4,1370,8,64]{1,3,2,0:T(8,128)(2,1)} %get-tuple-element.345, s32[]{:T(128)S(6)} %copy.121, bf16[4,1370,8,64]{1,3,2,0:T(8,128)(2,1)} %get-tuple-element.344), kind=kOutput, calls=%fused_computation.20.clone.3 | convolution fusion | flops 1951965056 | bytes 124986304 | tf_op jit(solution)/shard_map/while/body/eval_jaxpr/qhd,khd->hqk/dot_general | solution.py:42
  2033.8 49.0 %multiply_convert_fusion.4 = bf16[8,1370,1370]{1,2,0:T(8,128)(2,1)} fusion(f32[8,1370,1370]{1,2,0:T(8,128)} %get-tuple-element.300, f32[8,1370,1370]{1,2,0:T(8,128)} %fusion.135, f32[8,1370]{1,0:T(8,128)S(1)} %get-tuple-element.301), kind=kLoop, calls=%fused_computation.19.clone.1 | loop fusion | flops 45045600 | bytes 150195840 | tf_op jit(solution)/shard_map/while/body/eval_jaxpr/convert_element_type | solution.py:44
  2118.1 24.1 fusion.135
  2165.4 42.5 %multiply_reduce_fusion.5 = (f32[8,1370]{1,0:T(8,128)S(1)}, f32[8,1370,1370]{1,2,0:T(8,128)}) fusion(f32[8,1370,1370]{1,2,0:T(8,128)} %fusion.135, bf16[4,1370,8,64]{1,3,2,0:T(8,128)(2,1)} %get-tuple-element.345, s32[]{:T(128)S(6)} %copy.121, bf16[4,1370,8,64]{1,3,2,0:T(8,128)(2,1)} %get-tuple-element.344), kind=kOutput, calls=%fused_computation.20.clone.3 | convolution fusion | flops 1951965056 | bytes 124986304 | tf_op jit(solution)/shard_map/while/body/eval_jaxpr/qhd,khd->hqk/dot_general | solution.py:42
  2207.9 48.9 %multiply_convert_fusion.4 = bf16[8,1370,1370]{1,2,0:T(8,128)(2,1)} fusion(f32[8,1370,1370]{1,2,0:T(8,128)} %get-tuple-element.300, f32[8,1370,1370]{1,2,0:T(8,128)} %fusion.135, f32[8,1370]{1,0:T(8,128)S(1)} %get-tuple-element.301), kind=kLoop, calls=%fused_computation.19.clone.1 | loop fusion | flops 45045600 | bytes 150195840 | tf_op jit(solution)/shard_map/while/body/eval_jaxpr/convert_element_type | solution.py:44
  2291.9 24.1 fusion.135
  2339.2 42.5 %multiply_reduce_fusion.5 = (f32[8,1370]{1,0:T(8,128)S(1)}, f32[8,1370,1370]{1,2,0:T(8,128)}) fusion(f32[8,1370,1370]{1,2,0:T(8,128)} %fusion.135, bf16[4,1370,8,64]{1,3,2,0:T(8,128)(2,1)} %get-tuple-element.345, s32[]{:T(128)S(6)} %copy.121, bf16[4,1370,8,64]{1,3,2,0:T(8,128)(2,1)} %get-tuple-element.344), kind=kOutput, calls=%fused_computation.20.clone.3 | convolution fusion | flops 1951965056 | bytes 124986304 | tf_op jit(solution)/shard_map/while/body/eval_jaxpr/qhd,khd->hqk/dot_general | solution.py:42
  2381.7 48.9 %multiply_convert_fusion.4 = bf16[8,1370,1370]{1,2,0:T(8,128)(2,1)} fusion(f32[8,1370,1370]{1,2,0:T(8,128)} %get-tuple-element.300, f32[8,1370,1370]{1,2,0:T(8,128)} %fusion.135, f32[8,1370]{1,0:T(8,128)S(1)} %get-tuple-element.301), kind=kLoop, calls=%fused_computation.19.clone.1 | loop fusion | flops 45045600 | bytes 150195840 | tf_op jit(solution)/shard_map/while/body/eval_jaxpr/convert_element_type | solution.py:44
  2465.8 24.1 fusion.135
  2513.0 42.6 %multiply_reduce_fusion.5 = (f32[8,1370]{1,0:T(8,128)S(1)}, f32[8,1370,1370]{1,2,0:T(8,128)}) fusion(f32[8,1370,1370]{1,2,0:T(8,128)} %fusion.135, bf16[4,1370,8,64]{1,3,2,0:T(8,128)(2,1)} %get-tuple-element.345, s32[]{:T(128)S(6)} %copy.121, bf16[4,1370,8,64]{1,3,2,0:T(8,128)(2,1)} %get-tuple-element.344), kind=kOutput, calls=%fused_computation.20.clone.3 | convolution fusion | flops 1951965056 | bytes 124986304 | tf_op jit(solution)/shard_map/while/body/eval_jaxpr/qhd,khd->hqk/dot_general | solution.py:42
  2555.7 48.9 %multiply_convert_fusion.4 = bf16[8,1370,1370]{1,2,0:T(8,128)(2,1)} fusion(f32[8,1370,1370]{1,2,0:T(8,128)} %get-tuple-element.300, f32[8,1370,1370]{1,2,0:T(8,128)} %fusion.135, f32[8,1370]{1,0:T(8,128)S(1)} %get-tuple-element.301), kind=kLoop, calls=%fused_computation.19.clone.1 | loop fusion | flops 45045600 | bytes 150195840 | tf_op jit(solution)/shard_map/while/body/eval_jaxpr/convert_element_type | solution.py:44
  2656.6 29.1 reshape.208
  2685.7 23.7 bitcast_convert_fusion
  2709.4 131.7 %fusion.3 = bf16[2752,1024]{1,0:T(8,128)(2,1)} fusion(bf16[5480,1024]{1,0:T(8,128)(2,1)} %bitcast_convert_fusion), kind=kCustom, calls=%all-reduce-scatter.3 | all-reduce-scatter fusion | flops 5636097 | bytes 16859648
  2854.3 28.1 concatenate.11
  2917.3 25.6 convolution_convert_fusion.5
  2944.5 31.6 %all-reduce.4 = bf16[4096]{0:T(1024)(128)(2,1)S(1)} all-reduce(bf16[4096]{0:T(1024)(128)(2,1)S(1)} %dynamic_update_slice.25), channel_id=10, replica_groups=mesh['dp'=16,'tensor'=2] {'dp'}, use_global_device_ids=true, to_apply=%region_35.36.clone | all-reduce | flops 4096 | bytes 16384
  3022.6 67.9 %reduce-scatter.16.cloned.1.call-done = bf16[64,3,512]{2,0,1:T(8,128)(2,1)} async-done(((bf16[1024,3,512]{2,0,1:T(8,128)(2,1)}), bf16[64,3,512]{2,0,1:T(8,128)(2,1)}) %reduce-scatter.16.cloned.1.call-update) | async-done | bytes 196624 | tf_op jit(solution)/shard_map/reduce_scatter | solution.py:236
  (269 shorter events, 750.9 us)
Async XLA Ops:
  7.3 174.7 %all-gather.23.cloned.1.call-start = ((), (), s32[]{:S(2)}) async-start(), calls=%async_computation.13 | async-start | bytes 16859136 | tf_op jit(solution)/shard_map/all_gather | solution.py:117
  10.8 36.0 %copy-start.3 = (f32[2740]{0:T(1024)}, f32[2740]{0:T(1024)S(1)}, u32[]{:S(2)}) copy-start(f32[2740]{0:T(1024)S(1)} %broadcast_multiply_fusion.1) | copy-start | bytes 32884
  15.0 41.5 %copy-start.7 = (f32[2740]{0:T(1024)}, f32[2740]{0:T(1024)S(1)}, u32[]{:S(2)}) copy-start(f32[2740]{0:T(1024)S(1)} %fusion.74) | copy-start | bytes 32884
  39.5 17.0 copy-start.15
  39.5 17.0 copy-start.21
  46.8 182.7 %all-gather.15.cloned.1.call-start = ((), (), s32[]{:S(2)}) async-start(), calls=%async_computation.5 | async-start | bytes 3342336 | tf_op jit(solution)/shard_map/all_gather | solution.py:88
  47.5 574.4 %all-gather.17.cloned.1.call-start = ((), (), s32[]{:S(2)}) async-start(), calls=%async_computation.6 | async-start | bytes 1114112 | tf_op jit(solution)/shard_map/all_gather | solution.py:89
  48.2 930.2 %all-gather.27.cloned.1.call-start = ((), (), s32[]{:S(2)}) async-start(), calls=%async_computation.15 | async-start | bytes 16859136 | tf_op jit(solution)/shard_map/all_gather | solution.py:164
  56.6 1038.8 %all-gather.25.cloned.1.call-start = ((), (), s32[]{:S(2)}) async-start(), calls=%async_computation.14 | async-start | bytes 16859136 | tf_op jit(solution)/shard_map/all_gather | solution.py:149
  635.3 267.6 %copy-start.44 = (u32[32]{0:T(128)S(1)}, u32[32]{0:T(128)}, u32[]{:S(2)}) copy-start(u32[32]{0:T(128)} %constant.145) | copy-start | bytes 388
  899.4 5.3 collective-permute-start
  904.1 29.9 copy-start.19
  904.1 29.9 copy-start.23
  957.9 190.2 %all-gather.19.cloned.1.call-start = ((), (), s32[]{:S(2)}) async-start(), calls=%async_computation.7 | async-start | bytes 4456448 | tf_op jit(solution)/shard_map/all_gather | solution.py:136
  958.5 312.1 %all-gather.21.cloned.1.call-start = ((), (), s32[]{:S(2)}) async-start(), calls=%async_computation.8 | async-start | bytes 4456448 | tf_op jit(solution)/shard_map/all_gather | solution.py:137
  959.2 933.6 %all-gather.29.cloned.1.call-start = ((), (), s32[]{:S(2)}) async-start(), calls=%async_computation.16 | async-start | bytes 16859136 | tf_op jit(solution)/shard_map/all_gather | solution.py:191
  1484.0 167.4 %collective-permute-start.2 = (bf16[12,1024]{1,0:T(8,128)(2,1)S(1)}, bf16[12,1024]{1,0:T(8,128)(2,1)S(1)}, u32[]{:S(2)}, u32[]{:S(2)}) collective-permute-start(bf16[12,1024]{1,0:T(8,128)(2,1)S(1)} %slice.129), channel_id=1, source_target_pairs={{0,1},{2,3},{4,5},{6,7},{8,9},{10,11},{12,13},{14,15},{16,17},{18,... | collective-permute-start | bytes 73736
  1516.2 162.9 %copy-start.6 = (f32[2740]{0:T(1024)S(1)}, f32[2740]{0:T(1024)}, u32[]{:S(2)}) copy-start(f32[2740]{0:T(1024)} %copy-done.5) | copy-start | bytes 32884
  1516.2 162.9 %copy-start.18 = (f32[1,1024]{1,0:T(1,128)S(1)}, f32[1,1024]{1,0:T(1,128)}, u32[]{:S(2)}) copy-start(f32[1,1024]{1,0:T(1,128)} %get-tuple-element.187) | copy-start | bytes 12292
  1647.8 50.8 %collective-permute-start.1 = (bf16[12,1024]{1,0:T(8,128)(2,1)S(1)}, bf16[12,1024]{1,0:T(8,128)(2,1)S(1)}, u32[]{:S(2)}, u32[]{:S(2)}) collective-permute-start(bf16[12,1024]{1,0:T(8,128)(2,1)S(1)} %slice.128), channel_id=1, source_target_pairs={{0,1},{2,3},{4,5},{6,7},{8,9},{10,11},{12,13},{14,15},{16,17},{18,... | collective-permute-start | bytes 73736
  1679.1 9.4 copy-start.1
  1679.1 9.4 copy-start.10
  1688.5 37.7 %copy-start.20 = (f32[1,1024]{1,0:T(1,128)S(1)}, f32[1,1024]{1,0:T(1,128)}, u32[]{:S(2)}) copy-start(f32[1,1024]{1,0:T(1,128)} %get-tuple-element.196) | copy-start | bytes 12292
  1688.5 37.6 %copy-start.22 = (f32[1,1024]{1,0:T(1,128)S(1)}, f32[1,1024]{1,0:T(1,128)}, u32[]{:S(2)}) copy-start(f32[1,1024]{1,0:T(1,128)} %copy-done.21) | copy-start | bytes 12292
  1688.5 37.6 %copy-start.24 = (f32[1,1024]{1,0:T(1,128)S(1)}, f32[1,1024]{1,0:T(1,128)}, u32[]{:S(2)}) copy-start(f32[1,1024]{1,0:T(1,128)} %get-tuple-element.191) | copy-start | bytes 12292
  1688.5 37.6 %copy-start.25 = (f32[1,1024]{1,0:T(1,128)S(1)}, f32[1,1024]{1,0:T(1,128)}, u32[]{:S(2)}) copy-start(f32[1,1024]{1,0:T(1,128)} %get-tuple-element.188) | copy-start | bytes 12292
  1757.2 1218.9 %reduce-scatter.22.cloned.1.call-start = ((), (), s32[]{:S(2)}) async-start(), calls=%async_computation.12 | async-start | bytes 4456448 | tf_op jit(solution)/shard_map/reduce_scatter | solution.py:245
  1793.2 1184.8 %reduce-scatter.20.cloned.1.call-start = ((), (), s32[]{:S(2)}) async-start(), calls=%async_computation.11 | async-start | bytes 4456448 | tf_op jit(solution)/shard_map/reduce_scatter | solution.py:242
  1828.1 1165.2 %reduce-scatter.24.cloned.1.call-start = ((), (), s32[]{:S(2)}) async-start(), calls=%async_computation.17 | async-start | bytes 278528
  1834.7 68.5 %copy-start.46 = (bf16[1024,512]{1,0:T(8,128)(2,1)S(1)}, bf16[1024,512]{1,0:T(8,128)(2,1)}, u32[]{:S(2)}) copy-start(bf16[1024,512]{1,0:T(8,128)(2,1)} %all-gather.17.cloned.1.call-done) | copy-start | bytes 3145732
  2656.6 29.1 copy-start.45
  2848.1 38.6 %copy-start.4 = (f32[2740]{0:T(1024)S(1)}, f32[2740]{0:T(1024)}, u32[]{:S(2)}) copy-start(f32[2740]{0:T(1024)} %copy-done.3) | copy-start | bytes 32884
  2848.1 38.6 %copy-start.16 = (f32[1,1024]{1,0:T(1,128)S(1)}, f32[1,1024]{1,0:T(1,128)}, u32[]{:S(2)}) copy-start(f32[1,1024]{1,0:T(1,128)} %copy-done.15) | copy-start | bytes 12292
  2849.1 5.2 collective-permute-start.3
  2882.4 12.7 copy-start.14
  2882.4 12.7 slice-start
  2882.4 12.7 slice-start.2
  2882.4 12.7 copy-start.8
  2886.8 16.3 copy-start.27
  2886.8 16.3 copy-start.28
  2886.8 16.3 copy-start.29
  2886.8 16.3 copy-start.30
  2886.8 16.3 copy-start.31
  2886.8 16.3 copy-start.32
  2904.1 117.0 %reduce-scatter.18.cloned.1.call-start = ((), (), s32[]{:S(2)}) async-start(), calls=%async_computation.10 | async-start | bytes 1114112 | tf_op jit(solution)/shard_map/reduce_scatter | solution.py:239
  2917.3 25.7 copy-start.48
  2917.3 26.9 copy-start.33
  2917.3 173.3 %reduce-scatter.16.cloned.1.call-start = ((), (), s32[]{:S(2)}) async-start(), calls=%async_computation.9 | async-start | bytes 3342336 | tf_op jit(solution)/shard_map/reduce_scatter | solution.py:236
  (22 other events, 144.0 us)
Sparse Core Ops, SparseCore 0:
  46.9 135.0 all-gather.22
  184.2 45.1 all-gather.14
  231.6 36.7 all-gather.16
  270.4 136.6 all-gather.26
  958.0 137.2 all-gather.24
  1097.4 50.7 all-gather.18
  1150.3 49.0 all-gather.20
  1757.4 135.4 all-gather.28
  1896.7 72.3 reduce-scatter.21
  1973.3 71.8 reduce-scatter.19
  2904.2 56.9 reduce-scatter.23
  2964.7 56.3 reduce-scatter.17
  3025.4 65.1 reduce-scatter.15
where the time goes:
time: 3110 us; the launch traced here: 3100 us
  matrix products  1090 us (35%)
  blocking collectives  738 us (24%)
  waiting for transfers between devices  461 us (15%)
  other arithmetic  434 us (14%)
  local copies, waits for them, and re-layouts  345 us (11%)
    unnamed x5, blocking collectives  690 us
    convert_element_type x4, other arithmetic, attend_backward(): score_grad = (probs * (prob_grad - row_term)).astype(jnp.bfloat16)  196 us
    dot_general x4, matrix products, attend_backward(): jnp.einsum('qhd,khd->hqk', mixed_grad, values, preferred_element_type=jnp...  170 us
    unnamed x124, local copies, waits for them, and re-layouts  167 us
    all_gather x1, waiting for transfers between devices, body(): lax.all_gather(normed_one.astype(jnp.bfloat16), 'tensor', axis=0, tiled=T...  125 us
    dot_general x1, matrix products, body(): jnp.dot(rows_two, expand_part, preferred_element_type=jnp.float32)  123 us
    all_gather x1, waiting for transfers between devices, body(): rows_two = lax.all_gather(sent_two, 'tensor', axis=0, tiled=True)  106 us
    dot_general x4, matrix products, attend_backward(): jnp.einsum('qhd,khd->hqk', queries, keys, preferred_element_type=jnp.floa...  97 us
  transfers between devices with their start and end apart: 17, of which 9 were waited for; matrix products, arithmetic and copies ran while one was open for 72% of the time, Pallas kernels for 0%

commit v1 on v0

v1 whole, which is shorter than its diff:
```python
import functools

import jax
import jax.numpy as jnp
from jax import lax
from jax.experimental import pallas as pl
from jax.experimental.pallas import tpu as pltpu
from jax.sharding import PartitionSpec as P

HD = 64
SEQ = 1370
PAIR = 128
F32 = jnp.float32
BF16 = jnp.bfloat16
FACTOR = HD ** (-0.5)
FACTOR_2 = FACTOR * 1.4426950408889634
VMEM = 56 * 2**20


def dot(left, right, left_dim, right_dim):
    dims = (((left_dim,), (right_dim,)), ((), ()))
    return lax.dot_general(left, right, dims, preferred_element_type=F32)


class Tree:
    def __init__(self, mesh):
        self.dp = mesh.shape["dp"]
        self.tensor = mesh.shape["tensor"]
        dp_bits = self.dp.bit_length() - 1
        tensor_bits = self.tensor.bit_length() - 1
        if 1 << dp_bits != self.dp or 1 << tensor_bits != self.tensor or dp_bits < 2:
            raise ValueError("mesh sizes")
        high = [("dp", bit) for bit in range(dp_bits - 1, 1, -1)]
        tensor_stages = [("tensor", bit) for bit in range(tensor_bits - 1, -1, -1)]
        self.orders = (
            high + [("dp", 1)] + tensor_stages,
            high + tensor_stages + [("dp", 1)],
        )
        self.half_blocks = self.dp * self.tensor // 2

    def swap(self, value, stage):
        axis, bit = stage
        size = self.dp if axis == "dp" else self.tensor
        return lax.ppermute(value, axis, [(i, i ^ (1 << bit)) for i in range(size)])

    def tables(self):
        me_dp = lax.axis_index("dp")
        me_tensor = lax.axis_index("tensor")
        place = jnp.arange(self.half_blocks, dtype=jnp.int32)
        pairs = self.dp // 2
        relative = {
            "dp": ((place % pairs) << 1) ^ (me_dp & ~1),
            "tensor": (place // pairs) ^ me_tensor,
        }
        rows = []
        for order in self.orders:
            index = jnp.zeros_like(place)
            for position, (axis, bit) in enumerate(order):
                index = index + (((relative[axis] >> bit) & 1) << position)
            rows.append(index)
        core = jnp.full_like(place, me_dp & 1)
        return jnp.stack(rows + [core]).astype(jnp.int32)

    def gather(self, shard, tables, widths):
        rows, width = shard.shape
        half = rows // 2
        pieces = []
        for order, start in zip(self.orders, (0, half)):
            held = shard[start : start + half][None]
            for stage in order:
                held = jnp.concatenate([held, self.swap(held, stage)], axis=0)
            pieces += [held, self.swap(held, ("dp", 0))]
        return self.assemble(pieces, tables, half, widths)

    def assemble(self, pieces, tables, half, widths):
        pairs = self.dp // 2
        total = sum(widths)

        def kernel(tables_ref, own_a, far_a, own_b, far_b, *outs):
            core = tables_ref[2, 0]

            def put(first_a, second_a, first_b, second_b):
                at = 0
                for out, width in zip(outs, widths):
                    columns = slice(at, at + width)
                    out[0:half] = first_a[:, columns]
                    out[half : 2 * half] = first_b[:, columns]
                    out[2 * half : 3 * half] = second_a[:, columns]
                    out[3 * half : 4 * half] = second_b[:, columns]
                    at += width

            @pl.when(core == 0)
            def _():
                put(own_a, far_a, own_b, far_b)

            @pl.when(core != 0)
            def _():
                put(far_a, own_a, far_b, own_b)

        spec_a = pl.BlockSpec((None, half, total), lambda i, table: (table[0, i], 0, 0))
        spec_b = pl.BlockSpec((None, half, total), lambda i, table: (table[1, i], 0, 0))
        return pl.pallas_call(
            kernel,
            grid_spec=pltpu.PrefetchScalarGridSpec(
                num_scalar_prefetch=1,
                grid=(self.half_blocks,),
                in_specs=[spec_a, spec_a, spec_b, spec_b],
                out_specs=[
                    pl.BlockSpec((4 * half, width), lambda i, table: (i % pairs, i // pairs))
                    for width in widths
                ],
            ),
            out_shape=[
                jax.ShapeDtypeStruct((self.dp * 2 * half, self.tensor * width), BF16)
                for width in widths
            ],
            compiler_params=pltpu.CompilerParams(vmem_limit_bytes=VMEM),
        )(tables, *pieces)

    def split(self, arrays, tables, half, widths):
        pairs = self.dp // 2
        total = sum(widths)

        def kernel(tables_ref, *refs):
            sources, (own_a, far_a, own_b, far_b) = refs[: len(widths)], refs[len(widths) :]
            core = tables_ref[2, 0]

            def take(first_a, second_a, first_b, second_b):
                at = 0
                for source, width in zip(sources, widths):
                    columns = slice(at, at + width)
                    first_a[:, columns] = source[0:half]
                    first_b[:, columns] = source[half : 2 * half]
                    second_a[:, columns] = source[2 * half : 3 * half]
                    second_b[:, columns] = source[3 * half : 4 * half]
                    at += width

            @pl.when(core == 0)
            def _():
                take(own_a, far_a, own_b, far_b)

            @pl.when(core != 0)
            def _():
                take(far_a, own_a, far_b, own_b)

        spec_a = pl.BlockSpec((None, half, total), lambda i, table: (table[0, i], 0, 0))
        spec_b = pl.BlockSpec((None, half, total), lambda i, table: (table[1, i], 0, 0))
        shape = jax.ShapeDtypeStruct((self.half_blocks, half, total), BF16)
        return pl.pallas_call(
            kernel,
            grid_spec=pltpu.PrefetchScalarGridSpec(
                num_scalar_prefetch=1,
                grid=(self.half_blocks,),
                in_specs=[
                    pl.BlockSpec((4 * half, width), lambda i, table: (i % pairs, i // pairs))
                    for width in widths
                ],
                out_specs=[spec_a, spec_a, spec_b, spec_b],
            ),
            out_shape=[shape] * 4,
            compiler_params=pltpu.CompilerParams(vmem_limit_bytes=VMEM),
        )(tables, *arrays)

    def scatter(self, arrays, tables):
        rows = arrays[0].shape[0] // self.dp
        widths = [array.shape[1] // self.tensor for array in arrays]
        own_a, far_a, own_b, far_b = self.split(arrays, tables, rows // 2, widths)
        halves = []
        for order, own, far in zip(self.orders, (own_a, own_b), (far_a, far_b)):
            held, sent = own, far
            stages = [("dp", 0)] + order[::-1]
            for number, stage in enumerate(stages):
                held = held.astype(F32) + self.swap(sent, stage).astype(F32)
                if number + 1 < len(stages):
                    held = held.astype(BF16)
                    middle = held.shape[0] // 2
                    held, sent = held[:middle], held[middle:]
            halves.append(held[0])
        whole = jnp.concatenate(halves, axis=0)
        parts, at = [], 0
        for width in widths:
            parts.append(whole[:, at : at + width])
            at += width
        return parts

    def gather_rows(self, row):
        held = row[None]
        bits = range(self.dp.bit_length() - 2, -1, -1)
        for bit in bits:
            held = jnp.concatenate([self.swap(held, ("dp", bit)), held], axis=0)
        index = self.row_index()
        return held[index]

    def row_index(self):
        bits = self.dp.bit_length() - 1
        relative = jnp.arange(self.dp) ^ lax.axis_index("dp")
        index = jnp.zeros_like(relative)
        for position, bit in enumerate(range(bits - 1, -1, -1)):
            index = index + ((1 - ((relative >> bit) & 1)) << position)
        return index

    def scatter_rows(self, rows):
        relative = rows[jnp.arange(self.dp) ^ lax.axis_index("dp")]
        held = relative
        for bit in range(self.tensor.bit_length() - 1):
            held = held + self.swap(held, ("tensor", bit))
        for bit in range(self.dp.bit_length() - 2, -1, -1):
            middle = held.shape[0] // 2
            held = held[:middle] + self.swap(held[middle:], ("dp", bit))
        return held[0]


def split_pair(block):
    lane = lax.broadcasted_iota(jnp.int32, block.shape, 1)
    zero = jnp.zeros_like(block)
    return jnp.concatenate(
        [jnp.where(lane < HD, block, zero), jnp.where(lane >= HD, block, zero)], axis=0
    )


def join_pair(block):
    rows = block.shape[0] // 2
    lane = lax.broadcasted_iota(jnp.int32, (rows, PAIR), 1)
    return jnp.where(lane < HD, block[:rows], block[rows:])


def mask_keys(scores, segment, valid, fill):
    if valid == segment:
        return scores
    start = valid // 128 * 128
    parts = []
    for base in range(0, scores.shape[1], segment):
        if start:
            parts.append(scores[:, base : base + start])
        tail = scores[:, base + start : base + segment]
        lane = lax.broadcasted_iota(jnp.int32, tail.shape, 1) + start
        parts.append(jnp.where(lane < valid, tail, fill))
    return jnp.concatenate(parts, axis=1)


def attend_forward_kernel(segment, valid, query_ref, pair_ref, mixed_ref, logsum_ref, value_ref):
    keys = pair_ref.at[:, PAIR : 2 * PAIR]
    value_ref[:, 0:PAIR] = pair_ref[:, 2 * PAIR : 3 * PAIR]
    value_ref[:, PAIR : 2 * PAIR] = jnp.ones((value_ref.shape[0], PAIR), BF16)
    for chunk in range(query_ref.shape[0] // 128):
        rows = pl.ds(chunk * 128, 128)
        queries = split_pair(query_ref[rows, 0:PAIR])
        scores = mask_keys(dot(queries, keys[...], 1, 1), segment, valid, -1e30)
        peak = jnp.max(scores, axis=1, keepdims=True)
        weights = jnp.exp2((scores - peak) * FACTOR_2).astype(BF16)
        mixed = dot(weights, value_ref[...], 1, 0)
        total = mixed[:, PAIR:]
        mixed_ref[rows, :] = join_pair(mixed[:, :PAIR] / total).astype(BF16)
        logsum_ref[rows, :] = join_pair(peak * FACTOR_2 + jnp.log2(total))


def attend_backward_kernel(
    segment, valid, joint, query_ref, pair_ref, mixed_ref, grad_ref, logsum_ref, *rest
):
    if joint:
        out_ref, key_sum, value_sum = rest
        query_out = out_ref.at[:, 0:PAIR]
        key_out = out_ref.at[:, PAIR : 2 * PAIR]
        value_out = out_ref.at[:, 2 * PAIR : 3 * PAIR]
    else:
        query_out, pair_out, key_sum, value_sum = rest
        key_out = pair_out.at[:, 0:PAIR]
        value_out = pair_out.at[:, PAIR : 2 * PAIR]
    keys = pair_ref.at[:, PAIR : 2 * PAIR]
    values = pair_ref.at[:, 2 * PAIR : 3 * PAIR]
    key_total = value_total = None
    for chunk in range(query_ref.shape[0] // 128):
        rows = pl.ds(chunk * 128, 128)
        queries = split_pair(query_ref[rows, 0:PAIR])
        grad = grad_ref[rows, :]
        grads = split_pair(grad)
        row_term = jnp.sum(
            split_pair(grad.astype(F32) * mixed_ref[rows, :].astype(F32)), axis=1, keepdims=True
        )
        logsum = logsum_ref[rows, :]
        logsum = jnp.concatenate([logsum[:, 0:1], logsum[:, HD : HD + 1]], axis=0)
        scores = dot(queries, keys[...], 1, 1)
        probs = mask_keys(jnp.exp2(scores * FACTOR_2 - logsum), segment, valid, 0.0)
        prob_grad = dot(grads, values[...], 1, 1)
        score_grad = (probs * (prob_grad - row_term)).astype(BF16)
        query_grad = join_pair(dot(score_grad, keys[...], 1, 0)) * FACTOR
        query_out[rows, :] = query_grad.astype(BF16)
        value_part = dot(grads.T, probs.astype(BF16), 1, 0)
        key_part = dot(queries.T, score_grad, 1, 0)
        if chunk == 0:
            value_sum[...] = value_part
            key_sum[...] = key_part
        else:
            value_sum[...] += value_part
            key_sum[...] += key_part
    key_out[...] = (key_sum[...] * FACTOR).T.astype(BF16)
    value_out[...] = value_sum[...].T.astype(BF16)


def attend_cost(products, images, pairs, rows, key_rows):
    area = images * pairs * 2 * rows * key_rows
    return pl.CostEstimate(
        flops=2 * products * area * HD * 4,
        bytes_accessed=images * pairs * rows * PAIR * 16,
        transcendentals=area,
    )


def attend_forward(triple, gathered, segment, valid):
    images, rows, width = triple.shape
    key_rows = gathered.shape[1]
    pairs = width // (3 * PAIR)
    at = lambda i, g: (i, 0, g)
    return pl.pallas_call(
        functools.partial(attend_forward_kernel, segment, valid),
        grid=(images, pairs),
        in_specs=[
            pl.BlockSpec((None, rows, 3 * PAIR), at),
            pl.BlockSpec((None, key_rows, 3 * PAIR), at),
        ],
        out_specs=[
            pl.BlockSpec((None, rows, PAIR), at),
            pl.BlockSpec((None, rows, PAIR), at),
        ],
        out_shape=[
            jax.ShapeDtypeStruct((images, rows, pairs * PAIR), BF16),
            jax.ShapeDtypeStruct((images, rows, pairs * PAIR), F32),
        ],
        scratch_shapes=[pltpu.VMEM((key_rows, 2 * PAIR), BF16)],
        cost_estimate=attend_cost(2, images, pairs, rows, key_rows),
        compiler_params=pltpu.CompilerParams(vmem_limit_bytes=VMEM),
    )(triple, gathered)


def attend_backward(triple, gathered, mixed, mixed_grad, logsum, segment, valid):
    images, rows, width = triple.shape
    key_rows = gathered.shape[1]
    pairs = width // (3 * PAIR)
    joint = key_rows == rows
    at = lambda i, g: (i, 0, g)
    row_spec = pl.BlockSpec((None, rows, PAIR), at)
    triple_spec = pl.BlockSpec((None, rows, 3 * PAIR), at)
    if joint:
        out_specs = [triple_spec]
        out_shape = [jax.ShapeDtypeStruct(triple.shape, BF16)]
    else:
        out_specs = [row_spec, pl.BlockSpec((None, key_rows, 2 * PAIR), at)]
        out_shape = [
            jax.ShapeDtypeStruct((images, rows, pairs * PAIR), BF16),
            jax.ShapeDtypeStruct((images, key_rows, pairs * 2 * PAIR), BF16),
        ]
    outs = pl.pallas_call(
        functools.partial(attend_backward_kernel, segment, valid, joint),
        grid=(images, pairs),
        in_specs=[
            triple_spec,
            pl.BlockSpec((None, key_rows, 3 * PAIR), at),
            row_spec,
            row_spec,
            row_spec,
        ],
        out_specs=out_specs,
        out_shape=out_shape,
        scratch_shapes=[pltpu.VMEM((PAIR, key_rows), F32)] * 2,
        cost_estimate=attend_cost(5, images, pairs, rows, key_rows),
        compiler_params=pltpu.CompilerParams(vmem_limit_bytes=VMEM),
    )(triple, gathered, mixed, mixed_grad, logsum)
    if joint:
        return outs[0]
    query_grad, pair_grad = outs
    shares = key_rows // rows
    tensor = lax.axis_size("tensor")
    groups = [list(range(base, base + shares)) for base in range(0, tensor, shares)]
    pair_grad = lax.psum_scatter(
        pair_grad, "tensor", scatter_dimension=1, axis_index_groups=groups, tiled=True
    )
    return jnp.concatenate(
        [
            query_grad.reshape(images, rows, pairs, PAIR),
            pair_grad.reshape(images, rows, pairs, 2 * PAIR),
        ],
        axis=3,
    ).reshape(images, rows, width)


def norm_parts(values):
    centre = jnp.mean(values, axis=-1, keepdims=True)
    centred = values - centre
    spread = jnp.mean(centred * centred, axis=-1, keepdims=True)
    inverse = lax.rsqrt(spread + 1e-06)
    return centred * inverse, inverse


def norm_backward(grad, gain, normed, inverse):
    scaled = grad * gain
    return inverse * (
        scaled
        - jnp.mean(scaled, axis=-1, keepdims=True)
        - normed * jnp.mean(scaled * normed, axis=-1, keepdims=True)
    )


def gelu_parts(values):
    below = 0.5 * lax.erfc(-values * (0.5**0.5))
    density = jnp.exp(-0.5 * values * values) * 0.3989422804014327
    return values * below, below + values * density


def body(
    mesh,
    tokens,
    cotangent,
    attention_gain,
    attention_shift,
    triple_weight,
    query_bias,
    value_bias,
    merge_weight,
    merge_bias,
    attention_scale,
    forward_gain,
    forward_shift,
    expand_weight,
    expand_bias,
    reduce_weight,
    reduce_bias,
    forward_scale,
):
    tree = Tree(mesh)
    tables = tree.tables()
    count, width = tokens.shape
    segment_rows = min(count, SEQ)
    images = count // segment_rows
    shares = SEQ // segment_rows
    if images * segment_rows != count or shares * segment_rows != SEQ:
        raise ValueError("token rows")
    padded = -(-segment_rows // 128) * 128
    rows = images * padded

    def pad(values):
        shaped = values.reshape(images, segment_rows, width)
        shaped = jnp.pad(shaped, ((0, 0), (0, padded - segment_rows), (0, 0)))
        return shaped.reshape(rows, width)

    def unpad(values):
        return values.reshape(images, padded, width)[:, :segment_rows].reshape(count, width)

    vectors = [
        attention_gain,
        attention_shift,
        query_bias,
        value_bias,
        merge_bias,
        attention_scale,
        forward_gain,
        forward_shift,
        reduce_bias,
        forward_scale,
        expand_bias,
    ]
    sizes = [vector.shape[0] for vector in vectors]
    packed = jnp.concatenate(vectors)
    extent = -(-packed.shape[0] // 1024) * 1024
    packed = jnp.pad(packed, (0, extent - packed.shape[0])).astype(F32)
    gathered = tree.gather_rows(packed.reshape(-1, 128)).reshape(tree.dp, extent)
    full, at = [], 0
    for size in sizes:
        full.append(gathered[:, at : at + size].reshape(-1))
        at += size
    (
        gain_one,
        shift_one,
        query_shift,
        value_shift,
        merge_shift,
        scale_one,
        gain_two,
        shift_two,
        reduce_shift,
        scale_two,
        expand_shift,
    ) = full

    shard_rows, _, local = triple_weight.shape
    local_pairs = local // PAIR
    triple_shard = (
        triple_weight.reshape(shard_rows, 3, local_pairs, PAIR)
        .transpose(0, 2, 1, 3)
        .reshape(shard_rows, 3 * local)
    )
    (triple_full,) = tree.gather(triple_shard, tables, [3 * local])
    widths = [merge_weight.shape[1], expand_weight.shape[1], reduce_weight.shape[1]]
    merge_full, expand_full, reduce_full = tree.gather(
        jnp.concatenate([merge_weight, expand_weight, reduce_weight], axis=1), tables, widths
    )

    inputs = pad(tokens).astype(F32)
    normal_one, inverse_one = norm_parts(inputs)
    normed_one = (normal_one * gain_one + shift_one).astype(BF16)
    pairs = tree.tensor * local_pairs
    bias = jnp.stack(
        [
            query_shift.reshape(pairs, PAIR),
            jnp.zeros((pairs, PAIR), F32),
            value_shift.reshape(pairs, PAIR),
        ],
        axis=1,
    ).reshape(-1)
    triple = (dot(normed_one, triple_full, 1, 0) + bias).astype(BF16)
    triple = triple.reshape(images, padded, -1)
    pair_rows = triple
    if shares > 1:
        groups = [list(range(base, base + shares)) for base in range(0, tree.tensor, shares)]
        pair_rows = lax.all_gather(
            triple, "tensor", axis=1, axis_index_groups=groups, tiled=True
        )
    mixed, logsum = attend_forward(triple, pair_rows, padded, segment_rows)
    mixed_rows = mixed.reshape(rows, width)
    branch_one = dot(mixed_rows, merge_full, 1, 1) + merge_shift
    middle = inputs + scale_one * branch_one
    normal_two, inverse_two = norm_parts(middle)
    normed_two = (normal_two * gain_two + shift_two).astype(BF16)

    upstream = pad(cotangent).astype(F32)
    back_two = (upstream * scale_two).astype(BF16)
    gate_input = dot(normed_two, expand_full, 1, 0) + expand_shift
    activated, slope = gelu_parts(gate_input)
    activated = activated.astype(BF16)
    slope = slope.astype(BF16)
    gate_grad = (dot(back_two, reduce_full, 1, 0) * slope.astype(F32)).astype(BF16)
    branch_two = dot(activated, reduce_full, 1, 1) + reduce_shift
    result = unpad((middle + scale_two * branch_two).astype(BF16))
    reduce_grad = dot(back_two, activated, 0, 0).astype(BF16)
    expand_grad = dot(normed_two, gate_grad, 0, 0).astype(BF16)
    expand_out, reduce_out = tree.scatter([expand_grad, reduce_grad], tables)
    normed_two_grad = dot(gate_grad, expand_full, 1, 1)

    middle_grad = upstream + norm_backward(normed_two_grad, gain_two, normal_two, inverse_two)
    back_one = (middle_grad * scale_one).astype(BF16)
    mixed_grad = dot(back_one, merge_full, 1, 0).astype(BF16).reshape(images, padded, width)
    merge_grad = dot(back_one, mixed_rows, 0, 0).astype(BF16)
    (merge_out,) = tree.scatter([merge_grad], tables)
    triple_grad = attend_backward(
        triple, pair_rows, mixed, mixed_grad, logsum, padded, segment_rows
    )
    triple_grad = triple_grad.reshape(rows, -1)
    weight_grad = dot(normed_one, triple_grad, 0, 0).astype(BF16)
    (triple_out,) = tree.scatter([weight_grad], tables)
    triple_out = (
        triple_out.reshape(shard_rows, local_pairs, 3, PAIR)
        .transpose(0, 2, 1, 3)
        .reshape(shard_rows, 3, local)
    )
    normed_one_grad = dot(triple_grad, triple_full, 1, 1)
    tokens_grad = middle_grad + norm_backward(normed_one_grad, gain_one, normal_one, inverse_one)
    tokens_grad = unpad(tokens_grad.astype(BF16))

    bias_sums = jnp.sum(triple_grad, axis=0, dtype=F32).reshape(pairs, 3, PAIR)
    sums = [
        jnp.sum(normed_one_grad * normal_one, axis=0),
        jnp.sum(normed_one_grad, axis=0),
        bias_sums[:, 0].reshape(-1),
        bias_sums[:, 2].reshape(-1),
        jnp.sum(middle_grad, axis=0) * scale_one,
        jnp.sum(middle_grad * branch_one, axis=0),
        jnp.sum(normed_two_grad * normal_two, axis=0),
        jnp.sum(normed_two_grad, axis=0),
        jnp.sum(upstream, axis=0) * scale_two,
        jnp.sum(upstream * branch_two, axis=0),
        jnp.sum(gate_grad, axis=0, dtype=F32),
    ]
    columns = jnp.concatenate([total.reshape(tree.dp, -1) for total in sums], axis=1)
    columns = jnp.pad(columns, ((0, 0), (0, extent - columns.shape[1])))
    mine = tree.scatter_rows(columns.reshape(tree.dp, -1, 128)).reshape(-1)
    vector_out, at = [], 0
    for size in sizes:
        vector_out.append(mine[at : at + size])
        at += size
    return (
        result,
        tokens_grad,
        vector_out[0],
        vector_out[1],
        triple_out,
        vector_out[2],
        vector_out[3],
        merge_out,
        vector_out[4],
        vector_out[5],
        vector_out[6],
        vector_out[7],
        expand_out,
        vector_out[10],
        reduce_out,
        vector_out[8],
        vector_out[9],
    )


def solution(mesh):
    rows = P(("dp", "tensor"), None)
    vector = P("dp")
    weight = P("dp", "tensor")
    triple = P("dp", None, "tensor")
    parameters = (
        vector,
        vector,
        triple,
        vector,
        vector,
        weight,
        vector,
        vector,
        vector,
        vector,
        weight,
        vector,
        weight,
        vector,
        vector,
    )
    return jax.shard_map(
        functools.partial(body, mesh),
        mesh=mesh,
        in_specs=(rows, rows) + parameters,
        out_specs=(rows, rows) + parameters,
        check_vma=False,
    )
```

time: 3110 us -> 1180 us (0.38)
  blocking collectives: 738 us -> 0 us
  matrix products: 1090 us -> 445 us
  other arithmetic: 434 us -> 73.1 us
  Pallas kernels: 0 us -> 325 us
  waiting for transfers between devices: 461 us -> 174 us
  local copies, waits for them, and re-layouts: 345 us -> 87 us
  starting transfers between devices: 13.7 us -> 67.7 us
    unnamed x5 -> x0, blocking collectives: 690 us -> none
    dot_general x40 -> x12, matrix products: 1090 us -> 445 us  [dot(): return lax.dot_general(left, right, dims, preferred_element_type=F32)]
    all_gather x8 -> x0, waiting for transfers between devices: 367 us -> none  [the longest x1 125 us: body(): lax.all_gather(normed_one.astype(jnp.bfloat16), 'tensor', axis=0, tiled=T...]
    pallas_call x0 -> x7, Pallas kernels: none -> 325 us  [the longest x1 152 us: attend_backward(): pl.pallas_call(functools.partial(attend_backward_kernel, segment, valid,...]
    convert_element_type x13 -> x27, other arithmetic: 217 us -> 40.8 us  [the longest x24 17.4 us: scatter(): held = held.astype(BF16)]
    ppermute x0 -> x59, waiting for transfers between devices: none -> 174 us  [swap(): return lax.ppermute(value, axis, [(i, i ^ 1 << bit) for i in range(size)])]
    reduce_sum x16 -> x5, other arithmetic: 177 us -> 24 us  [the longest x2 9.96 us: norm_parts(): spread = jnp.mean(centred * centred, axis=-1, keepdims=True)]
    unnamed x124 -> x126, local copies, waits for them, and re-layouts: 167 us -> 21.6 us
  transfers between devices with their start and end apart: 17 -> 59, of which waited for: 9 -> 32; matrix products, arithmetic and copies ran while one was open for 72% -> 16% of each run, Pallas kernels for 0% -> 13%
where the time goes in v1:
time: 1180 us; the launch traced here: 1170 us
  matrix products  445 us (38%)
  Pallas kernels  325 us (28%)
  waiting for transfers between devices  174 us (15%)
  local copies, waits for them, and re-layouts  87 us (7%)
  other arithmetic  73.1 us (6%)
  starting transfers between devices  67.7 us (6%)
    dot_general x12, matrix products, dot(): return lax.dot_general(left, right, dims, preferred_element_type=F32)  445 us
    ppermute x59, waiting for transfers between devices, swap(): return lax.ppermute(value, axis, [(i, i ^ 1 << bit) for i in range(size)])  174 us
    pallas_call x1, Pallas kernels, attend_backward(): pl.pallas_call(functools.partial(attend_backward_kernel, segment, valid,...  152 us
    pallas_call x1, Pallas kernels, attend_forward(): pl.pallas_call(functools.partial(attend_forward_kernel, segment, valid),...  102 us
    ppermute x59, starting transfers between devices, swap(): return lax.ppermute(value, axis, [(i, i ^ 1 << bit) for i in range(size)])  67.7 us
    pallas_call x3, Pallas kernels, split(): pl.pallas_call(kernel, grid_spec=pltpu.PrefetchScalarGridSpec(num_scalar_...  40.2 us
    pallas_call x2, Pallas kernels, assemble(): pl.pallas_call(kernel, grid_spec=pltpu.PrefetchScalarGridSpec(num_scalar_...  31.3 us
  transfers between devices with their start and end apart: 59, of which 32 were waited for; matrix products, arithmetic and copies ran while one was open for 16% of the time, Pallas kernels for 13%

profile of v1, /device:TPU:0, one launch (start us, length us, event | category | flops | bytes accessed | tf_op | source)
XLA Modules:
  0.0 1174.0 jit_solution(14194223788350280452)
XLA Ops:
  0.7 7.4 concatenate.98
  24.6 6.1 reshape.420
  30.8 6.2 reshape.413
  40.5 4.2 fusion.17
  59.6 6.9 fusion.13
  66.6 4.8 fusion.27
  76.0 4.3 collective-permute-done.5
  103.8 9.4 collective-permute-done.20
  118.0 20.7 %collective-permute-done.16 = bf16[4,32,4608]{2,1,0:T(8,128)(2,1)S(1)} collective-permute-done((bf16[4,32,4608]{2,1,0:T(8,128)(2,1)S(1)}, bf16[4,32,4608]{2,1,0:T(8,128)(2,1)S(1)}, u32[]{:S(2)}, u32[]{:S(2)}) %collective-permute-start.16) | collective-permute-done | bytes 1179680 | tf_op jit(solution)/shard_map/ppermute | solution.py:44
  147.2 12.2 %shard_map.296 = bf16[1024,3072]{1,0:T(8,128)(2,1)} custom-call(s32[3,16]{1,0:T(4,128)} %add_add_fusion.tables_ref, bf16[16,32,1536]{2,1,0:T(8,128)(2,1)} %constant_dynamic-update-slice_fusion.5.own_a, bf16[16,32,1536]{2,1,0:T(8,128)(2,1)} %collective-permute-done.8.far_a, bf16[16,32,1536]{2,1,0:T(8,128)(2,1)} %constant_dynamic-update-slice_fusion.10.own_b, ...), custom_call_target="tpu_custom_call" | custom-call | tf_op jit(solution)/shard_map/pallas_call | solution.py:102
  159.4 23.4 %add_convert_fusion = bf16[2816,3072]{1,0:T(8,128)(2,1)} fusion(bf16[2816,1024]{1,0:T(8,128)(2,1)S(1)} %bitcast.127, bf16[1024,3072]{1,0:T(8,128)(2,1)} %shard_map.296, f32[3072]{0:T(1024)S(1)} %add.359), kind=kOutput, calls=%fused_computation.29 | convolution fusion | flops 17734041600 | bytes 29372416 | tf_op jit(solution)/shard_map/dot_general | solution.py:22
  182.8 7.6 collective-permute-done.17
  195.8 101.8 %shard_map.297 = (bf16[2,1408,1024]{2,1,0:T(8,128)(2,1)}, f32[2,1408,1024]{2,1,0:T(8,128)}) custom-call(bf16[2,1408,3072]{2,1,0:T(8,128)(2,1)} %bitcast.138, bf16[2,1408,3072]{2,1,0:T(8,128)(2,1)} %bitcast.139), custom_call_target="tpu_custom_call" | custom-call | flops 64961380352 | bytes 46137344 | tf_op jit(solution)/shard_map/pallas_call | solution.py:314
  297.5 19.1 %shard_map.298 = (bf16[1024,1024]{1,0:T(8,128)(2,1)}, bf16[1024,4096]{1,0:T(8,128)(2,1)}, bf16[1024,4096]{1,0:T(8,128)(2,1)}) custom-call(s32[3,16]{1,0:T(4,128)} %add_add_fusion.tables_ref, bf16[16,32,4608]{2,1,0:T(8,128)(2,1)} %constant_dynamic-update-slice_fusion.18.own_a, bf16[16,32,4608]{2,1,0:T(8,128)(2,1)} %collective-permute-done.18.far_a, ...), custom_call_target="tpu_custom_call" | custom-call | tf_op jit(solution)/shard_map/pallas_call | solution.py:102
  316.7 15.1 %fusion.53 = (f32[2816]{0:T(1024)S(1)}, f32[2816,1024]{1,0:T(8,128)}, f32[2816,1024]{1,0:T(8,128)}) fusion(f32[1024]{0:T(1024)S(1)} %add.362, f32[1024]{0:T(1024)S(1)} %mul.187, bf16[2,1370,1024]{2,1,0:T(8,128)(2,1)S(1)} %bitcast.119, bf16[2816,1024]{1,0:T(8,128)(2,1)} %bitcast.142, bf16[1024,1024]{1,0:T(8,128)(2,1)} %get-tuple-element.35), kind=kOutput, calls=%fused_computation.208 | convolution fusion | flops 5919994880 | bytes 36563968 | tf_op jit(solution)/shard_map/dot_general | solution.py:22
  331.7 5.7 multiply_reduce_fusion.3
  339.3 130.6 %multiply_convert_fusion.1 = (bf16[2816,4096]{1,0:T(8,128)(2,1)}, f32[2816,4096]{1,0:T(8,128)}, f32[2816,4096]{1,0:T(8,128)}) fusion(f32[4096]{0:T(1024)S(1)} %bitcast.136, bf16[1024,4096]{1,0:T(8,128)(2,1)} %get-tuple-element.36, f32[2816,1024]{1,0:T(8,128)S(1)} %copy-done.2, f32[1024]{0:T(1024)S(1)} %add.367, f32[1024]{0:T(1024)S(1)} %mul.201, ...), kind=kOutput, calls=%fused_computation.13 | convolution fusion | flops 24398004224 | bytes 135313408 | tf_op jit(solution)/shard_map/dot_general | solution.py:22
  469.9 49.4 %convert_reduce_fusion = (f32[4096]{0:T(1024)}, bf16[2816,4096]{1,0:T(8,128)(2,1)}) fusion(f32[2816,4096]{1,0:T(8,128)} %get-tuple-element.65, f32[2816,4096]{1,0:T(8,128)} %get-tuple-element.104, f32[4096]{0:T(1024)S(1)} %bitcast.137, bf16[2816,1024]{1,0:T(8,128)(2,1)} %fusion.13, bf16[1024,4096]{1,0:T(8,128)(2,1)} %get-tuple-element.37), kind=kOutput, calls=%fused_computation.11 | convolution fusion | flops 23760728064 | bytes 129531904 | tf_op jit(solution)/shard_map/dot_general | solution.py:22
  519.3 37.8 %multiply_reduce_fusion = (f32[1024]{0:T(1024)}, f32[2816]{0:T(1024)S(1)}, f32[2816]{0:T(1024)S(1)}, f32[1024]{0:T(1024)}, f32[2816,1024]{1,0:T(8,128)}) fusion(f32[2816,1024]{1,0:T(8,128)} %get-tuple-element.67, f32[2816]{0:T(1024)S(1)} %add_rsqrt_fusion, f32[2816]{0:T(1024)S(1)} %broadcast_multiply_fusion.4, f32[1024]{0:T(1024)S(1)} %mul.201, ...), kind=kOutput, calls=%fused_computation.60 | convolution fusion | flops 23648268288 | bytes 54583296 | tf_op jit(solution)/shard_map/dot_general | solution.py:22
  557.1 36.9 %convolution_convert_fusion.1.refs_0_ = bf16[1024,4096]{1,0:T(8,128)(2,1)} fusion(bf16[2816,4096]{1,0:T(8,128)(2,1)} %get-tuple-element.108, f32[2816,1024]{1,0:T(8,128)} %get-tuple-element.67, f32[1024]{0:T(1024)S(1)} %add.367, f32[1024]{0:T(1024)S(1)} %mul.201, f32[2816]{0:T(1024)S(1)} %add_rsqrt_fusion, f32[2816]{0:T(1024)S(1)} %broadcast_multiply_fusion.4), kind=kOutput, calls=%fused_computation.73 | convolution fusion | flops 23640932352 | bytes 43022336 | tf_op jit(solution)/shard_map/dot_general | solution.py:22
  594.0 31.0 %convolution_convert_fusion.refs_1_ = bf16[1024,4096]{1,0:T(8,128)(2,1)} fusion(bf16[2816,1024]{1,0:T(8,128)(2,1)} %fusion.13, bf16[2816,4096]{1,0:T(8,128)(2,1)} %get-tuple-element.64), kind=kOutput, calls=%fused_computation.72 | convolution fusion | flops 23626514432 | bytes 37224448 | tf_op jit(solution)/shard_map/dot_general | solution.py:22
  625.1 38.8 %fusion.14 = (f32[1024]{0:T(1024)}, bf16[2816,1024]{1,0:T(8,128)(2,1)}, f32[1024]{0:T(1024)}, f32[1024]{0:T(1024)}, f32[2816,1024]{1,0:T(8,128)}) fusion(f32[1024]{0:T(1024)S(1)} %copy-done.30, bf16[2,1370,1024]{2,1,0:T(8,128)(2,1)S(1)} %bitcast.123, f32[2816,1024]{1,0:T(8,128)} %get-tuple-element.67, f32[1024]{0:T(1024)S(1)} %copy-done.25, ...), kind=kOutput, calls=%fused_computation.36 | convolution fusion | flops 23677108224 | bytes 89047040 | tf_op jit(solution)/shard_map/dot_general | solution.py:22
  663.9 12.3 %convolution_convert_fusion.2 = bf16[2816,1024]{1,0:T(8,128)(2,1)} fusion(bf16[1024,1024]{1,0:T(8,128)(2,1)S(1)} %copy-done.38, f32[2816,1024]{1,0:T(8,128)} %get-tuple-element.72, f32[1024]{0:T(1024)S(1)} %copy-done.28), kind=kOutput, calls=%fused_computation.78 | convolution fusion | flops 5914230784 | bytes 19402752 | tf_op jit(solution)/shard_map/dot_general | solution.py:22
  676.2 152.2 %shard_map.299 = bf16[2,1408,3072]{2,1,0:T(8,128)(2,1)} custom-call(bf16[2,1408,3072]{2,1,0:T(8,128)(2,1)} %bitcast.140, bf16[2,1408,3072]{2,1,0:T(8,128)(2,1)} %bitcast.141, bf16[2,1408,1024]{2,1,0:T(8,128)(2,1)} %get-tuple-element.34.mixed_ref, bf16[2,1408,1024]{2,1,0:T(8,128)(2,1)} %bitcast.144, f32[2,1408,1024]{2,1,0:T(8,128)} %get-tuple-element.38.logsum_ref), custom_call_target="tpu_custom_call" | custom-call | flops 162403450880 | bytes 46137344 | tf_op jit(solution)/shard_map/pallas_call | solution.py:352
  828.4 7.1 convert_reduce_fusion.1
  835.6 29.8 %fusion.33 = (f32[1024]{0:T(1024)S(1)}, f32[2816]{0:T(1024)S(1)}, f32[2816]{0:T(1024)S(1)}, f32[1024]{0:T(1024)S(1)}, f32[2816,1024]{1,0:T(8,128)}) fusion(f32[2816]{0:T(1024)S(1)} %copy-done.14, f32[2816]{0:T(1024)S(1)} %copy-done.12, bf16[2,1370,1024]{2,1,0:T(8,128)(2,1)} %reshape.413, f32[1024]{0:T(1024)S(1)} %copy-done.20, ...), kind=kOutput, calls=%fused_computation.59 | convolution fusion | flops 17745571840 | bytes 40796160 | tf_op jit(solution)/shard_map/dot_general | solution.py:22
  869.3 27.6 %bitcast_convert_fusion.refs_0_ = bf16[1024,3072]{1,0:T(8,128)(2,1)} fusion(bf16[2,1408,3072]{2,1,0:T(8,128)(2,1)} %shard_map.299, f32[1024]{0:T(1024)S(1)} %copy-done.23, f32[1024]{0:T(1024)S(1)} %copy-done.20, f32[2,1408]{1,0:T(2,128)S(1)} %copy-done.18, f32[2,1408]{1,0:T(2,128)S(1)} %copy-done.16, bf16[2,1370,1024]{2,1,0:T(8,128)(2,1)} %reshape.413), kind=kOutput, calls=%fused_computation.30 | convolution fusion | flops 17737187328 | bytes 29235200 | tf_op jit(solution)/shard_map/dot_general | solution.py:22
  897.4 11.9 %fusion.40.refs_0_ = bf16[1024,1024]{1,0:T(8,128)(2,1)} fusion(bf16[2816,1024]{1,0:T(8,128)(2,1)} %bitcast.143, f32[2816,1024]{1,0:T(8,128)} %get-tuple-element.72, f32[1024]{0:T(1024)S(1)} %copy-done.29), kind=kOutput, calls=%fused_computation.88 | convolution fusion | flops 5912395776 | bytes 19402752 | tf_op jit(solution)/shard_map/dot_general | solution.py:22
  914.6 10.1 shard_map.301
  925.2 11.6 fusion.32
  936.9 5.6 slice.377
  942.5 6.2 reshape.419
  948.7 5.6 slice.378
  954.3 6.2 reshape.424
  960.5 11.9 %shard_map.300 = (bf16[16,32,1536]{2,1,0:T(8,128)(2,1)}, bf16[16,32,1536]{2,1,0:T(8,128)(2,1)}, bf16[16,32,1536]{2,1,0:T(8,128)(2,1)}, bf16[16,32,1536]{2,1,0:T(8,128)(2,1)}) custom-call(s32[3,16]{1,0:T(4,128)} %add_add_fusion.tables_ref, bf16[1024,3072]{1,0:T(8,128)(2,1)} %bitcast_convert_fusion.refs_0_), custom_call_target="tpu_custom_call" | custom-call | tf_op jit(solution)/shard_map/pallas_call | solution.py:149
  973.0 18.2 %shard_map.302 = (bf16[16,32,4096]{2,1,0:T(8,128)(2,1)}, bf16[16,32,4096]{2,1,0:T(8,128)(2,1)}, bf16[16,32,4096]{2,1,0:T(8,128)(2,1)}, bf16[16,32,4096]{2,1,0:T(8,128)(2,1)}) custom-call(s32[3,16]{1,0:T(4,128)} %add_add_fusion.tables_ref, bf16[1024,4096]{1,0:T(8,128)(2,1)} %convolution_convert_fusion.1.refs_0_, ...), custom_call_target="tpu_custom_call" | custom-call | tf_op jit(solution)/shard_map/pallas_call | solution.py:149
  994.9 6.0 collective-permute-done.45
  1002.4 4.5 collective-permute-done.46
  1034.8 11.6 collective-permute-done.35
  1047.1 4.2 collective-permute-done.30
  1077.7 4.2 collective-permute-done.33
  1082.7 26.0 %collective-permute-done.55 = bf16[8,32,4096]{2,1,0:T(8,128)(2,1)} collective-permute-done((bf16[8,32,4096]{2,1,0:T(8,128)(2,1)}, bf16[8,32,4096]{2,1,0:T(8,128)(2,1)}, u32[]{:S(2)}, u32[]{:S(2)}) %collective-permute-start.55) | collective-permute-done | bytes 2097184 | tf_op jit(solution)/shard_map/ppermute | solution.py:44
  1113.2 7.7 collective-permute-done.50
  1131.0 5.6 collective-permute-done.56
  1138.2 4.7 collective-permute-done.51
  1146.1 6.5 collective-permute-done.57
  1154.7 8.8 collective-permute-done.52
  1166.5 6.1 collective-permute-done.53
  (383 shorter events, 180.2 us)
Async XLA Ops:
  8.1 41.0 %collective-permute-start = (f32[1,8,128]{2,1,0:T(8,128)S(1)}, f32[1,8,128]{2,1,0:T(8,128)S(1)}, u32[]{:S(2)}, u32[]{:S(2)}) collective-permute-start(f32[1,8,128]{2,1,0:T(8,128)S(1)} %bitcast_convert_fusion.1), channel_id=1, source_target_pairs={{0,16},{2,18},{4,20},{6,22},{8,24},{10,26},{12,28},{14,30},{16,0},... | collective-permute-start | bytes 12296 | tf_op jit(solution)/shard_map/ppermute | solution.py:44
  13.5 59.0 %collective-permute-start.4 = (bf16[1,32,1536]{2,1,0:T(8,128)(2,1)S(1)}, bf16[1,32,1536]{2,1,0:T(8,128)(2,1)S(1)}, u32[]{:S(2)}, u32[]{:S(2)}) collective-permute-start(bf16[1,32,1536]{2,1,0:T(8,128)(2,1)S(1)} %broadcast_in_dim.8), channel_id=1, source_target_pairs={{0,16},{2,18},{4,20},{6,22},{8,24},{10,26},{12,28},{14,30},{16,0},... | collective-permute-start | bytes 294920 | tf_op jit(solution)/shard_map/ppermute | solution.py:44
  13.7 60.5 %collective-permute-start.9 = (bf16[1,32,1536]{2,1,0:T(8,128)(2,1)S(1)}, bf16[1,32,1536]{2,1,0:T(8,128)(2,1)S(1)}, u32[]{:S(2)}, u32[]{:S(2)}) collective-permute-start(bf16[1,32,1536]{2,1,0:T(8,128)(2,1)S(1)} %broadcast_in_dim.9), channel_id=1, source_target_pairs={{0,16},{2,18},{4,20},{6,22},{8,24},{10,26},{12,28},{14,30},{16,0},... | collective-permute-start | bytes 294920 | tf_op jit(solution)/shard_map/ppermute | solution.py:44
  19.5 66.2 %collective-permute-start.14 = (bf16[1,32,4608]{2,1,0:T(8,128)(2,1)S(1)}, bf16[1,32,4608]{2,1,0:T(8,128)(2,1)S(1)}, u32[]{:S(2)}, u32[]{:S(2)}) collective-permute-start(bf16[1,32,4608]{2,1,0:T(8,128)(2,1)S(1)} %get-tuple-element.76), channel_id=1, source_target_pairs={{0,16},{2,18},{4,20},{6,22},{8,24},{10,26},{12,28},{14,30},{16,0},... | collective-permute-start | bytes 884744 | tf_op jit(solution)/shard_map/ppermute | solution.py:44
  19.6 67.9 %collective-permute-start.19 = (bf16[1,32,4608]{2,1,0:T(8,128)(2,1)S(1)}, bf16[1,32,4608]{2,1,0:T(8,128)(2,1)S(1)}, u32[]{:S(2)}, u32[]{:S(2)}) collective-permute-start(bf16[1,32,4608]{2,1,0:T(8,128)(2,1)S(1)} %get-tuple-element.75), channel_id=1, source_target_pairs={{0,16},{2,18},{4,20},{6,22},{8,24},{10,26},{12,28},{14,30},{16,0},... | collective-permute-start | bytes 884744 | tf_op jit(solution)/shard_map/ppermute | solution.py:44
  72.5 7.8 collective-permute-start.5
  74.2 9.9 collective-permute-start.10
  80.3 10.5 collective-permute-start.6
  84.2 12.1 %collective-permute-start.11 = (bf16[4,32,1536]{2,1,0:T(8,128)(2,1)S(1)}, bf16[4,32,1536]{2,1,0:T(8,128)(2,1)S(1)}, u32[]{:S(2)}, u32[]{:S(2)}) collective-permute-start(bf16[4,32,1536]{2,1,0:T(8,128)(2,1)S(1)} %pad_maximum_fusion.10), channel_id=1, source_target_pairs={{0,1},{1,0},{2,3},{3,2},{4,5},{5,4},{6,7},{7,6},{8,9},{9,8},{10,11... | collective-permute-start | bytes 1179656 | tf_op jit(solution)/shard_map/ppermute | solution.py:44
  85.8 16.3 %collective-permute-start.15 = (bf16[2,32,4608]{2,1,0:T(8,128)(2,1)S(1)}, bf16[2,32,4608]{2,1,0:T(8,128)(2,1)S(1)}, u32[]{:S(2)}, u32[]{:S(2)}) collective-permute-start(bf16[2,32,4608]{2,1,0:T(8,128)(2,1)S(1)} %pad_maximum_fusion.6), channel_id=1, source_target_pairs={{0,8},{2,10},{4,12},{6,14},{8,0},{10,2},{12,4},{14,6},{16,24},{18,... | collective-permute-start | bytes 1769480 | tf_op jit(solution)/shard_map/ppermute | solution.py:44
  87.5 25.7 %collective-permute-start.20 = (bf16[2,32,4608]{2,1,0:T(8,128)(2,1)S(1)}, bf16[2,32,4608]{2,1,0:T(8,128)(2,1)S(1)}, u32[]{:S(2)}, u32[]{:S(2)}) collective-permute-start(bf16[2,32,4608]{2,1,0:T(8,128)(2,1)S(1)} %pad_maximum_fusion.7), channel_id=1, source_target_pairs={{0,8},{2,10},{4,12},{6,14},{8,0},{10,2},{12,4},{14,6},{16,24},{18,... | collective-permute-start | bytes 1769480 | tf_op jit(solution)/shard_map/ppermute | solution.py:44
  91.0 24.6 %collective-permute-start.7 = (bf16[8,32,1536]{2,1,0:T(8,128)(2,1)S(1)}, bf16[8,32,1536]{2,1,0:T(8,128)(2,1)S(1)}, u32[]{:S(2)}, u32[]{:S(2)}) collective-permute-start(bf16[8,32,1536]{2,1,0:T(8,128)(2,1)S(1)} %pad_maximum_fusion.4), channel_id=1, source_target_pairs={{0,1},{1,0},{2,3},{3,2},{4,5},{5,4},{6,7},{7,6},{8,9},{9,8},{10,11... | collective-permute-start | bytes 2359304 | tf_op jit(solution)/shard_map/ppermute | solution.py:44
  96.3 20.5 %collective-permute-start.12 = (bf16[8,32,1536]{2,1,0:T(8,128)(2,1)S(1)}, bf16[8,32,1536]{2,1,0:T(8,128)(2,1)S(1)}, u32[]{:S(2)}, u32[]{:S(2)}) collective-permute-start(bf16[8,32,1536]{2,1,0:T(8,128)(2,1)S(1)} %pad_maximum_fusion.5), channel_id=1, source_target_pairs={{0,4},{2,6},{4,0},{6,2},{8,12},{10,14},{12,8},{14,10},{16,20},{18,... | collective-permute-start | bytes 2359304 | tf_op jit(solution)/shard_map/ppermute | solution.py:44
  102.3 36.4 %collective-permute-start.16 = (bf16[4,32,4608]{2,1,0:T(8,128)(2,1)S(1)}, bf16[4,32,4608]{2,1,0:T(8,128)(2,1)S(1)}, u32[]{:S(2)}, u32[]{:S(2)}) collective-permute-start(bf16[4,32,4608]{2,1,0:T(8,128)(2,1)S(1)} %pad_maximum_fusion.2), channel_id=1, source_target_pairs={{0,4},{2,6},{4,0},{6,2},{8,12},{10,14},{12,8},{14,10},{16,20},{18,... | collective-permute-start | bytes 3538952 | tf_op jit(solution)/shard_map/ppermute | solution.py:44
  113.3 28.5 %collective-permute-start.21 = (bf16[4,32,4608]{2,1,0:T(8,128)(2,1)S(1)}, bf16[4,32,4608]{2,1,0:T(8,128)(2,1)S(1)}, u32[]{:S(2)}, u32[]{:S(2)}) collective-permute-start(bf16[4,32,4608]{2,1,0:T(8,128)(2,1)S(1)} %pad_maximum_fusion.3), channel_id=1, source_target_pairs={{0,1},{1,0},{2,3},{3,2},{4,5},{5,4},{6,7},{7,6},{8,9},{9,8},{10,11... | collective-permute-start | bytes 3538952 | tf_op jit(solution)/shard_map/ppermute | solution.py:44
  116.5 30.7 %collective-permute-start.8 = (bf16[16,32,1536]{2,1,0:T(8,128)(2,1)}, bf16[16,32,1536]{2,1,0:T(8,128)(2,1)}, u32[]{:S(2)}, u32[]{:S(2)}) collective-permute-start(bf16[16,32,1536]{2,1,0:T(8,128)(2,1)} %constant_dynamic-update-slice_fusion.5.own_a), channel_id=1, source_target_pairs={{0,2},{2,0},{4,6},{6,4},{8,10},{10,8},{12,14},{14,12},{16,18},{18,... | collective-permute-start | bytes 4718600 | tf_op jit(solution)/shard_map/ppermute | solution.py:44
  117.8 29.4 %collective-permute-start.13 = (bf16[16,32,1536]{2,1,0:T(8,128)(2,1)}, bf16[16,32,1536]{2,1,0:T(8,128)(2,1)}, u32[]{:S(2)}, u32[]{:S(2)}) collective-permute-start(bf16[16,32,1536]{2,1,0:T(8,128)(2,1)} %constant_dynamic-update-slice_fusion.10.own_b), channel_id=1, source_target_pairs={{0,2},{2,0},{4,6},{6,4},{8,10},{10,8},{12,14},{14,12},{16,18},{18,... | collective-permute-start | bytes 4718600 | tf_op jit(solution)/shard_map/ppermute | solution.py:44
  140.3 50.1 %collective-permute-start.17 = (bf16[8,32,4608]{2,1,0:T(8,128)(2,1)}, bf16[8,32,4608]{2,1,0:T(8,128)(2,1)}, u32[]{:S(2)}, u32[]{:S(2)}) collective-permute-start(bf16[8,32,4608]{2,1,0:T(8,128)(2,1)} %pad_maximum_fusion), channel_id=1, source_target_pairs={{0,1},{1,0},{2,3},{3,2},{4,5},{5,4},{6,7},{7,6},{8,9},{9,8},{10,11... | collective-permute-start | bytes 7077896 | tf_op jit(solution)/shard_map/ppermute | solution.py:44
  143.5 50.2 %collective-permute-start.22 = (bf16[8,32,4608]{2,1,0:T(8,128)(2,1)}, bf16[8,32,4608]{2,1,0:T(8,128)(2,1)S(1)}, u32[]{:S(2)}, u32[]{:S(2)}) collective-permute-start(bf16[8,32,4608]{2,1,0:T(8,128)(2,1)} %pad_maximum_fusion.1), channel_id=1, source_target_pairs={{0,4},{2,6},{4,0},{6,2},{8,12},{10,14},{12,8},{14,10},{16,20},{18,... | collective-permute-start | bytes 7077896 | tf_op jit(solution)/shard_map/ppermute | solution.py:44
  193.7 103.8 %collective-permute-start.18 = (bf16[16,32,4608]{2,1,0:T(8,128)(2,1)}, bf16[16,32,4608]{2,1,0:T(8,128)(2,1)}, u32[]{:S(2)}, u32[]{:S(2)}) collective-permute-start(bf16[16,32,4608]{2,1,0:T(8,128)(2,1)} %constant_dynamic-update-slice_fusion.18.own_a), channel_id=1, source_target_pairs={{0,2},{2,0},{4,6},{6,4},{8,10},{10,8},{12,14},{14,12},{16,18},{18,... | collective-permute-start | bytes 14155784 | tf_op jit(solution)/shard_map/ppermute | solution.py:44
  195.2 102.3 %collective-permute-start.23 = (bf16[16,32,4608]{2,1,0:T(8,128)(2,1)}, bf16[16,32,4608]{2,1,0:T(8,128)(2,1)}, u32[]{:S(2)}, u32[]{:S(2)}) collective-permute-start(bf16[16,32,4608]{2,1,0:T(8,128)(2,1)} %constant_dynamic-update-slice_fusion.23.own_b), channel_id=1, source_target_pairs={{0,2},{2,0},{4,6},{6,4},{8,10},{10,8},{12,14},{14,12},{16,18},{18,... | collective-permute-start | bytes 14155784 | tf_op jit(solution)/shard_map/ppermute | solution.py:44
  867.7 29.2 %collective-permute-start.24 = (f32[16,8,128]{2,1,0:T(8,128)S(1)}, f32[16,8,128]{2,1,0:T(8,128)S(1)}, u32[]{:S(2)}, u32[]{:S(2)}) collective-permute-start(f32[16,8,128]{2,1,0:T(8,128)S(1)} %gather_fusion.1), channel_id=1, source_target_pairs={{0,1},{1,0},{2,3},{3,2},{4,5},{5,4},{6,7},{7,6},{8,9},{9,8},{10,11... | collective-permute-start | bytes 196616 | tf_op jit(solution)/shard_map/ppermute | solution.py:44
  897.0 12.3 %collective-permute-start.25 = (f32[8,8,128]{2,1,0:T(8,128)S(1)}, f32[8,8,128]{2,1,0:T(8,128)S(1)}, u32[]{:S(2)}, u32[]{:S(2)}) collective-permute-start(f32[8,8,128]{2,1,0:T(8,128)S(1)} %slice.382), channel_id=1, source_target_pairs={{0,16},{2,18},{4,20},{6,22},{8,24},{10,26},{12,28},{14,30},{16,0},... | collective-permute-start | bytes 98312 | tf_op jit(solution)/shard_map/ppermute | solution.py:44
  913.1 11.6 collective-permute-start.27
  924.6 67.6 %collective-permute-start.44 = (bf16[16,32,512]{2,1,0:T(8,128)(2,1)}, bf16[16,32,512]{2,1,0:T(8,128)(2,1)S(1)}, u32[]{:S(2)}, u32[]{:S(2)}) collective-permute-start(bf16[16,32,512]{2,1,0:T(8,128)(2,1)} %get-tuple-element.46), channel_id=1, source_target_pairs={{0,2},{2,0},{4,6},{6,4},{8,10},{10,8},{12,14},{14,12},{16,18},{18,... | collective-permute-start | bytes 1572872 | tf_op jit(solution)/shard_map/ppermute | solution.py:44
  924.7 66.5 %collective-permute-start.28 = (f32[1,8,128]{2,1,0:T(8,128)S(1)}, f32[1,8,128]{2,1,0:T(8,128)S(1)}, u32[]{:S(2)}, u32[]{:S(2)}) collective-permute-start(f32[1,8,128]{2,1,0:T(8,128)S(1)} %slice.388), channel_id=1, source_target_pairs={{0,2},{2,0},{4,6},{6,4},{8,10},{10,8},{12,14},{14,12},{16,18},{18,... | collective-permute-start | bytes 12296 | tf_op jit(solution)/shard_map/ppermute | solution.py:44
  972.4 55.8 %collective-permute-start.34 = (bf16[16,32,1536]{2,1,0:T(8,128)(2,1)}, bf16[16,32,1536]{2,1,0:T(8,128)(2,1)}, u32[]{:S(2)}, u32[]{:S(2)}) collective-permute-start(bf16[16,32,1536]{2,1,0:T(8,128)(2,1)} %get-tuple-element.42), channel_id=1, source_target_pairs={{0,2},{2,0},{4,6},{6,4},{8,10},{10,8},{12,14},{14,12},{16,18},{18,... | collective-permute-start | bytes 4718600 | tf_op jit(solution)/shard_map/ppermute | solution.py:44
  972.4 59.3 %collective-permute-start.29 = (bf16[16,32,1536]{2,1,0:T(8,128)(2,1)}, bf16[16,32,1536]{2,1,0:T(8,128)(2,1)}, u32[]{:S(2)}, u32[]{:S(2)}) collective-permute-start(bf16[16,32,1536]{2,1,0:T(8,128)(2,1)} %get-tuple-element.40), channel_id=1, source_target_pairs={{0,2},{2,0},{4,6},{6,4},{8,10},{10,8},{12,14},{14,12},{16,18},{18,... | collective-permute-start | bytes 4718600 | tf_op jit(solution)/shard_map/ppermute | solution.py:44
  972.9 20.2 %collective-permute-start.39 = (bf16[16,32,512]{2,1,0:T(8,128)(2,1)S(1)}, bf16[16,32,512]{2,1,0:T(8,128)(2,1)S(1)}, u32[]{:S(2)}, u32[]{:S(2)}) collective-permute-start(bf16[16,32,512]{2,1,0:T(8,128)(2,1)S(1)} %copy-done.39), channel_id=1, source_target_pairs={{0,2},{2,0},{4,6},{6,4},{8,10},{10,8},{12,14},{14,12},{16,18},{18,... | collective-permute-start | bytes 1572872 | tf_op jit(solution)/shard_map/ppermute | solution.py:44
  991.2 71.7 %collective-permute-start.54 = (bf16[16,32,4096]{2,1,0:T(8,128)(2,1)}, bf16[16,32,4096]{2,1,0:T(8,128)(2,1)S(1)}, u32[]{:S(2)}, u32[]{:S(2)}) collective-permute-start(bf16[16,32,4096]{2,1,0:T(8,128)(2,1)} %get-tuple-element.50), channel_id=1, source_target_pairs={{0,2},{2,0},{4,6},{6,4},{8,10},{10,8},{12,14},{14,12},{16,18},{18,... | collective-permute-start | bytes 12582920 | tf_op jit(solution)/shard_map/ppermute | solution.py:44
  992.5 8.4 collective-permute-start.45
  993.3 8.2 collective-permute-start.40
  1000.9 68.5 %collective-permute-start.49 = (bf16[16,32,4096]{2,1,0:T(8,128)(2,1)}, bf16[16,32,4096]{2,1,0:T(8,128)(2,1)S(1)}, u32[]{:S(2)}, u32[]{:S(2)}) collective-permute-start(bf16[16,32,4096]{2,1,0:T(8,128)(2,1)} %get-tuple-element.48), channel_id=1, source_target_pairs={{0,2},{2,0},{4,6},{6,4},{8,10},{10,8},{12,14},{14,12},{16,18},{18,... | collective-permute-start | bytes 12582920 | tf_op jit(solution)/shard_map/ppermute | solution.py:44
  1026.1 8.0 collective-permute-start.43
  1030.7 15.7 %collective-permute-start.35 = (bf16[8,32,1536]{2,1,0:T(8,128)(2,1)S(1)}, bf16[8,32,1536]{2,1,0:T(8,128)(2,1)S(1)}, u32[]{:S(2)}, u32[]{:S(2)}) collective-permute-start(bf16[8,32,1536]{2,1,0:T(8,128)(2,1)S(1)} %slice.398), channel_id=1, source_target_pairs={{0,4},{2,6},{4,0},{6,2},{8,12},{10,14},{12,8},{14,10},{16,20},{18,... | collective-permute-start | bytes 2359304 | tf_op jit(solution)/shard_map/ppermute | solution.py:44
  1033.6 17.7 %collective-permute-start.30 = (bf16[8,32,1536]{2,1,0:T(8,128)(2,1)S(1)}, bf16[8,32,1536]{2,1,0:T(8,128)(2,1)S(1)}, u32[]{:S(2)}, u32[]{:S(2)}) collective-permute-start(bf16[8,32,1536]{2,1,0:T(8,128)(2,1)S(1)} %slice.390), channel_id=1, source_target_pairs={{0,1},{1,0},{2,3},{3,2},{4,5},{5,4},{6,7},{7,6},{8,9},{9,8},{10,11... | collective-permute-start | bytes 2359304 | tf_op jit(solution)/shard_map/ppermute | solution.py:44
  1046.7 8.9 collective-permute-start.36
  1051.6 7.8 collective-permute-start.31
  1059.6 15.5 %collective-permute-start.32 = (bf16[2,32,1536]{2,1,0:T(8,128)(2,1)S(1)}, bf16[2,32,1536]{2,1,0:T(8,128)(2,1)S(1)}, u32[]{:S(2)}, u32[]{:S(2)}) collective-permute-start(bf16[2,32,1536]{2,1,0:T(8,128)(2,1)S(1)} %slice.394), channel_id=1, source_target_pairs={{0,8},{2,10},{4,12},{6,14},{8,0},{10,2},{12,4},{14,6},{16,24},{18,... | collective-permute-start | bytes 589832 | tf_op jit(solution)/shard_map/ppermute | solution.py:44
  1062.2 15.3 %collective-permute-start.38 = (bf16[1,32,1536]{2,1,0:T(8,128)(2,1)S(1)}, bf16[1,32,1536]{2,1,0:T(8,128)(2,1)S(1)}, u32[]{:S(2)}, u32[]{:S(2)}) collective-permute-start(bf16[1,32,1536]{2,1,0:T(8,128)(2,1)S(1)} %slice.404), channel_id=1, source_target_pairs={{0,16},{2,18},{4,20},{6,22},{8,24},{10,26},{12,28},{14,30},{16,0},... | collective-permute-start | bytes 294920 | tf_op jit(solution)/shard_map/ppermute | solution.py:44
  1068.2 40.5 %collective-permute-start.55 = (bf16[8,32,4096]{2,1,0:T(8,128)(2,1)}, bf16[8,32,4096]{2,1,0:T(8,128)(2,1)}, u32[]{:S(2)}, u32[]{:S(2)}) collective-permute-start(bf16[8,32,4096]{2,1,0:T(8,128)(2,1)} %slice.430), channel_id=1, source_target_pairs={{0,4},{2,6},{4,0},{6,2},{8,12},{10,14},{12,8},{14,10},{16,20},{18,... | collective-permute-start | bytes 6291464 | tf_op jit(solution)/shard_map/ppermute | solution.py:44
  1074.7 46.2 %collective-permute-start.50 = (bf16[8,32,4096]{2,1,0:T(8,128)(2,1)}, bf16[8,32,4096]{2,1,0:T(8,128)(2,1)}, u32[]{:S(2)}, u32[]{:S(2)}) collective-permute-start(bf16[8,32,4096]{2,1,0:T(8,128)(2,1)} %slice.422), channel_id=1, source_target_pairs={{0,1},{1,0},{2,3},{3,2},{4,5},{5,4},{6,7},{7,6},{8,9},{9,8},{10,11... | collective-permute-start | bytes 6291464 | tf_op jit(solution)/shard_map/ppermute | solution.py:44
  1112.8 23.8 %collective-permute-start.56 = (bf16[4,32,4096]{2,1,0:T(8,128)(2,1)}, bf16[4,32,4096]{2,1,0:T(8,128)(2,1)S(1)}, u32[]{:S(2)}, u32[]{:S(2)}) collective-permute-start(bf16[4,32,4096]{2,1,0:T(8,128)(2,1)} %slice.432), channel_id=1, source_target_pairs={{0,1},{1,0},{2,3},{3,2},{4,5},{5,4},{6,7},{7,6},{8,9},{9,8},{10,11... | collective-permute-start | bytes 3145736 | tf_op jit(solution)/shard_map/ppermute | solution.py:44
  1126.2 16.7 %collective-permute-start.51 = (bf16[4,32,4096]{2,1,0:T(8,128)(2,1)}, bf16[4,32,4096]{2,1,0:T(8,128)(2,1)}, u32[]{:S(2)}, u32[]{:S(2)}) collective-permute-start(bf16[4,32,4096]{2,1,0:T(8,128)(2,1)} %slice.424), channel_id=1, source_target_pairs={{0,4},{2,6},{4,0},{6,2},{8,12},{10,14},{12,8},{14,10},{16,20},{18,... | collective-permute-start | bytes 3145736 | tf_op jit(solution)/shard_map/ppermute | solution.py:44
  1136.8 15.7 %collective-permute-start.57 = (bf16[2,32,4096]{2,1,0:T(8,128)(2,1)S(1)}, bf16[2,32,4096]{2,1,0:T(8,128)(2,1)S(1)}, u32[]{:S(2)}, u32[]{:S(2)}) collective-permute-start(bf16[2,32,4096]{2,1,0:T(8,128)(2,1)S(1)} %slice.434), channel_id=1, source_target_pairs={{0,8},{2,10},{4,12},{6,14},{8,0},{10,2},{12,4},{14,6},{16,24},{18,... | collective-permute-start | bytes 1572872 | tf_op jit(solution)/shard_map/ppermute | solution.py:44
  1144.8 18.8 %collective-permute-start.52 = (bf16[2,32,4096]{2,1,0:T(8,128)(2,1)S(1)}, bf16[2,32,4096]{2,1,0:T(8,128)(2,1)S(1)}, u32[]{:S(2)}, u32[]{:S(2)}) collective-permute-start(bf16[2,32,4096]{2,1,0:T(8,128)(2,1)S(1)} %slice.426), channel_id=1, source_target_pairs={{0,8},{2,10},{4,12},{6,14},{8,0},{10,2},{12,4},{14,6},{16,24},{18,... | collective-permute-start | bytes 1572872 | tf_op jit(solution)/shard_map/ppermute | solution.py:44
  1152.7 13.7 %collective-permute-start.58 = (bf16[1,32,4096]{2,1,0:T(8,128)(2,1)S(1)}, bf16[1,32,4096]{2,1,0:T(8,128)(2,1)S(1)}, u32[]{:S(2)}, u32[]{:S(2)}) collective-permute-start(bf16[1,32,4096]{2,1,0:T(8,128)(2,1)S(1)} %slice.436), channel_id=1, source_target_pairs={{0,16},{2,18},{4,20},{6,22},{8,24},{10,26},{12,28},{14,30},{16,0},... | collective-permute-start | bytes 786440 | tf_op jit(solution)/shard_map/ppermute | solution.py:44
  1163.8 8.8 collective-permute-start.53
  (61 other events, 1878.7 us)

commit v2 on v1

--- a/solution.py
+++ b/solution.py
@@ -30,18 +30,36 @@
         tensor_bits = self.tensor.bit_length() - 1
         if 1 << dp_bits != self.dp or 1 << tensor_bits != self.tensor or dp_bits < 2:
             raise ValueError("mesh sizes")
-        high = [("dp", bit) for bit in range(dp_bits - 1, 1, -1)]
-        tensor_stages = [("tensor", bit) for bit in range(tensor_bits - 1, -1, -1)]
+        high = [("dp", tuple(range(dp_bits - 1, 1, -1)))]
+        tensor_stages = [("tensor", (bit,)) for bit in range(tensor_bits - 1, -1, -1)]
         self.orders = (
-            high + [("dp", 1)] + tensor_stages,
-            high + tensor_stages + [("dp", 1)],
+            high + [("dp", (1,))] + tensor_stages,
+            high + tensor_stages + [("dp", (1,))],
         )
         self.half_blocks = self.dp * self.tensor // 2
 
-    def swap(self, value, stage):
-        axis, bit = stage
+    def masks(self, stage):
+        bits = stage[1]
+        return [
+            sum(1 << bit for place, bit in enumerate(bits) if choice >> place & 1)
+            for choice in range(1, 1 << len(bits))
+        ]
+
+    def swap(self, value, axis, mask):
         size = self.dp if axis == "dp" else self.tensor
-        return lax.ppermute(value, axis, [(i, i ^ (1 << bit)) for i in range(size)])
+        return lax.ppermute(value, axis, [(i, i ^ mask) for i in range(size)])
+
+    def spread(self, held, stage):
+        return jnp.concatenate(
+            [held] + [self.swap(held, stage[0], mask) for mask in self.masks(stage)], axis=0
+        )
+
+    def add_up(self, held, stage):
+        size = held.shape[0] >> len(stage[1])
+        total = held[:size]
+        for place, mask in enumerate(self.masks(stage), 1):
+            total = total + self.swap(held[place * size : (place + 1) * size], stage[0], mask)
+        return total
 
     def tables(self):
         me_dp = lax.axis_index("dp")
@@ -55,26 +73,22 @@
         rows = []
         for order in self.orders:
             index = jnp.zeros_like(place)
-            for position, (axis, bit) in enumerate(order):
+            flat = [(axis, bit) for axis, bits in order for bit in bits]
+            for position, (axis, bit) in enumerate(flat):
                 index = index + (((relative[axis] >> bit) & 1) << position)
             rows.append(index)
         core = jnp.full_like(place, me_dp & 1)
         return jnp.stack(rows + [core]).astype(jnp.int32)
 
-    def gather(self, shard, tables, widths):
-        rows, width = shard.shape
-        half = rows // 2
-        pieces = []
-        for order, start in zip(self.orders, (0, half)):
-            held = shard[start : start + half][None]
-            for stage in order:
-                held = jnp.concatenate([held, self.swap(held, stage)], axis=0)
-            pieces += [held, self.swap(held, ("dp", 0))]
-        return self.assemble(pieces, tables, half, widths)
+    def gather(self, shard):
+        half = shard.shape[0] // 2
+        return Gather(self, [shard[:half][None], shard[half:][None]])
 
     def assemble(self, pieces, tables, half, widths):
         pairs = self.dp // 2
         total = sum(widths)
+        if 4 * half * self.half_blocks * total < 5 * 2**20:
+            return self.assemble_whole(pieces, tables, half, widths)
 
         def kernel(tables_ref, own_a, far_a, own_b, far_b, *outs):
             core = tables_ref[2, 0]
@@ -117,9 +131,79 @@
             compiler_params=pltpu.CompilerParams(vmem_limit_bytes=VMEM),
         )(tables, *pieces)
 
+    def assemble_whole(self, pieces, tables, half, widths):
+        pairs = self.dp // 2
+
+        def kernel(tables_ref, own_a, far_a, own_b, far_b, *outs):
+            core = tables_ref[2, 0]
+
+            @pl.loop(0, pairs)
+            def _(pair):
+                own = pl.multiple_of((2 * pair + core) * 2 * half, 2 * half)
+                far = pl.multiple_of((2 * pair + 1 - core) * 2 * half, 2 * half)
+                for tensor in range(self.tensor):
+                    at_a = tables_ref[0, tensor * pairs + pair]
+                    at_b = tables_ref[1, tensor * pairs + pair]
+                    at = 0
+                    for out, width in zip(outs, widths):
+                        source = slice(at, at + width)
+                        columns = slice(tensor * width, (tensor + 1) * width)
+                        out[pl.ds(own, half), columns] = own_a[at_a, :, source]
+                        out[pl.ds(own + half, half), columns] = own_b[at_b, :, source]
+                        out[pl.ds(far, half), columns] = far_a[at_a, :, source]
+                        out[pl.ds(far + half, half), columns] = far_b[at_b, :, source]
+                        at += width
+
+        return self.whole_call(
+            kernel,
+            tables,
+            pieces,
+            [(self.dp * 2 * half, self.tensor * width) for width in widths],
+        )
+
+    def split_whole(self, arrays, tables, half, widths):
+        pairs = self.dp // 2
+
+        def kernel(tables_ref, *refs):
+            sources, (own_a, far_a, own_b, far_b) = refs[: len(widths)], refs[len(widths) :]
+            core = tables_ref[2, 0]
+
+            @pl.loop(0, pairs)
+            def _(pair):
+                own = pl.multiple_of((2 * pair + core) * 2 * half, 2 * half)
+                far = pl.multiple_of((2 * pair + 1 - core) * 2 * half, 2 * half)
+                for tensor in range(self.tensor):
+                    at_a = tables_ref[0, tensor * pairs + pair]
+                    at_b = tables_ref[1, tensor * pairs + pair]
+                    at = 0
+                    for source, width in zip(sources, widths):
+                        target = slice(at, at + width)
+                        columns = slice(tensor * width, (tensor + 1) * width)
+                        own_a[at_a, :, target] = source[pl.ds(own, half), columns]
+                        own_b[at_b, :, target] = source[pl.ds(own + half, half), columns]
+                        far_a[at_a, :, target] = source[pl.ds(far, half), columns]
+                        far_b[at_b, :, target] = source[pl.ds(far + half, half), columns]
+                        at += width
+
+        return self.whole_call(
+            kernel, tables, arrays, [(self.half_blocks, half, sum(widths))] * 4
+        )
+
+    def whole_call(self, kernel, tables, values, shapes):
+        vmem = pl.BlockSpec(memory_space=pltpu.VMEM)
+        return pl.pallas_call(
+            kernel,
+            in_specs=[pl.BlockSpec(memory_space=pltpu.SMEM)] + [vmem] * len(values),
+            out_specs=[vmem] * len(shapes),
+            out_shape=[jax.ShapeDtypeStruct(shape, BF16) for shape in shapes],
+            compiler_params=pltpu.CompilerParams(vmem_limit_bytes=VMEM),
+        )(tables, *values)
+
     def split(self, arrays, tables, half, widths):
         pairs = self.dp // 2
         total = sum(widths)
+        if 4 * half * self.half_blocks * total < 5 * 2**20:
+            return self.split_whole(arrays, tables, half, widths)
 
         def kernel(tables_ref, *refs):
             sources, (own_a, far_a, own_b, far_b) = refs[: len(widths)], refs[len(widths) :]
@@ -164,50 +248,105 @@
     def scatter(self, arrays, tables):
         rows = arrays[0].shape[0] // self.dp
         widths = [array.shape[1] // self.tensor for array in arrays]
-        own_a, far_a, own_b, far_b = self.split(arrays, tables, rows // 2, widths)
-        halves = []
-        for order, own, far in zip(self.orders, (own_a, own_b), (far_a, far_b)):
-            held, sent = own, far
-            stages = [("dp", 0)] + order[::-1]
-            for number, stage in enumerate(stages):
-                held = held.astype(F32) + self.swap(sent, stage).astype(F32)
-                if number + 1 < len(stages):
-                    held = held.astype(BF16)
-                    middle = held.shape[0] // 2
-                    held, sent = held[:middle], held[middle:]
-            halves.append(held[0])
-        whole = jnp.concatenate(halves, axis=0)
+        return Scatter(self, self.split(arrays, tables, rows // 2, widths), widths)
+
+    def row_stages(self):
+        bits = tuple(range(self.dp.bit_length() - 1))
+        return [("dp", bits[2:]), ("dp", bits[:2])]
+
+    def gather_rows(self, row):
+        held = row[None]
+        stages = self.row_stages()
+        for stage in stages:
+            held = self.spread(held, stage)
+        relative = jnp.arange(self.dp) ^ lax.axis_index("dp")
+        index = jnp.zeros_like(relative)
+        for position, bit in enumerate(bit for stage in stages for bit in stage[1]):
+            index = index + (((relative >> bit) & 1) << position)
+        return held[index]
+
+    def scatter_rows(self, rows):
+        stages = self.row_stages()
+        place = jnp.arange(self.dp)
+        relative = jnp.zeros_like(place)
+        for position, bit in enumerate(bit for stage in stages for bit in stage[1]):
+            relative = relative + (((place >> position) & 1) << bit)
+        held = rows[relative ^ lax.axis_index("dp")]
+        for bit in range(self.tensor.bit_length() - 1):
+            held = held + self.swap(held, "tensor", 1 << bit)
+        for stage in stages[::-1]:
+            held = self.add_up(held, stage)
+        return held[0]
+
+
+class Gather:
+    def __init__(self, tree, held):
+        self.tree = tree
+        self.held = held
+        self.done = 0
+        self.stages = len(tree.orders[0])
+
+    def step(self):
+        if self.done < self.stages:
+            self.held = [
+                self.tree.spread(held, order[self.done])
+                for held, order in zip(self.held, self.tree.orders)
+            ]
+        elif self.done == self.stages:
+            self.held = self.held + [self.tree.swap(held, "dp", 1) for held in self.held]
+        self.done += 1
+
+    def finish(self, tables, widths):
+        while self.done <= self.stages:
+            self.step()
+        own_a, own_b, far_a, far_b = self.held
+        half = own_a.shape[1]
+        return self.tree.assemble([own_a, far_a, own_b, far_b], tables, half, widths)
+
+
+class Scatter:
+    def __init__(self, tree, pieces, widths):
+        own_a, far_a, own_b, far_b = pieces
+        self.tree = tree
+        self.widths = widths
+        self.held = [own_a, own_b]
+        self.sent = [[far_a], [far_b]]
+        self.orders = [[("dp", (0,))] + order[::-1] for order in tree.orders]
+        self.done = 0
+
+    def step(self):
+        if self.done == len(self.orders[0]):
+            return
+        last = self.done + 1 == len(self.orders[0])
+        for side, order in enumerate(self.orders):
+            stage = order[self.done]
+            held = self.held[side].astype(F32)
+            for value, mask in zip(self.sent[side], self.tree.masks(stage)):
+                held = held + self.tree.swap(value, stage[0], mask).astype(F32)
+            if not last:
+                held = held.astype(BF16)
+                count = 1 << len(order[self.done + 1][1])
+                size = held.shape[0] // count
+                held, *self.sent[side] = [
+                    held[place * size : (place + 1) * size] for place in range(count)
+                ]
+            self.held[side] = held
+        self.done += 1
+
+    def finish(self):
+        while self.done < len(self.orders[0]):
+            self.step()
+        whole = jnp.concatenate([held[0] for held in self.held], axis=0)
         parts, at = [], 0
-        for width in widths:
+        for width in self.widths:
             parts.append(whole[:, at : at + width])
             at += width
         return parts
 
-    def gather_rows(self, row):
-        held = row[None]
-        bits = range(self.dp.bit_length() - 2, -1, -1)
-        for bit in bits:
-            held = jnp.concatenate([self.swap(held, ("dp", bit)), held], axis=0)
-        index = self.row_index()
-        return held[index]
-
-    def row_index(self):
-        bits = self.dp.bit_length() - 1
-        relative = jnp.arange(self.dp) ^ lax.axis_index("dp")
-        index = jnp.zeros_like(relative)
-        for position, bit in enumerate(range(bits - 1, -1, -1)):
-            index = index + ((1 - ((relative >> bit) & 1)) << position)
-        return index
-
-    def scatter_rows(self, rows):
-        relative = rows[jnp.arange(self.dp) ^ lax.axis_index("dp")]
-        held = relative
-        for bit in range(self.tensor.bit_length() - 1):
-            held = held + self.swap(held, ("tensor", bit))
-        for bit in range(self.dp.bit_length() - 2, -1, -1):
-            middle = held.shape[0] // 2
-            held = held[:middle] + self.swap(held[middle:], ("dp", bit))
-        return held[0]
+
+def after(value, *chains):
+    waits = [(chain.held, getattr(chain, "sent", ())) for chain in chains]
+    return lax.optimization_barrier((value, waits))[0]
 
 
 def split_pair(block):
@@ -238,7 +377,8 @@
     return jnp.concatenate(parts, axis=1)
 
 
-def attend_forward_kernel(segment, valid, query_ref, pair_ref, mixed_ref, logsum_ref, value_ref):
+def attend_forward_kernel(segment, valid, ticket_ref, query_ref, pair_ref, *rest):
+    mixed_ref, logsum_ref, value_ref = rest[-3:]
     keys = pair_ref.at[:, PAIR : 2 * PAIR]
     value_ref[:, 0:PAIR] = pair_ref[:, 2 * PAIR : 3 * PAIR]
     value_ref[:, PAIR : 2 * PAIR] = jnp.ones((value_ref.shape[0], PAIR), BF16)
@@ -255,15 +395,15 @@
 
 
 def attend_backward_kernel(
-    segment, valid, joint, query_ref, pair_ref, mixed_ref, grad_ref, logsum_ref, *rest
+    segment, valid, joint, ticket_ref, query_ref, pair_ref, mixed_ref, grad_ref, logsum_ref, *rest
 ):
     if joint:
-        out_ref, key_sum, value_sum = rest
+        out_ref, key_sum, value_sum = rest[-3:]
         query_out = out_ref.at[:, 0:PAIR]
         key_out = out_ref.at[:, PAIR : 2 * PAIR]
         value_out = out_ref.at[:, 2 * PAIR : 3 * PAIR]
     else:
-        query_out, pair_out, key_sum, value_sum = rest
+        query_out, pair_out, key_sum, value_sum = rest[-4:]
         key_out = pair_out.at[:, 0:PAIR]
         value_out = pair_out.at[:, PAIR : 2 * PAIR]
     keys = pair_ref.at[:, PAIR : 2 * PAIR]
@@ -306,70 +446,90 @@
     )
 
 
-def attend_forward(triple, gathered, segment, valid):
-    images, rows, width = triple.shape
+def attend_forward(piece, ticket, triple, gathered, kept, segment, valid):
+    groups, part_pairs, all_pairs, part_at, all_at = piece
+    images, rows, _ = triple.shape
     key_rows = gathered.shape[1]
-    pairs = width // (3 * PAIR)
-    at = lambda i, g: (i, 0, g)
+    pairs = groups * all_pairs
+    narrow = lambda i, g, t: (i, 0, g * part_pairs + part_at)
+    wide = lambda i, g, t: (i, 0, g * all_pairs + all_at)
+    unread = pl.BlockSpec(memory_space=pl.ANY)
     return pl.pallas_call(
         functools.partial(attend_forward_kernel, segment, valid),
-        grid=(images, pairs),
-        in_specs=[
-            pl.BlockSpec((None, rows, 3 * PAIR), at),
-            pl.BlockSpec((None, key_rows, 3 * PAIR), at),
-        ],
-        out_specs=[
-            pl.BlockSpec((None, rows, PAIR), at),
-            pl.BlockSpec((None, rows, PAIR), at),
-        ],
+        grid_spec=pltpu.PrefetchScalarGridSpec(
+            num_scalar_prefetch=1,
+            grid=(images, groups),
+            in_specs=[
+                pl.BlockSpec((None, rows, 3 * PAIR), narrow),
+                pl.BlockSpec((None, key_rows, 3 * PAIR), narrow),
+            ]
+            + [unread] * len(kept),
+            out_specs=[
+                pl.BlockSpec((None, rows, PAIR), wide),
+                pl.BlockSpec((None, rows, PAIR), wide),
+            ],
+            scratch_shapes=[pltpu.VMEM((key_rows, 2 * PAIR), BF16)],
+        ),
         out_shape=[
             jax.ShapeDtypeStruct((images, rows, pairs * PAIR), BF16),
             jax.ShapeDtypeStruct((images, rows, pairs * PAIR), F32),
         ],
-        scratch_shapes=[pltpu.VMEM((key_rows, 2 * PAIR), BF16)],
-        cost_estimate=attend_cost(2, images, pairs, rows, key_rows),
+        input_output_aliases={3 + place: place for place in range(len(kept))},
+        cost_estimate=attend_cost(2, images, groups, rows, key_rows),
         compiler_params=pltpu.CompilerParams(vmem_limit_bytes=VMEM),
-    )(triple, gathered)
-
-
-def attend_backward(triple, gathered, mixed, mixed_grad, logsum, segment, valid):
+    )(ticket, triple, gathered, *kept)
+
+
+def attend_backward(piece, ticket, triple, gathered, mixed, mixed_grad, logsum, kept, segment, valid):
+    groups, part_pairs, all_pairs, part_at, all_at = piece
     images, rows, width = triple.shape
     key_rows = gathered.shape[1]
-    pairs = width // (3 * PAIR)
     joint = key_rows == rows
-    at = lambda i, g: (i, 0, g)
-    row_spec = pl.BlockSpec((None, rows, PAIR), at)
-    triple_spec = pl.BlockSpec((None, rows, 3 * PAIR), at)
+    narrow = lambda i, g, t: (i, 0, g * part_pairs + part_at)
+    wide = lambda i, g, t: (i, 0, g * all_pairs + all_at)
+    wide_spec = pl.BlockSpec((None, rows, PAIR), wide)
+    triple_spec = pl.BlockSpec((None, rows, 3 * PAIR), narrow)
+    pairs = groups * part_pairs
     if joint:
         out_specs = [triple_spec]
         out_shape = [jax.ShapeDtypeStruct(triple.shape, BF16)]
     else:
-        out_specs = [row_spec, pl.BlockSpec((None, key_rows, 2 * PAIR), at)]
+        out_specs = [
+            pl.BlockSpec((None, rows, PAIR), narrow),
+            pl.BlockSpec((None, key_rows, 2 * PAIR), narrow),
+        ]
         out_shape = [
             jax.ShapeDtypeStruct((images, rows, pairs * PAIR), BF16),
             jax.ShapeDtypeStruct((images, key_rows, pairs * 2 * PAIR), BF16),
         ]
-    outs = pl.pallas_call(
+    return pl.pallas_call(
         functools.partial(attend_backward_kernel, segment, valid, joint),
-        grid=(images, pairs),
-        in_specs=[
-            triple_spec,
-            pl.BlockSpec((None, key_rows, 3 * PAIR), at),
-            row_spec,
-            row_spec,
-            row_spec,
-        ],
-        out_specs=out_specs,
+        grid_spec=pltpu.PrefetchScalarGridSpec(
+            num_scalar_prefetch=1,
+            grid=(images, groups),
+            in_specs=[
+                triple_spec,
+                pl.BlockSpec((None, key_rows, 3 * PAIR), narrow),
+                wide_spec,
+                wide_spec,
+                wide_spec,
+            ]
+            + [pl.BlockSpec(memory_space=pl.ANY)] * len(kept),
+            out_specs=out_specs,
+            scratch_shapes=[pltpu.VMEM((PAIR, key_rows), F32)] * 2,
+        ),
         out_shape=out_shape,
-        scratch_shapes=[pltpu.VMEM((PAIR, key_rows), F32)] * 2,
-        cost_estimate=attend_cost(5, images, pairs, rows, key_rows),
+        input_output_aliases={6 + place: place for place in range(len(kept))},
+        cost_estimate=attend_cost(5, images, groups, rows, key_rows),
         compiler_params=pltpu.CompilerParams(vmem_limit_bytes=VMEM),
-    )(triple, gathered, mixed, mixed_grad, logsum)
-    if joint:
+    )(ticket, triple, gathered, mixed, mixed_grad, logsum, *kept)
+
+
+def join_grads(outs, pairs, shares, tensor):
+    if len(outs) == 1:
         return outs[0]
     query_grad, pair_grad = outs
-    shares = key_rows // rows
-    tensor = lax.axis_size("tensor")
+    images, rows, _ = query_grad.shape
     groups = [list(range(base, base + shares)) for base in range(0, tensor, shares)]
     pair_grad = lax.psum_scatter(
         pair_grad, "tensor", scatter_dimension=1, axis_index_groups=groups, tiled=True
@@ -380,7 +540,7 @@
             pair_grad.reshape(images, rows, pairs, 2 * PAIR),
         ],
         axis=3,
-    ).reshape(images, rows, width)
+    ).reshape(images, rows, pairs * 3 * PAIR)
 
 
 def norm_parts(values):
@@ -400,10 +560,113 @@
     )
 
 
+TAIL_RATE = 0.3275911 * 0.5**0.5
+TAIL = (0.5307027145, -0.7265760135, 0.7107068705, -0.142248368, 0.127414796)
+
+
 def gelu_parts(values):
-    below = 0.5 * lax.erfc(-values * (0.5**0.5))
-    density = jnp.exp(-0.5 * values * values) * 0.3989422804014327
-    return values * below, below + values * density
+    point = 1.0 / (1.0 + TAIL_RATE * jnp.abs(values))
+    total = TAIL[0] * point
+    for factor in TAIL[1:]:
+        total = (total + factor) * point
+    bell = jnp.exp2((-0.5 * 1.4426950408889634) * (values * values))
+    tail = total * bell
+    below = jnp.where(values < 0.0, tail, 1.0 - tail)
+    return values * below, below + (values * 0.3989422804014327) * bell
+
+
+def feed_kernel(tile, *refs):
+    (normed_ref, back_ref, expand_ref, reduce_ref, bias_ref) = refs[:5]
+    (out_ref, grad_ref, expand_out, reduce_out, bias_out) = refs[5:10]
+    (out_sum, grad_sum, active_ref, gate_ref, stage_ref) = refs[10:]
+    rows = normed_ref.shape[0]
+    expand = expand_ref[...]
+    reduce = reduce_ref[...]
+    bias = bias_ref[0:1, :]
+
+    def tiles(first):
+        total = None
+        for base in range(0, rows, tile):
+            here = pl.ds(base, tile)
+            active, slope = gelu_parts(dot(normed_ref[here, :], expand, 1, 0) + bias)
+            active = active.astype(BF16)
+            gate = dot(back_ref[here, :], reduce, 1, 0) * slope
+            part = jnp.sum(gate.reshape(tile // 8, 8, gate.shape[1]), axis=0)
+            total = part if total is None else total + part
+            gate = gate.astype(BF16)
+            active_ref[here, :] = active
+            gate_ref[here, :] = gate
+            out = dot(active, reduce, 1, 1)
+            grad = dot(gate, expand, 1, 1)
+            if first:
+                out_sum[here, :] = out
+                grad_sum[here, :] = grad
+            else:
+                out_sum[here, :] += out
+                grad_sum[here, :] += grad
+        bias_out[...] = total
+
+    @pl.when(pl.program_id(0) == 0)
+    def _():
+        tiles(True)
+
+    @pl.when(pl.program_id(0) != 0)
+    def _():
+        tiles(False)
+
+    reduce_out[...] = dot(active_ref[...], back_ref[...], 0, 0).T.astype(BF16)
+    expand_out[...] = dot(gate_ref[...], normed_ref[...], 0, 0).T.astype(BF16)
+
+    @pl.when(pl.program_id(0) == pl.num_programs(0) - 1)
+    def _():
+        stage_rows = stage_ref.shape[0]
+
+        @pl.loop(0, rows // stage_rows)
+        def _(i):
+            here = pl.ds(pl.multiple_of(i * stage_rows, stage_rows), stage_rows)
+            stage_ref[...] = out_sum[here, :].astype(BF16)
+            pltpu.sync_copy(stage_ref, out_ref.at[here, :])
+            stage_ref[...] = grad_sum[here, :].astype(BF16)
+            pltpu.sync_copy(stage_ref, grad_ref.at[here, :])
+
+
+def feed_forward(normed, back, expand, reduce, bias):
+    rows, width = normed.shape
+    hidden = expand.shape[1]
+    block = 256
+    tile = rows // 4
+    whole = pl.BlockSpec(memory_space=pltpu.VMEM)
+    left = pl.BlockSpec(memory_space=pl.ANY)
+    columns = pl.BlockSpec((width, block), lambda f: (0, f))
+    vector = pl.BlockSpec((8, block), lambda f: (0, f))
+    bias = jnp.broadcast_to(bias[None], (8, hidden))
+    out, grad, expand_grad, reduce_grad, bias_grad = pl.pallas_call(
+        functools.partial(feed_kernel, tile),
+        grid=(hidden // block,),
+        in_specs=[whole, whole, columns, columns, vector],
+        out_specs=[left, left, columns, columns, vector],
+        out_shape=[
+            jax.ShapeDtypeStruct((rows, width), BF16),
+            jax.ShapeDtypeStruct((rows, width), BF16),
+            jax.ShapeDtypeStruct((width, hidden), BF16),
+            jax.ShapeDtypeStruct((width, hidden), BF16),
+            jax.ShapeDtypeStruct((8, hidden), F32),
+        ],
+        scratch_shapes=[
+            pltpu.VMEM((rows, width), F32),
+            pltpu.VMEM((rows, width), F32),
+            pltpu.VMEM((rows, block), BF16),
+            pltpu.VMEM((rows, block), BF16),
+            pltpu.VMEM((128, width), BF16),
+        ],
+        cost_estimate=pl.CostEstimate(
+            flops=12 * rows * width * hidden,
+            bytes_accessed=8 * rows * width + 8 * width * hidden,
+            transcendentals=rows * hidden,
+        ),
+        compiler_params=pltpu.CompilerParams(vmem_limit_bytes=60 * 2**20),
+    )(normed, back, expand, reduce, bias)
+    return out, grad, expand_grad, reduce_grad, jnp.sum(bias_grad, axis=0)
 
 
 def body(
@@ -456,17 +719,11 @@
         forward_shift,
         reduce_bias,
         forward_scale,
-        expand_bias,
     ]
-    sizes = [vector.shape[0] for vector in vectors]
-    packed = jnp.concatenate(vectors)
-    extent = -(-packed.shape[0] // 1024) * 1024
-    packed = jnp.pad(packed, (0, extent - packed.shape[0])).astype(F32)
-    gathered = tree.gather_rows(packed.reshape(-1, 128)).reshape(tree.dp, extent)
-    full, at = [], 0
-    for size in sizes:
-        full.append(gathered[:, at : at + size].reshape(-1))
-        at += size
+    short = attention_gain.shape[0]
+    packed = jnp.concatenate([jnp.stack(vectors), expand_bias.reshape(-1, short)], axis=0)
+    spare = ((0, -packed.shape[0] % 8), (0, -short % 128))
+    gathered = tree.gather_rows(jnp.pad(packed.astype(F32), spare))
     (
         gain_one,
         shift_one,
@@ -478,20 +735,28 @@
         shift_two,
         reduce_shift,
         scale_two,
-        expand_shift,
-    ) = full
+    ) = [gathered[:, place, :short].reshape(-1) for place in range(len(vectors))]
+    expand_shift = gathered[:, len(vectors) : packed.shape[0], :short].reshape(-1)
 
     shard_rows, _, local = triple_weight.shape
     local_pairs = local // PAIR
+    parts = 2 if local_pairs % 2 == 0 else 1
+    part_pairs = local_pairs // parts
+    part_width = part_pairs * 3 * PAIR
     triple_shard = (
         triple_weight.reshape(shard_rows, 3, local_pairs, PAIR)
         .transpose(0, 2, 1, 3)
         .reshape(shard_rows, 3 * local)
     )
-    (triple_full,) = tree.gather(triple_shard, tables, [3 * local])
-    widths = [merge_weight.shape[1], expand_weight.shape[1], reduce_weight.shape[1]]
-    merge_full, expand_full, reduce_full = tree.gather(
-        jnp.concatenate([merge_weight, expand_weight, reduce_weight], axis=1), tables, widths
+    first = tree.gather(jnp.concatenate([triple_shard, merge_weight], axis=1))
+    for _ in range(first.stages + 1):
+        first.step()
+    feed_chain = tree.gather(
+        after(jnp.concatenate([expand_weight, reduce_weight], axis=1), first)
+    )
+    feed_chain.step()
+    *triple_full, merge_full = first.finish(
+        tables, [part_width] * parts + [merge_weight.shape[1]]
     )
 
     inputs = pad(tokens).astype(F32)
@@ -500,82 +765,133 @@
     pairs = tree.tensor * local_pairs
     bias = jnp.stack(
         [
-            query_shift.reshape(pairs, PAIR),
-            jnp.zeros((pairs, PAIR), F32),
-            value_shift.reshape(pairs, PAIR),
+            query_shift.reshape(tree.tensor, parts, part_pairs, PAIR),
+            jnp.zeros((tree.tensor, parts, part_pairs, PAIR), F32),
+            value_shift.reshape(tree.tensor, parts, part_pairs, PAIR),
         ],
-        axis=1,
-    ).reshape(-1)
-    triple = (dot(normed_one, triple_full, 1, 0) + bias).astype(BF16)
-    triple = triple.reshape(images, padded, -1)
-    pair_rows = triple
-    if shares > 1:
-        groups = [list(range(base, base + shares)) for base in range(0, tree.tensor, shares)]
-        pair_rows = lax.all_gather(
-            triple, "tensor", axis=1, axis_index_groups=groups, tiled=True
+        axis=3,
+    )
+    triples, pair_rows = [], []
+    for part in range(parts):
+        triple = dot(normed_one, triple_full[part], 1, 0) + bias[:, part].reshape(-1)
+        triple = triple.astype(BF16).reshape(images, padded, -1)
+        triples.append(triple)
+        if shares > 1:
+            groups = [list(range(base, base + shares)) for base in range(0, tree.tensor, shares)]
+            triple = lax.all_gather(
+                triple, "tensor", axis=1, axis_index_groups=groups, tiled=True
+            )
+        pair_rows.append(triple)
+
+    places = [(part, at) for part in range(parts) for at in range(part_pairs)]
+    ticket = jnp.zeros((1,), jnp.int32)
+    kept = ()
+    for number, (part, at) in enumerate(places):
+        piece = (tree.tensor, part_pairs, local_pairs, at, part * part_pairs + at)
+        passed = ticket
+        if number in (1, 2):
+            passed = after(ticket, feed_chain)
+            feed_chain.step()
+        kept = attend_forward(
+            piece, passed, triples[part], pair_rows[part], kept, padded, segment_rows
         )
-    mixed, logsum = attend_forward(triple, pair_rows, padded, segment_rows)
+    mixed, logsum = kept
     mixed_rows = mixed.reshape(rows, width)
-    branch_one = dot(mixed_rows, merge_full, 1, 1) + merge_shift
+    branch_one = dot(mixed_rows, merge_full, 1, 1) + after(merge_shift, feed_chain)
     middle = inputs + scale_one * branch_one
     normal_two, inverse_two = norm_parts(middle)
     normed_two = (normal_two * gain_two + shift_two).astype(BF16)
+    expand_full, reduce_full = feed_chain.finish(
+        tables, [expand_weight.shape[1], reduce_weight.shape[1]]
+    )
 
     upstream = pad(cotangent).astype(F32)
     back_two = (upstream * scale_two).astype(BF16)
-    gate_input = dot(normed_two, expand_full, 1, 0) + expand_shift
-    activated, slope = gelu_parts(gate_input)
-    activated = activated.astype(BF16)
-    slope = slope.astype(BF16)
-    gate_grad = (dot(back_two, reduce_full, 1, 0) * slope.astype(F32)).astype(BF16)
-    branch_two = dot(activated, reduce_full, 1, 1) + reduce_shift
+    feed_out, normed_two_grad, expand_grad, reduce_grad, expand_bias_grad = feed_forward(
+        normed_two, back_two, expand_full, reduce_full, expand_shift
+    )
+    feed_chain = tree.scatter([expand_grad, reduce_grad], tables)
+    normed_two_grad = normed_two_grad.astype(F32)
+    branch_two = feed_out.astype(F32) + reduce_shift
     result = unpad((middle + scale_two * branch_two).astype(BF16))
-    reduce_grad = dot(back_two, activated, 0, 0).astype(BF16)
-    expand_grad = dot(normed_two, gate_grad, 0, 0).astype(BF16)
-    expand_out, reduce_out = tree.scatter([expand_grad, reduce_grad], tables)
-    normed_two_grad = dot(gate_grad, expand_full, 1, 1)
-
     middle_grad = upstream + norm_backward(normed_two_grad, gain_two, normal_two, inverse_two)
     back_one = (middle_grad * scale_one).astype(BF16)
+    feed_chain.step()
     mixed_grad = dot(back_one, merge_full, 1, 0).astype(BF16).reshape(images, padded, width)
     merge_grad = dot(back_one, mixed_rows, 0, 0).astype(BF16)
-    (merge_out,) = tree.scatter([merge_grad], tables)
-    triple_grad = attend_backward(
-        triple, pair_rows, mixed, mixed_grad, logsum, padded, segment_rows
-    )
-    triple_grad = triple_grad.reshape(rows, -1)
-    weight_grad = dot(normed_one, triple_grad, 0, 0).astype(BF16)
-    (triple_out,) = tree.scatter([weight_grad], tables)
-    triple_out = (
-        triple_out.reshape(shard_rows, local_pairs, 3, PAIR)
-        .transpose(0, 2, 1, 3)
-        .reshape(shard_rows, 3, local)
-    )
-    normed_one_grad = dot(triple_grad, triple_full, 1, 1)
-    tokens_grad = middle_grad + norm_backward(normed_one_grad, gain_one, normal_one, inverse_one)
+    chains, part_grads, kept = [feed_chain], [], ()
+    for number, (part, at) in enumerate(places):
+        piece = (tree.tensor, part_pairs, local_pairs, at, part * part_pairs + at)
+        kept = attend_backward(
+            piece,
+            after(ticket, *chains),
+            triples[part],
+            pair_rows[part],
+            mixed,
+            mixed_grad,
+            logsum,
+            kept,
+            padded,
+            segment_rows,
+        )
+        for chain in chains:
+            chain.step()
+        if at == part_pairs - 1:
+            grad = join_grads(kept, tree.tensor * part_pairs, shares, tree.tensor)
+            grad = grad.reshape(rows, -1)
+            part_grads.append(grad)
+            kept = ()
+            sent = [dot(normed_one, grad, 0, 0).astype(BF16)]
+            if part == 0:
+                sent.append(merge_grad)
+            chains.append(tree.scatter(sent, tables))
+            if part + 1 < parts:
+                chains[-1].step()
+    normed_one_grad = None
+    for grad, full_part in zip(part_grads, triple_full):
+        term = dot(grad, after(full_part, *chains[1:]), 1, 1)
+        normed_one_grad = term if normed_one_grad is None else normed_one_grad + term
+        for chain in chains:
+            chain.step()
+    late_gain = after(gain_one, *chains[1:])
+    tokens_grad = middle_grad + norm_backward(normed_one_grad, late_gain, normal_one, inverse_one)
     tokens_grad = unpad(tokens_grad.astype(BF16))
-
-    bias_sums = jnp.sum(triple_grad, axis=0, dtype=F32).reshape(pairs, 3, PAIR)
+    expand_out, reduce_out = chains[0].finish()
+    first_out, merge_out = chains[1].finish()
+    triple_parts = [first_out] + [chain.finish()[0] for chain in chains[2:]]
+    triple_out = jnp.concatenate(
+        [part.reshape(shard_rows, part_pairs, 3, PAIR) for part in triple_parts], axis=1
+    )
+    triple_out = triple_out.transpose(0, 2, 1, 3).reshape(shard_rows, 3, local)
+
+    bias_sums = jnp.stack(
+        [
+            jnp.sum(grad, axis=0, dtype=F32).reshape(tree.tensor, part_pairs, 3, PAIR)
+            for grad in part_grads
+        ],
+        axis=1,
+    )
     sums = [
         jnp.sum(normed_one_grad * normal_one, axis=0),
         jnp.sum(normed_one_grad, axis=0),
-        bias_sums[:, 0].reshape(-1),
-        bias_sums[:, 2].reshape(-1),
+        bias_sums[:, :, :, 0].reshape(-1),
+        bias_sums[:, :, :, 2].reshape(-1),
         jnp.sum(middle_grad, axis=0) * scale_one,
         jnp.sum(middle_grad * branch_one, axis=0),
         jnp.sum(normed_two_grad * normal_two, axis=0),
         jnp.sum(normed_two_grad, axis=0),
         jnp.sum(upstream, axis=0) * scale_two,
         jnp.sum(upstream * branch_two, axis=0),
-        jnp.sum(gate_grad, axis=0, dtype=F32),
+        expand_bias_grad,
     ]
-    columns = jnp.concatenate([total.reshape(tree.dp, -1) for total in sums], axis=1)
-    columns = jnp.pad(columns, ((0, 0), (0, extent - columns.shape[1])))
-    mine = tree.scatter_rows(columns.reshape(tree.dp, -1, 128)).reshape(-1)
-    vector_out, at = [], 0
-    for size in sizes:
-        vector_out.append(mine[at : at + size])
-        at += size
+    columns = jnp.concatenate(
+        [total.reshape(tree.dp, -1, short) for total in sums[:-1]]
+        + [sums[-1].reshape(tree.dp, -1, short)],
+        axis=1,
+    )
+    mine = tree.scatter_rows(jnp.pad(columns, ((0, 0),) + spare))
+    vector_out = [mine[place, :short] for place in range(len(vectors))]
+    vector_out.append(mine[len(vectors) : packed.shape[0], :short].reshape(-1))
     return (
         result,
         tokens_grad,

time: 1180 us -> 1050 us (0.89)
  matrix products: 445 us -> 133 us
  Pallas kernels: 325 us -> 553 us
  waiting for transfers between devices: 174 us -> 87.8 us
  other arithmetic: 73.1 us -> 96.9 us
  starting transfers between devices: 67.7 us -> 86.4 us
    dot_general x12 -> x9, matrix products: 445 us -> 133 us  [dot(): return lax.dot_general(left, right, dims, preferred_element_type=F32)]
    pallas_call x0 -> x4, Pallas kernels: none -> 243 us  [the longest x1 227 us: feed_forward(): pl.pallas_call(functools.partial(feed_kernel, tile), grid=(hidden // bloc...]
    ppermute x59 -> x73, waiting for transfers between devices: 174 us -> 87.8 us  [swap(): return lax.ppermute(value, axis, [(i, i ^ mask) for i in range(size)])]
    reduce_sum x1 -> x5, other arithmetic: 7.1 us -> 30.2 us  [the longest x1 14.4 us: body(): jnp.sum(middle_grad * branch_one, axis=0)]
    pallas_call x3 -> x1, Pallas kernels: 40.2 us -> 18.5 us  [split(): pl.pallas_call(kernel, grid_spec=pltpu.PrefetchScalarGridSpec(num_scalar_...]
    ppermute x59 -> x73, starting transfers between devices: 67.7 us -> 86.4 us  [swap(): return lax.ppermute(value, axis, [(i, i ^ mask) for i in range(size)])]
    pallas_call x2 -> x1, Pallas kernels: 31.3 us -> 17.9 us  [assemble(): pl.pallas_call(kernel, grid_spec=pltpu.PrefetchScalarGridSpec(num_scalar_...]
    pallas_call x1 -> x4, Pallas kernels: 152 us -> 163 us  [attend_backward(): pl.pallas_call(functools.partial(attend_backward_kernel, segment, valid,...]
  transfers between devices with their start and end apart: 59 -> 73, of which waited for: 32 -> 21; matrix products, arithmetic and copies ran while one was open for 16% -> 28% of each run, Pallas kernels for 13% -> 28%
where the time goes in v2:
time: 1050 us; the launch traced here: 1040 us
  Pallas kernels  553 us (53%)
  matrix products  133 us (13%)
  other arithmetic  96.9 us (9%)
  waiting for transfers between devices  87.8 us (8%)
  starting transfers between devices  86.4 us (8%)
  local copies, waits for them, and re-layouts  81.8 us (8%)
    pallas_call x1, Pallas kernels, feed_forward(): pl.pallas_call(functools.partial(feed_kernel, tile), grid=(hidden // bloc...  227 us
    pallas_call x4, Pallas kernels, attend_backward(): pl.pallas_call(functools.partial(attend_backward_kernel, segment, valid,...  163 us
    dot_general x9, matrix products, dot(): return lax.dot_general(left, right, dims, preferred_element_type=F32)  133 us
    pallas_call x4, Pallas kernels, attend_forward(): pl.pallas_call(functools.partial(attend_forward_kernel, segment, valid),...  111 us
    ppermute x73, waiting for transfers between devices, swap(): return lax.ppermute(value, axis, [(i, i ^ mask) for i in range(size)])  87.8 us
    ppermute x73, starting transfers between devices, swap(): return lax.ppermute(value, axis, [(i, i ^ mask) for i in range(size)])  86.4 us
    convert_element_type x18, other arithmetic, step(): held = held.astype(BF16)  23.7 us
  transfers between devices with their start and end apart: 73, of which 21 were waited for; matrix products, arithmetic and copies ran while one was open for 28% of the time, Pallas kernels for 28%

profile of v2, /device:TPU:0, one launch (start us, length us, event | category | flops | bytes accessed | tf_op | source)
XLA Modules:
  0.0 1041.4 jit_solution(11329589728754500316)
XLA Ops:
  16.0 6.1 reshape.485
  28.1 6.2 reshape.492
  48.4 7.1 collective-permute-done.12
  62.9 7.0 collective-permute-done.9
  77.4 19.5 %collective-permute-done.10 = bf16[8,32,2048]{2,1,0:T(8,128)(2,1)S(1)} collective-permute-done((bf16[8,32,2048]{2,1,0:T(8,128)(2,1)}, bf16[8,32,2048]{2,1,0:T(8,128)(2,1)S(1)}, u32[]{:S(2)}, u32[]{:S(2)}) %collective-permute-start.10) | collective-permute-done | bytes 1048608 | tf_op jit(solution)/shard_map/ppermute | solution.py:50
  102.8 6.9 fusion.8.refs_1_
  109.8 4.9 fusion.22
  115.6 3.6 collective-permute-start.20
  119.2 7.3 shard_map.296
  126.5 13.2 %add_convert_fusion.1 = bf16[2816,1536]{1,0:T(8,128)(2,1)} fusion(bf16[2816,1024]{1,0:T(8,128)(2,1)S(1)} %copy-done.8, bf16[1024,1536]{1,0:T(8,128)(2,1)} %get-tuple-element.96, f32[1536]{0:T(1024)S(1)} %add.412), kind=kOutput, calls=%fused_computation.5 | convolution fusion | flops 8867020800 | bytes 17569792 | tf_op jit(solution)/shard_map/dot_general | solution.py:22
  139.6 11.3 %add_convert_fusion = bf16[2816,1536]{1,0:T(8,128)(2,1)} fusion(bf16[2816,1024]{1,0:T(8,128)(2,1)S(1)} %copy-done.8, bf16[1024,1536]{1,0:T(8,128)(2,1)S(1)} %copy-done.54, f32[1536]{0:T(1024)S(1)} %add.415), kind=kOutput, calls=%fused_computation.4 | convolution fusion | flops 8867020800 | bytes 17569792 | tf_op jit(solution)/shard_map/dot_general | solution.py:22
  150.9 27.8 %shard_map.297 = (bf16[2,1408,1024]{2,1,0:T(8,128)(2,1)}, f32[2,1408,1024]{2,1,0:T(8,128)}) custom-call(s32[1]{0:T(128)} %constant.65.clone.1.ticket_ref, bf16[2,1408,1536]{2,1,0:T(8,128)(2,1)} %bitcast.192, bf16[2,1408,1536]{2,1,0:T(8,128)(2,1)} %bitcast.193), custom_call_target="tpu_custom_call" | custom-call | flops 16240345088 | bytes 11534336 | tf_op jit(solution)/shard_map/pallas_call | solution.py:457
  180.5 3.6 collective-permute-start.24
  185.2 8.8 collective-permute-done.22
  194.1 4.7 collective-permute-done.23
  199.5 27.6 %shard_map.298 = (bf16[2,1408,1024]{2,1,0:T(8,128)(2,1)}, f32[2,1408,1024]{2,1,0:T(8,128)}) custom-call(s32[1]{0:T(128)} %constant.65.clone.1.ticket_ref, bf16[2,1408,1536]{2,1,0:T(8,128)(2,1)} %bitcast.194, bf16[2,1408,1536]{2,1,0:T(8,128)(2,1)} %bitcast.195, ...), custom_call_target="tpu_custom_call", output_to_operand_aliasing={{0}: (3, {}), {1}: (4, {})} | custom-call | flops 16240345088 | bytes 11534336 | tf_op jit(solution)/shard_map/pallas_call | solution.py:457
  237.7 27.6 %shard_map.299 = (bf16[2,1408,1024]{2,1,0:T(8,128)(2,1)}, f32[2,1408,1024]{2,1,0:T(8,128)}) custom-call(s32[1]{0:T(128)} %constant.65.clone.1.ticket_ref, bf16[2,1408,1536]{2,1,0:T(8,128)(2,1)} %bitcast.184, bf16[2,1408,1536]{2,1,0:T(8,128)(2,1)} %bitcast.185, ...), custom_call_target="tpu_custom_call", output_to_operand_aliasing={{0}: (3, {}), {1}: (4, {})} | custom-call | flops 16240345088 | bytes 11534336 | tf_op jit(solution)/shard_map/pallas_call | solution.py:457
  265.3 28.0 %shard_map.300 = (bf16[2,1408,1024]{2,1,0:T(8,128)(2,1)}, f32[2,1408,1024]{2,1,0:T(8,128)}) custom-call(s32[1]{0:T(128)} %constant.65.clone.1.ticket_ref, bf16[2,1408,1536]{2,1,0:T(8,128)(2,1)} %bitcast.186, bf16[2,1408,1536]{2,1,0:T(8,128)(2,1)} %bitcast.187, ...), custom_call_target="tpu_custom_call", output_to_operand_aliasing={{0}: (3, {}), {1}: (4, {})} | custom-call | flops 16240345088 | bytes 11534336 | tf_op jit(solution)/shard_map/pallas_call | solution.py:457
  297.0 18.8 %fusion.64 = (f32[2816]{0:T(1024)S(1)}, f32[2816,1024]{1,0:T(8,128)S(1)}, f32[2816,1024]{1,0:T(8,128)}) fusion(f32[1024]{0:T(1024)S(1)} %reshape_squeeze.2, f32[1024]{0:T(1024)S(1)} %mul.155, bf16[2,1370,1024]{2,1,0:T(8,128)(2,1)} %reshape.485, bf16[2816,1024]{1,0:T(8,128)(2,1)} %bitcast.204, bf16[1024,1024]{1,0:T(8,128)(2,1)S(1)} %copy-done.55), kind=kOutput, calls=%fused_computation.239 | convolution fusion | flops 5919994880 | bytes 36563968 | tf_op jit(solution)/shard_map/dot_general | solution.py:22
  319.9 4.0 add_convert_fusion.3.refs_0_
  324.0 17.9 %shard_map.301 = (bf16[1024,4096]{1,0:T(8,128)(2,1)}, bf16[1024,4096]{1,0:T(8,128)(2,1)}) custom-call(s32[3,16]{1,0:T(4,128)} %add_add_fusion.tables_ref, bf16[16,32,4096]{2,1,0:T(8,128)(2,1)} %constant_dynamic-update-slice_fusion.41.own_a, bf16[16,32,4096]{2,1,0:T(8,128)(2,1)} %collective-permute-done.28.far_a, ...), custom_call_target="tpu_custom_call" | custom-call | tf_op jit(solution)/shard_map/pallas_call | solution.py:116
  342.6 226.6 %shard_map.302 = (bf16[2816,1024]{1,0:T(8,128)(2,1)}, bf16[2816,1024]{1,0:T(8,128)(2,1)}, bf16[1024,4096]{1,0:T(8,128)(2,1)}, bf16[1024,4096]{1,0:T(8,128)(2,1)}, f32[8,4096]{1,0:T(8,128)}) custom-call(bf16[2816,1024]{1,0:T(8,128)(2,1)} %add_convert_fusion.3.refs_0_, bf16[2816,1024]{1,0:T(8,128)(2,1)} %fusion.8.refs_1_, ...), custom_call_target="tpu_custom_call" | custom-call | flops 141733920768 | bytes 56623104 | tf_op jit(solution)/shard_map/pallas_call | solution.py:643
  569.2 9.8 fusion.7
  579.1 18.5 %shard_map.303 = (bf16[16,32,4096]{2,1,0:T(8,128)(2,1)}, bf16[16,32,4096]{2,1,0:T(8,128)(2,1)}, bf16[16,32,4096]{2,1,0:T(8,128)(2,1)}, bf16[16,32,4096]{2,1,0:T(8,128)(2,1)}) custom-call(s32[3,16]{1,0:T(4,128)} %add_add_fusion.tables_ref, bf16[1024,4096]{1,0:T(8,128)(2,1)} %get-tuple-element.76.refs_0_, bf16[1024,4096]{1,0:T(8,128)(2,1)} %get-tuple-element.77.refs_1_), custom_call_target="tpu_custom_call" | custom-call | tf_op jit(solution)/shard_map/pallas_call | solution.py:233
  598.1 14.4 %multiply_reduce_fusion = (f32[1024]{0:T(1024)S(1)}, f32[1024]{0:T(1024)S(1)}, f32[2816,1024]{1,0:T(8,128)S(1)}, bf16[2816,1024]{1,0:T(8,128)(2,1)S(1)}, f32[1024]{0:T(1024)S(1)}) fusion(f32[2816,1024]{1,0:T(8,128)} %get-tuple-element.210, f32[1024]{0:T(1024)S(1)} %copy-done.49, f32[2816]{0:T(1024)S(1)} %broadcast_multiply_fusion.2, ...), kind=kLoop, calls=%fused_computation.45 | loop fusion | flops 60552192 | bytes 57589760 | tf_op jit(solution)/shard_map/reduce_sum | solution.py:880
  612.5 11.4 %fusion.32.refs_1_ = bf16[1024,1024]{1,0:T(8,128)(2,1)} fusion(bf16[2816,1024]{1,0:T(8,128)(2,1)} %bitcast.205, f32[2816,1024]{1,0:T(8,128)S(1)} %get-tuple-element.119, f32[1024]{0:T(1024)S(1)} %copy-done.53), kind=kOutput, calls=%fused_computation.66 | convolution fusion | flops 5912395776 | bytes 19402752 | tf_op jit(solution)/shard_map/dot_general | solution.py:22
  627.0 6.3 reshape.494
  638.3 12.5 %convolution_convert_fusion = bf16[2816,1024]{1,0:T(8,128)(2,1)} fusion(bf16[1024,1024]{1,0:T(8,128)(2,1)S(1)} %copy-done.56, f32[2816,1024]{1,0:T(8,128)} %copy-done.3, f32[1024]{0:T(1024)S(1)} %copy-done.53), kind=kOutput, calls=%fused_computation.58 | convolution fusion | flops 5914230784 | bytes 19402752 | tf_op jit(solution)/shard_map/dot_general | solution.py:22
  650.8 3.9 add_convert_fusion.5
  656.8 3.7 add_convert_fusion.4
  665.0 40.7 %shard_map.304.rest_0_ = bf16[2,1408,1536]{2,1,0:T(8,128)(2,1)} custom-call(s32[1]{0:T(128)} %constant.65.clone.1.ticket_ref, bf16[2,1408,1536]{2,1,0:T(8,128)(2,1)} %bitcast.196, bf16[2,1408,1536]{2,1,0:T(8,128)(2,1)} %bitcast.197, bf16[2,1408,1024]{2,1,0:T(8,128)(2,1)} %get-tuple-element.69.mixed_ref, bf16[2,1408,1024]{2,1,0:T(8,128)(2,1)} %bitcast.200, ...), custom_call_target="tpu_custom_call" | custom-call | flops 40600862720 | bytes 11534336 | tf_op jit(solution)/shard_map/pallas_call | solution.py:505
  707.5 4.1 collective-permute-done.33
  717.8 40.6 %shard_map.305 = bf16[2,1408,1536]{2,1,0:T(8,128)(2,1)} custom-call(s32[1]{0:T(128)} %constant.65.clone.1.ticket_ref, bf16[2,1408,1536]{2,1,0:T(8,128)(2,1)} %bitcast.198, bf16[2,1408,1536]{2,1,0:T(8,128)(2,1)} %bitcast.199, bf16[2,1408,1024]{2,1,0:T(8,128)(2,1)} %get-tuple-element.69.mixed_ref, ...), custom_call_target="tpu_custom_call", output_to_operand_aliasing={{}: (6, {})} | custom-call | flops 40600862720 | bytes 11534336 | tf_op jit(solution)/shard_map/pallas_call | solution.py:505
  758.5 14.9 %bitcast_convert_fusion.1.refs_0_ = bf16[1024,1536]{1,0:T(8,128)(2,1)} fusion(bf16[2,1408,1536]{2,1,0:T(8,128)(2,1)} %shard_map.305, f32[1024]{0:T(1024)S(1)} %copy-done.47, f32[1024]{0:T(1024)S(1)} %copy-done.36, f32[2,1408]{1,0:T(2,128)S(1)} %copy-done.34, f32[2,1408]{1,0:T(2,128)S(1)} %copy-done.29, bf16[2,1370,1024]{2,1,0:T(8,128)(2,1)S(1)} %bitcast.158), kind=kOutput, calls=%fused_computation.56 | convolution fusion | flops 8877244416 | bytes 17438720 | tf_op jit(solution)/shard_map/dot_general | solution.py:22
  773.3 5.3 shard_map.306
  779.1 4.7 convert_reduce_fusion.1
  788.9 4.3 collective-permute-start.42
  801.8 40.6 %shard_map.307.rest_0_ = bf16[2,1408,1536]{2,1,0:T(8,128)(2,1)} custom-call(s32[1]{0:T(128)} %constant.65.clone.1.ticket_ref, bf16[2,1408,1536]{2,1,0:T(8,128)(2,1)} %bitcast.188, bf16[2,1408,1536]{2,1,0:T(8,128)(2,1)} %bitcast.189, bf16[2,1408,1024]{2,1,0:T(8,128)(2,1)} %get-tuple-element.69.mixed_ref, bf16[2,1408,1024]{2,1,0:T(8,128)(2,1)} %bitcast.202, ...), custom_call_target="tpu_custom_call" | custom-call | flops 40600862720 | bytes 11534336 | tf_op jit(solution)/shard_map/pallas_call | solution.py:505
  846.7 9.0 collective-permute-done.45
  862.0 40.9 %shard_map.308 = bf16[2,1408,1536]{2,1,0:T(8,128)(2,1)} custom-call(s32[1]{0:T(128)} %constant.65.clone.1.ticket_ref, bf16[2,1408,1536]{2,1,0:T(8,128)(2,1)} %bitcast.190, bf16[2,1408,1536]{2,1,0:T(8,128)(2,1)} %bitcast.191, bf16[2,1408,1024]{2,1,0:T(8,128)(2,1)} %get-tuple-element.69.mixed_ref, ...), custom_call_target="tpu_custom_call", output_to_operand_aliasing={{}: (6, {})} | custom-call | flops 40600862720 | bytes 11534336 | tf_op jit(solution)/shard_map/pallas_call | solution.py:505
  903.0 15.0 %bitcast_convert_fusion.refs_0_ = bf16[1024,1536]{1,0:T(8,128)(2,1)} fusion(bf16[2,1408,1536]{2,1,0:T(8,128)(2,1)} %shard_map.308, f32[1024]{0:T(1024)S(1)} %copy-done.47, f32[1024]{0:T(1024)S(1)} %copy-done.36, f32[2,1408]{1,0:T(2,128)S(1)} %copy-done.34, f32[2,1408]{1,0:T(2,128)S(1)} %copy-done.29, bf16[2,1370,1024]{2,1,0:T(8,128)(2,1)S(1)} %bitcast.160), kind=kOutput, calls=%fused_computation.55 | convolution fusion | flops 8877244416 | bytes 17438720 | tf_op jit(solution)/shard_map/dot_general | solution.py:22
  919.3 3.8 shard_map.309
  930.4 15.1 %fusion.75 = f32[2816,1024]{1,0:T(8,128)} fusion(bf16[2816,1536]{1,0:T(8,128)(2,1)} %bitcast.164, bf16[1024,1536]{1,0:T(8,128)(2,1)} %get-tuple-element.95), kind=kOutput, calls=%fused_computation.250 | convolution fusion | flops 8858370048 | bytes 23330816 | tf_op jit(solution)/shard_map/dot_general | solution.py:22
  959.7 6.1 collective-permute-done.56
  970.6 21.0 %fusion.28 = (f32[1024]{0:T(1024)S(1)}, f32[2816]{0:T(1024)S(1)}, f32[2816]{0:T(1024)S(1)}, f32[1024]{0:T(1024)S(1)}, f32[2816,1024]{1,0:T(8,128)}) fusion(f32[2816]{0:T(1024)S(1)} %copy-done.27, f32[2816]{0:T(1024)S(1)} %copy-done.25, bf16[2,1370,1024]{2,1,0:T(8,128)(2,1)} %reshape.485, f32[1024]{0:T(1024)S(1)} %copy-done.36, f32[2816,1024]{1,0:T(8,128)} %fusion.75, ...), kind=kOutput, calls=%fused_computation.44 | convolution fusion | flops 8890081280 | bytes 40534016 | tf_op jit(solution)/shard_map/dot_general | solution.py:22
  993.7 4.0 collective-permute-done.58
  1006.6 10.6 %fusion.27 = bf16[2816,1024]{1,0:T(8,128)(2,1)S(1)} fusion(f32[2816,1024]{1,0:T(8,128)} %copy-done.3, f32[2816,1024]{1,0:T(8,128)} %get-tuple-element.211, f32[2816]{0:T(1024)S(1)} %broadcast_multiply_fusion, f32[2816]{0:T(1024)S(1)} %broadcast_multiply_fusion.1, f32[1024]{0:T(1024)S(1)} %copy-done.36, f32[2816]{0:T(1024)S(1)} %copy-done.27, ...), kind=kLoop, calls=%fused_computation.43 | loop fusion | flops 28835840 | bytes 34496512 | tf_op jit(solution)/shard_map/convert_element_type | solution.py:858
  1020.4 6.2 reshape.499
  (434 shorter events, 183.4 us)
Async XLA Ops:
  2.9 35.7 %collective-permute-start = (f32[1,16,128]{2,1,0:T(8,128)S(1)}, f32[1,16,128]{2,1,0:T(8,128)S(1)}, u32[]{:S(2)}, u32[]{:S(2)}) collective-permute-start(f32[1,16,128]{2,1,0:T(8,128)S(1)} %bitcast_convert_fusion.2), channel_id=1, source_target_pairs={{0,8},{2,10},{4,12},{6,14},{8,0},{10,2},{12,4},{14,6},{16,24},{18,... | collective-permute-start | bytes 24584 | tf_op jit(solution)/shard_map/ppermute | solution.py:50
  6.0 34.1 %collective-permute-start.1 = (f32[1,16,128]{2,1,0:T(8,128)S(1)}, f32[1,16,128]{2,1,0:T(8,128)S(1)}, u32[]{:S(2)}, u32[]{:S(2)}) collective-permute-start(f32[1,16,128]{2,1,0:T(8,128)S(1)} %bitcast_convert_fusion.2), channel_id=1, source_target_pairs={{0,16},{2,18},{4,20},{6,22},{8,24},{10,26},{12,28},{14,30},{16,0},... | collective-permute-start | bytes 24584 | tf_op jit(solution)/shard_map/ppermute | solution.py:50
  8.6 33.0 %collective-permute-start.2 = (f32[1,16,128]{2,1,0:T(8,128)S(1)}, f32[1,16,128]{2,1,0:T(8,128)S(1)}, u32[]{:S(2)}, u32[]{:S(2)}) collective-permute-start(f32[1,16,128]{2,1,0:T(8,128)S(1)} %bitcast_convert_fusion.2), channel_id=1, source_target_pairs={{0,24},{2,26},{4,28},{6,30},{8,16},{10,18},{12,20},{14,22},{16,8},... | collective-permute-start | bytes 24584 | tf_op jit(solution)/shard_map/ppermute | solution.py:50
  10.8 33.7 %collective-permute-start.6 = (bf16[1,32,2048]{2,1,0:T(8,128)(2,1)S(1)}, bf16[1,32,2048]{2,1,0:T(8,128)(2,1)S(1)}, u32[]{:S(2)}, u32[]{:S(2)}) collective-permute-start(bf16[1,32,2048]{2,1,0:T(8,128)(2,1)S(1)} %get-tuple-element.169), channel_id=1, source_target_pairs={{0,16},{2,18},{4,20},{6,22},{8,24},{10,26},{12,28},{14,30},{16,0},... | collective-permute-start | bytes 393224 | tf_op jit(solution)/shard_map/ppermute | solution.py:50
  12.8 31.7 %collective-permute-start.7 = (bf16[1,32,2048]{2,1,0:T(8,128)(2,1)S(1)}, bf16[1,32,2048]{2,1,0:T(8,128)(2,1)S(1)}, u32[]{:S(2)}, u32[]{:S(2)}) collective-permute-start(bf16[1,32,2048]{2,1,0:T(8,128)(2,1)S(1)} %get-tuple-element.169), channel_id=1, source_target_pairs={{0,8},{2,10},{4,12},{6,14},{8,0},{10,2},{12,4},{14,6},{16,24},{18,... | collective-permute-start | bytes 393224 | tf_op jit(solution)/shard_map/ppermute | solution.py:50
  44.5 31.6 %collective-permute-start.3 = (f32[4,16,128]{2,1,0:T(8,128)S(1)}, f32[4,16,128]{2,1,0:T(8,128)S(1)}, u32[]{:S(2)}, u32[]{:S(2)}) collective-permute-start(f32[4,16,128]{2,1,0:T(8,128)S(1)} %pad_maximum_fusion.7), channel_id=1, source_target_pairs={{0,2},{2,0},{4,6},{6,4},{8,10},{10,8},{12,14},{14,12},{16,18},{18,... | collective-permute-start | bytes 98312 | tf_op jit(solution)/shard_map/ppermute | solution.py:50
  46.9 29.3 %collective-permute-start.4 = (f32[4,16,128]{2,1,0:T(8,128)S(1)}, f32[4,16,128]{2,1,0:T(8,128)S(1)}, u32[]{:S(2)}, u32[]{:S(2)}) collective-permute-start(f32[4,16,128]{2,1,0:T(8,128)S(1)} %pad_maximum_fusion.7), channel_id=1, source_target_pairs={{0,4},{2,6},{4,0},{6,2},{8,12},{10,14},{12,8},{14,10},{16,20},{18,... | collective-permute-start | bytes 98312 | tf_op jit(solution)/shard_map/ppermute | solution.py:50
  55.5 20.6 %collective-permute-start.5 = (f32[4,16,128]{2,1,0:T(8,128)S(1)}, f32[4,16,128]{2,1,0:T(8,128)S(1)}, u32[]{:S(2)}, u32[]{:S(2)}) collective-permute-start(f32[4,16,128]{2,1,0:T(8,128)S(1)} %pad_maximum_fusion.7), channel_id=1, source_target_pairs={{0,6},{2,4},{4,2},{6,0},{8,14},{10,12},{12,10},{14,8},{16,22},{18,... | collective-permute-start | bytes 98312 | tf_op jit(solution)/shard_map/ppermute | solution.py:50
  71.0 25.9 %collective-permute-start.10 = (bf16[8,32,2048]{2,1,0:T(8,128)(2,1)}, bf16[8,32,2048]{2,1,0:T(8,128)(2,1)S(1)}, u32[]{:S(2)}, u32[]{:S(2)}) collective-permute-start(bf16[8,32,2048]{2,1,0:T(8,128)(2,1)} %get-tuple-element.144), channel_id=1, source_target_pairs={{0,1},{1,0},{2,3},{3,2},{4,5},{5,4},{6,7},{7,6},{8,9},{9,8},{10,11... | collective-permute-start | bytes 3145736 | tf_op jit(solution)/shard_map/ppermute | solution.py:50
  74.4 25.6 %collective-permute-start.16 = (bf16[8,32,2048]{2,1,0:T(8,128)(2,1)}, bf16[8,32,2048]{2,1,0:T(8,128)(2,1)S(1)}, u32[]{:S(2)}, u32[]{:S(2)}) collective-permute-start(bf16[8,32,2048]{2,1,0:T(8,128)(2,1)} %copy-done.51), channel_id=1, source_target_pairs={{0,4},{2,6},{4,0},{6,2},{8,12},{10,14},{12,8},{14,10},{16,20},{18,... | collective-permute-start | bytes 3145736 | tf_op jit(solution)/shard_map/ppermute | solution.py:50
  98.0 16.7 %collective-permute-start.11 = (bf16[16,32,2048]{2,1,0:T(8,128)(2,1)}, bf16[16,32,2048]{2,1,0:T(8,128)(2,1)}, u32[]{:S(2)}, u32[]{:S(2)}) collective-permute-start(bf16[16,32,2048]{2,1,0:T(8,128)(2,1)} %constant_dynamic-update-slice_fusion.14.own_a), channel_id=1, source_target_pairs={{0,2},{2,0},{4,6},{6,4},{8,10},{10,8},{12,14},{14,12},{16,18},{18,... | collective-permute-start | bytes 6291464 | tf_op jit(solution)/shard_map/ppermute | solution.py:50
  114.7 65.8 %collective-permute-start.18 = (bf16[1,32,4096]{2,1,0:T(8,128)(2,1)S(1)}, bf16[1,32,4096]{2,1,0:T(8,128)(2,1)S(1)}, u32[]{:S(2)}, u32[]{:S(2)}) collective-permute-start(bf16[1,32,4096]{2,1,0:T(8,128)(2,1)S(1)} %get-tuple-element.141), channel_id=1, source_target_pairs={{0,16},{2,18},{4,20},{6,22},{8,24},{10,26},{12,28},{14,30},{16,0},... | collective-permute-start | bytes 786440 | tf_op jit(solution)/shard_map/ppermute | solution.py:50
  114.8 69.3 %collective-permute-start.19 = (bf16[1,32,4096]{2,1,0:T(8,128)(2,1)S(1)}, bf16[1,32,4096]{2,1,0:T(8,128)(2,1)S(1)}, u32[]{:S(2)}, u32[]{:S(2)}) collective-permute-start(bf16[1,32,4096]{2,1,0:T(8,128)(2,1)S(1)} %get-tuple-element.141), channel_id=1, source_target_pairs={{0,8},{2,10},{4,12},{6,14},{8,0},{10,2},{12,4},{14,6},{16,24},{18,... | collective-permute-start | bytes 786440 | tf_op jit(solution)/shard_map/ppermute | solution.py:50
  115.6 68.5 %collective-permute-start.20 = (bf16[1,32,4096]{2,1,0:T(8,128)(2,1)S(1)}, bf16[1,32,4096]{2,1,0:T(8,128)(2,1)S(1)}, u32[]{:S(2)}, u32[]{:S(2)}) collective-permute-start(bf16[1,32,4096]{2,1,0:T(8,128)(2,1)S(1)} %get-tuple-element.141), channel_id=1, source_target_pairs={{0,24},{2,26},{4,28},{6,30},{8,16},{10,18},{12,20},{14,22},{16,8},... | collective-permute-start | bytes 786440 | tf_op jit(solution)/shard_map/ppermute | solution.py:50
  179.7 19.1 %collective-permute-start.23 = (bf16[1,32,4096]{2,1,0:T(8,128)(2,1)S(1)}, bf16[1,32,4096]{2,1,0:T(8,128)(2,1)S(1)}, u32[]{:S(2)}, u32[]{:S(2)}) collective-permute-start(bf16[1,32,4096]{2,1,0:T(8,128)(2,1)S(1)} %get-tuple-element.140), channel_id=1, source_target_pairs={{0,8},{2,10},{4,12},{6,14},{8,0},{10,2},{12,4},{14,6},{16,24},{18,... | collective-permute-start | bytes 786440 | tf_op jit(solution)/shard_map/ppermute | solution.py:50
  180.5 18.3 %collective-permute-start.24 = (bf16[1,32,4096]{2,1,0:T(8,128)(2,1)S(1)}, bf16[1,32,4096]{2,1,0:T(8,128)(2,1)S(1)}, u32[]{:S(2)}, u32[]{:S(2)}) collective-permute-start(bf16[1,32,4096]{2,1,0:T(8,128)(2,1)S(1)} %get-tuple-element.140), channel_id=1, source_target_pairs={{0,24},{2,26},{4,28},{6,30},{8,16},{10,18},{12,20},{14,22},{16,8},... | collective-permute-start | bytes 786440 | tf_op jit(solution)/shard_map/ppermute | solution.py:50
  184.2 47.9 %collective-permute-start.21 = (bf16[4,32,4096]{2,1,0:T(8,128)(2,1)S(1)}, bf16[4,32,4096]{2,1,0:T(8,128)(2,1)S(1)}, u32[]{:S(2)}, u32[]{:S(2)}) collective-permute-start(bf16[4,32,4096]{2,1,0:T(8,128)(2,1)S(1)} %pad_maximum_fusion), channel_id=1, source_target_pairs={{0,4},{2,6},{4,0},{6,2},{8,12},{10,14},{12,8},{14,10},{16,20},{18,... | collective-permute-start | bytes 3145736 | tf_op jit(solution)/shard_map/ppermute | solution.py:50
  199.0 36.3 %collective-permute-start.25 = (bf16[4,32,4096]{2,1,0:T(8,128)(2,1)S(1)}, bf16[4,32,4096]{2,1,0:T(8,128)(2,1)S(1)}, u32[]{:S(2)}, u32[]{:S(2)}) collective-permute-start(bf16[4,32,4096]{2,1,0:T(8,128)(2,1)S(1)} %pad_maximum_fusion.1), channel_id=1, source_target_pairs={{0,1},{1,0},{2,3},{3,2},{4,5},{5,4},{6,7},{7,6},{8,9},{9,8},{10,11... | collective-permute-start | bytes 3145736 | tf_op jit(solution)/shard_map/ppermute | solution.py:50
  233.7 59.7 %collective-permute-start.26 = (bf16[8,32,4096]{2,1,0:T(8,128)(2,1)}, bf16[8,32,4096]{2,1,0:T(8,128)(2,1)S(1)}, u32[]{:S(2)}, u32[]{:S(2)}) collective-permute-start(bf16[8,32,4096]{2,1,0:T(8,128)(2,1)} %get-tuple-element.135), channel_id=1, source_target_pairs={{0,1},{1,0},{2,3},{3,2},{4,5},{5,4},{6,7},{7,6},{8,9},{9,8},{10,11... | collective-permute-start | bytes 6291464 | tf_op jit(solution)/shard_map/ppermute | solution.py:50
  236.8 58.2 %collective-permute-start.27 = (bf16[8,32,4096]{2,1,0:T(8,128)(2,1)}, bf16[8,32,4096]{2,1,0:T(8,128)(2,1)S(1)}, u32[]{:S(2)}, u32[]{:S(2)}) collective-permute-start(bf16[8,32,4096]{2,1,0:T(8,128)(2,1)} %get-tuple-element.133), channel_id=1, source_target_pairs={{0,4},{2,6},{4,0},{6,2},{8,12},{10,14},{12,8},{14,10},{16,20},{18,... | collective-permute-start | bytes 6291464 | tf_op jit(solution)/shard_map/ppermute | solution.py:50
  295.0 29.0 %collective-permute-start.28 = (bf16[16,32,4096]{2,1,0:T(8,128)(2,1)}, bf16[16,32,4096]{2,1,0:T(8,128)(2,1)}, u32[]{:S(2)}, u32[]{:S(2)}) collective-permute-start(bf16[16,32,4096]{2,1,0:T(8,128)(2,1)} %constant_dynamic-update-slice_fusion.41.own_a), channel_id=1, source_target_pairs={{0,2},{2,0},{4,6},{6,4},{8,10},{10,8},{12,14},{14,12},{16,18},{18,... | collective-permute-start | bytes 12582920 | tf_op jit(solution)/shard_map/ppermute | solution.py:50
  296.5 27.4 %collective-permute-start.29 = (bf16[16,32,4096]{2,1,0:T(8,128)(2,1)}, bf16[16,32,4096]{2,1,0:T(8,128)(2,1)}, u32[]{:S(2)}, u32[]{:S(2)}) collective-permute-start(bf16[16,32,4096]{2,1,0:T(8,128)(2,1)} %constant_dynamic-update-slice_fusion.47.own_b), channel_id=1, source_target_pairs={{0,2},{2,0},{4,6},{6,4},{8,10},{10,8},{12,14},{14,12},{16,18},{18,... | collective-permute-start | bytes 12582920 | tf_op jit(solution)/shard_map/ppermute | solution.py:50
  597.6 53.2 %collective-permute-start.30 = (bf16[16,32,4096]{2,1,0:T(8,128)(2,1)}, bf16[16,32,4096]{2,1,0:T(8,128)(2,1)}, u32[]{:S(2)}, u32[]{:S(2)}) collective-permute-start(bf16[16,32,4096]{2,1,0:T(8,128)(2,1)} %get-tuple-element.79), channel_id=1, source_target_pairs={{0,2},{2,0},{4,6},{6,4},{8,10},{10,8},{12,14},{14,12},{16,18},{18,... | collective-permute-start | bytes 12582920 | tf_op jit(solution)/shard_map/ppermute | solution.py:50
  597.6 59.2 %collective-permute-start.32 = (bf16[16,32,4096]{2,1,0:T(8,128)(2,1)}, bf16[16,32,4096]{2,1,0:T(8,128)(2,1)}, u32[]{:S(2)}, u32[]{:S(2)}) collective-permute-start(bf16[16,32,4096]{2,1,0:T(8,128)(2,1)} %get-tuple-element.81), channel_id=1, source_target_pairs={{0,2},{2,0},{4,6},{6,4},{8,10},{10,8},{12,14},{14,12},{16,18},{18,... | collective-permute-start | bytes 12582920 | tf_op jit(solution)/shard_map/ppermute | solution.py:50
  656.3 49.4 %collective-permute-start.31 = (bf16[8,32,4096]{2,1,0:T(8,128)(2,1)}, bf16[8,32,4096]{2,1,0:T(8,128)(2,1)S(1)}, u32[]{:S(2)}, u32[]{:S(2)}) collective-permute-start(bf16[8,32,4096]{2,1,0:T(8,128)(2,1)} %slice.389), channel_id=1, source_target_pairs={{0,1},{1,0},{2,3},{3,2},{4,5},{5,4},{6,7},{7,6},{8,9},{9,8},{10,11... | collective-permute-start | bytes 6291464 | tf_op jit(solution)/shard_map/ppermute | solution.py:50
  664.0 47.6 %collective-permute-start.33 = (bf16[8,32,4096]{2,1,0:T(8,128)(2,1)}, bf16[8,32,4096]{2,1,0:T(8,128)(2,1)}, u32[]{:S(2)}, u32[]{:S(2)}) collective-permute-start(bf16[8,32,4096]{2,1,0:T(8,128)(2,1)} %slice.392), channel_id=1, source_target_pairs={{0,4},{2,6},{4,0},{6,2},{8,12},{10,14},{12,8},{14,10},{16,20},{18,... | collective-permute-start | bytes 6291464 | tf_op jit(solution)/shard_map/ppermute | solution.py:50
  715.1 68.7 %collective-permute-start.40 = (bf16[4,32,4096]{2,1,0:T(8,128)(2,1)}, bf16[4,32,4096]{2,1,0:T(8,128)(2,1)}, u32[]{:S(2)}, u32[]{:S(2)}) collective-permute-start(bf16[4,32,4096]{2,1,0:T(8,128)(2,1)} %slice.394), channel_id=1, source_target_pairs={{0,4},{2,6},{4,0},{6,2},{8,12},{10,14},{12,8},{14,10},{16,20},{18,... | collective-permute-start | bytes 3145736 | tf_op jit(solution)/shard_map/ppermute | solution.py:50
  716.2 76.9 %collective-permute-start.44 = (bf16[4,32,4096]{2,1,0:T(8,128)(2,1)}, bf16[4,32,4096]{2,1,0:T(8,128)(2,1)}, u32[]{:S(2)}, u32[]{:S(2)}) collective-permute-start(bf16[4,32,4096]{2,1,0:T(8,128)(2,1)} %slice.395), channel_id=1, source_target_pairs={{0,1},{1,0},{2,3},{3,2},{4,5},{5,4},{6,7},{7,6},{8,9},{9,8},{10,11... | collective-permute-start | bytes 3145736 | tf_op jit(solution)/shard_map/ppermute | solution.py:50
  778.6 17.0 %collective-permute-start.34 = (bf16[16,32,1280]{2,1,0:T(8,128)(2,1)}, bf16[16,32,1280]{2,1,0:T(8,128)(2,1)}, u32[]{:S(2)}, u32[]{:S(2)}) collective-permute-start(bf16[16,32,1280]{2,1,0:T(8,128)(2,1)} %get-tuple-element.86), channel_id=1, source_target_pairs={{0,2},{2,0},{4,6},{6,4},{8,10},{10,8},{12,14},{14,12},{16,18},{18,... | collective-permute-start | bytes 3932168 | tf_op jit(solution)/shard_map/ppermute | solution.py:50
  778.6 20.2 %collective-permute-start.37 = (bf16[16,32,1280]{2,1,0:T(8,128)(2,1)}, bf16[16,32,1280]{2,1,0:T(8,128)(2,1)}, u32[]{:S(2)}, u32[]{:S(2)}) collective-permute-start(bf16[16,32,1280]{2,1,0:T(8,128)(2,1)} %get-tuple-element.88), channel_id=1, source_target_pairs={{0,2},{2,0},{4,6},{6,4},{8,10},{10,8},{12,14},{14,12},{16,18},{18,... | collective-permute-start | bytes 3932168 | tf_op jit(solution)/shard_map/ppermute | solution.py:50
  786.6 55.7 %collective-permute-start.43 = (bf16[1,32,4096]{2,1,0:T(8,128)(2,1)}, bf16[1,32,4096]{2,1,0:T(8,128)(2,1)S(1)}, u32[]{:S(2)}, u32[]{:S(2)}) collective-permute-start(bf16[1,32,4096]{2,1,0:T(8,128)(2,1)} %get-tuple-element.130), channel_id=1, source_target_pairs={{0,24},{2,26},{4,28},{6,30},{8,16},{10,18},{12,20},{14,22},{16,8},... | collective-permute-start | bytes 786440 | tf_op jit(solution)/shard_map/ppermute | solution.py:50
  788.9 55.3 %collective-permute-start.42 = (bf16[1,32,4096]{2,1,0:T(8,128)(2,1)}, bf16[1,32,4096]{2,1,0:T(8,128)(2,1)S(1)}, u32[]{:S(2)}, u32[]{:S(2)}) collective-permute-start(bf16[1,32,4096]{2,1,0:T(8,128)(2,1)} %get-tuple-element.131), channel_id=1, source_target_pairs={{0,8},{2,10},{4,12},{6,14},{8,0},{10,2},{12,4},{14,6},{16,24},{18,... | collective-permute-start | bytes 786440 | tf_op jit(solution)/shard_map/ppermute | solution.py:50
  793.1 51.5 %collective-permute-start.41 = (bf16[1,32,4096]{2,1,0:T(8,128)(2,1)}, bf16[1,32,4096]{2,1,0:T(8,128)(2,1)}, u32[]{:S(2)}, u32[]{:S(2)}) collective-permute-start(bf16[1,32,4096]{2,1,0:T(8,128)(2,1)} %get-tuple-element.129), channel_id=1, source_target_pairs={{0,16},{2,18},{4,20},{6,22},{8,24},{10,26},{12,28},{14,30},{16,0},... | collective-permute-start | bytes 786440 | tf_op jit(solution)/shard_map/ppermute | solution.py:50
  795.6 51.1 %collective-permute-start.47 = (bf16[1,32,4096]{2,1,0:T(8,128)(2,1)S(1)}, bf16[1,32,4096]{2,1,0:T(8,128)(2,1)S(1)}, u32[]{:S(2)}, u32[]{:S(2)}) collective-permute-start(bf16[1,32,4096]{2,1,0:T(8,128)(2,1)S(1)} %get-tuple-element.127), channel_id=1, source_target_pairs={{0,24},{2,26},{4,28},{6,30},{8,16},{10,18},{12,20},{14,22},{16,8},... | collective-permute-start | bytes 786440 | tf_op jit(solution)/shard_map/ppermute | solution.py:50
  798.8 47.9 %collective-permute-start.46 = (bf16[1,32,4096]{2,1,0:T(8,128)(2,1)S(1)}, bf16[1,32,4096]{2,1,0:T(8,128)(2,1)S(1)}, u32[]{:S(2)}, u32[]{:S(2)}) collective-permute-start(bf16[1,32,4096]{2,1,0:T(8,128)(2,1)S(1)} %get-tuple-element.128), channel_id=1, source_target_pairs={{0,8},{2,10},{4,12},{6,14},{8,0},{10,2},{12,4},{14,6},{16,24},{18,... | collective-permute-start | bytes 786440 | tf_op jit(solution)/shard_map/ppermute | solution.py:50
  844.6 16.6 %collective-permute-start.38 = (bf16[8,32,1280]{2,1,0:T(8,128)(2,1)S(1)}, bf16[8,32,1280]{2,1,0:T(8,128)(2,1)S(1)}, u32[]{:S(2)}, u32[]{:S(2)}) collective-permute-start(bf16[8,32,1280]{2,1,0:T(8,128)(2,1)S(1)} %slice.402), channel_id=1, source_target_pairs={{0,4},{2,6},{4,0},{6,2},{8,12},{10,14},{12,8},{14,10},{16,20},{18,... | collective-permute-start | bytes 1966088 | tf_op jit(solution)/shard_map/ppermute | solution.py:50
  860.3 63.4 %collective-permute-start.36 = (bf16[4,32,1280]{2,1,0:T(8,128)(2,1)}, bf16[4,32,1280]{2,1,0:T(8,128)(2,1)}, u32[]{:S(2)}, u32[]{:S(2)}) collective-permute-start(bf16[4,32,1280]{2,1,0:T(8,128)(2,1)} %slice.399), channel_id=1, source_target_pairs={{0,4},{2,6},{4,0},{6,2},{8,12},{10,14},{12,8},{14,10},{16,20},{18,... | collective-permute-start | bytes 983048 | tf_op jit(solution)/shard_map/ppermute | solution.py:50
  861.5 65.2 %collective-permute-start.39 = (bf16[4,32,1280]{2,1,0:T(8,128)(2,1)S(1)}, bf16[4,32,1280]{2,1,0:T(8,128)(2,1)}, u32[]{:S(2)}, u32[]{:S(2)}) collective-permute-start(bf16[4,32,1280]{2,1,0:T(8,128)(2,1)S(1)} %slice.404), channel_id=1, source_target_pairs={{0,1},{1,0},{2,3},{3,2},{4,5},{5,4},{6,7},{7,6},{8,9},{9,8},{10,11... | collective-permute-start | bytes 983048 | tf_op jit(solution)/shard_map/ppermute | solution.py:50
  923.0 31.7 %collective-permute-start.54 = (bf16[16,32,768]{2,1,0:T(8,128)(2,1)}, bf16[16,32,768]{2,1,0:T(8,128)(2,1)}, u32[]{:S(2)}, u32[]{:S(2)}) collective-permute-start(bf16[16,32,768]{2,1,0:T(8,128)(2,1)} %get-tuple-element.93), channel_id=1, source_target_pairs={{0,2},{2,0},{4,6},{6,4},{8,10},{10,8},{12,14},{14,12},{16,18},{18,... | collective-permute-start | bytes 2359304 | tf_op jit(solution)/shard_map/ppermute | solution.py:50
  923.0 34.4 %collective-permute-start.55 = (bf16[16,32,768]{2,1,0:T(8,128)(2,1)}, bf16[16,32,768]{2,1,0:T(8,128)(2,1)S(1)}, u32[]{:S(2)}, u32[]{:S(2)}) collective-permute-start(bf16[16,32,768]{2,1,0:T(8,128)(2,1)} %get-tuple-element.94), channel_id=1, source_target_pairs={{0,2},{2,0},{4,6},{6,4},{8,10},{10,8},{12,14},{14,12},{16,18},{18,... | collective-permute-start | bytes 2359304 | tf_op jit(solution)/shard_map/ppermute | solution.py:50
  924.8 20.7 %collective-permute-start.50 = (bf16[1,32,1280]{2,1,0:T(8,128)(2,1)S(1)}, bf16[1,32,1280]{2,1,0:T(8,128)(2,1)S(1)}, u32[]{:S(2)}, u32[]{:S(2)}) collective-permute-start(bf16[1,32,1280]{2,1,0:T(8,128)(2,1)S(1)} %get-tuple-element.149), channel_id=1, source_target_pairs={{0,24},{2,26},{4,28},{6,30},{8,16},{10,18},{12,20},{14,22},{16,8},... | collective-permute-start | bytes 245768 | tf_op jit(solution)/shard_map/ppermute | solution.py:50
  926.6 20.6 %collective-permute-start.49 = (bf16[1,32,1280]{2,1,0:T(8,128)(2,1)S(1)}, bf16[1,32,1280]{2,1,0:T(8,128)(2,1)S(1)}, u32[]{:S(2)}, u32[]{:S(2)}) collective-permute-start(bf16[1,32,1280]{2,1,0:T(8,128)(2,1)S(1)} %get-tuple-element.150), channel_id=1, source_target_pairs={{0,8},{2,10},{4,12},{6,14},{8,0},{10,2},{12,4},{14,6},{16,24},{18,... | collective-permute-start | bytes 245768 | tf_op jit(solution)/shard_map/ppermute | solution.py:50
  926.6 20.6 %collective-permute-start.48 = (bf16[1,32,1280]{2,1,0:T(8,128)(2,1)S(1)}, bf16[1,32,1280]{2,1,0:T(8,128)(2,1)S(1)}, u32[]{:S(2)}, u32[]{:S(2)}) collective-permute-start(bf16[1,32,1280]{2,1,0:T(8,128)(2,1)S(1)} %get-tuple-element.151), channel_id=1, source_target_pairs={{0,16},{2,18},{4,20},{6,22},{8,24},{10,26},{12,28},{14,30},{16,0},... | collective-permute-start | bytes 245768 | tf_op jit(solution)/shard_map/ppermute | solution.py:50
  968.3 59.5 %collective-permute-start.69 = (bf16[4,32,768]{2,1,0:T(8,128)(2,1)S(1)}, bf16[4,32,768]{2,1,0:T(8,128)(2,1)S(1)}, u32[]{:S(2)}, u32[]{:S(2)}) collective-permute-start(bf16[4,32,768]{2,1,0:T(8,128)(2,1)S(1)} %slice.427), channel_id=1, source_target_pairs={{0,1},{1,0},{2,3},{3,2},{4,5},{5,4},{6,7},{7,6},{8,9},{9,8},{10,11... | collective-permute-start | bytes 589832 | tf_op jit(solution)/shard_map/ppermute | solution.py:50
  969.4 62.9 %collective-permute-start.65 = (bf16[4,32,768]{2,1,0:T(8,128)(2,1)S(1)}, bf16[4,32,768]{2,1,0:T(8,128)(2,1)S(1)}, u32[]{:S(2)}, u32[]{:S(2)}) collective-permute-start(bf16[4,32,768]{2,1,0:T(8,128)(2,1)S(1)} %slice.426), channel_id=1, source_target_pairs={{0,4},{2,6},{4,0},{6,2},{8,12},{10,14},{12,8},{14,10},{16,20},{18,... | collective-permute-start | bytes 589832 | tf_op jit(solution)/shard_map/ppermute | solution.py:50
  1002.2 24.3 %collective-permute-start.64 = (f32[1,16,128]{2,1,0:T(8,128)S(1)}, f32[1,16,128]{2,1,0:T(8,128)S(1)}, u32[]{:S(2)}, u32[]{:S(2)}) collective-permute-start(f32[1,16,128]{2,1,0:T(8,128)S(1)} %get-tuple-element.194), channel_id=1, source_target_pairs={{0,24},{2,26},{4,28},{6,30},{8,16},{10,18},{12,20},{14,22},{16,8},... | collective-permute-start | bytes 24584 | tf_op jit(solution)/shard_map/ppermute | solution.py:50
  1004.8 21.7 %collective-permute-start.63 = (f32[1,16,128]{2,1,0:T(8,128)S(1)}, f32[1,16,128]{2,1,0:T(8,128)S(1)}, u32[]{:S(2)}, u32[]{:S(2)}) collective-permute-start(f32[1,16,128]{2,1,0:T(8,128)S(1)} %get-tuple-element.195), channel_id=1, source_target_pairs={{0,16},{2,18},{4,20},{6,22},{8,24},{10,26},{12,28},{14,30},{16,0},... | collective-permute-start | bytes 24584 | tf_op jit(solution)/shard_map/ppermute | solution.py:50
  1004.8 21.7 %collective-permute-start.62 = (f32[1,16,128]{2,1,0:T(8,128)S(1)}, f32[1,16,128]{2,1,0:T(8,128)S(1)}, u32[]{:S(2)}, u32[]{:S(2)}) collective-permute-start(f32[1,16,128]{2,1,0:T(8,128)S(1)} %get-tuple-element.193), channel_id=1, source_target_pairs={{0,8},{2,10},{4,12},{6,14},{8,0},{10,2},{12,4},{14,6},{16,24},{18,... | collective-permute-start | bytes 24584 | tf_op jit(solution)/shard_map/ppermute | solution.py:50
  (88 other events, 2719.8 us)

commit v3 on v2

--- a/solution.py
+++ b/solution.py
@@ -81,8 +81,7 @@
         return jnp.stack(rows + [core]).astype(jnp.int32)
 
     def gather(self, shard):
-        half = shard.shape[0] // 2
-        return Gather(self, [shard[:half][None], shard[half:][None]])
+        return Gather(self, [shard[None]])
 
     def assemble(self, pieces, tables, half, widths):
         pairs = self.dp // 2
@@ -287,7 +286,11 @@
         self.stages = len(tree.orders[0])
 
     def step(self):
-        if self.done < self.stages:
+        if self.done == 0:
+            whole = self.tree.spread(self.held[0], self.tree.orders[0][0])
+            half = whole.shape[1] // 2
+            self.held = [whole[:, :half], whole[:, half:]]
+        elif self.done < self.stages:
             self.held = [
                 self.tree.spread(held, order[self.done])
                 for held, order in zip(self.held, self.tree.orders)
@@ -315,28 +318,37 @@
         self.done = 0
 
     def step(self):
-        if self.done == len(self.orders[0]):
+        if self.issued():
             return
-        last = self.done + 1 == len(self.orders[0])
-        for side, order in enumerate(self.orders):
-            stage = order[self.done]
-            held = self.held[side].astype(F32)
-            for value, mask in zip(self.sent[side], self.tree.masks(stage)):
-                held = held + self.tree.swap(value, stage[0], mask).astype(F32)
-            if not last:
-                held = held.astype(BF16)
-                count = 1 << len(order[self.done + 1][1])
-                size = held.shape[0] // count
-                held, *self.sent[side] = [
-                    held[place * size : (place + 1) * size] for place in range(count)
-                ]
-            self.held[side] = held
+        totals = []
+        for held, sent, order in zip(self.held, self.sent, self.orders):
+            axis = order[self.done][0]
+            total = held.astype(F32)
+            for value, mask in zip(sent, self.tree.masks(order[self.done])):
+                total = total + self.tree.swap(value, axis, mask).astype(F32)
+            totals.append(total)
         self.done += 1
+        if self.issued():
+            self.held, self.sent = totals, []
+            return
+        if self.done + 1 == len(self.orders[0]):
+            totals = [jnp.concatenate(totals, axis=1)]
+        self.held, self.sent = [], []
+        for total, order in zip(totals, self.orders):
+            total = total.astype(BF16)
+            count = 1 << len(order[self.done][1])
+            size = total.shape[0] // count
+            parts = [total[place * size : (place + 1) * size] for place in range(count)]
+            self.held.append(parts[0])
+            self.sent.append(parts[1:])
+
+    def issued(self):
+        return self.done == len(self.orders[0])
 
     def finish(self):
-        while self.done < len(self.orders[0]):
+        while not self.issued():
             self.step()
-        whole = jnp.concatenate([held[0] for held in self.held], axis=0)
+        whole = self.held[0][0]
         parts, at = [], 0
         for width in self.widths:
             parts.append(whole[:, at : at + width])
@@ -344,9 +356,37 @@
         return parts
 
 
-def after(value, *chains):
-    waits = [(chain.held, getattr(chain, "sent", ())) for chain in chains]
-    return lax.optimization_barrier((value, waits))[0]
+def held_by(*chains):
+    arrays = []
+    for chain in chains:
+        arrays += chain.held
+        for sent in getattr(chain, "sent", ()):
+            arrays += sent
+    return arrays
+
+
+def hold(arrays, *others):
+    count = len(arrays)
+
+    def kernel(*refs):
+        refs[-1][...] = jnp.zeros(refs[-1].shape, F32)
+
+    unread = pl.BlockSpec(memory_space=pl.ANY)
+    outs = pl.pallas_call(
+        kernel,
+        in_specs=[unread] * (count + len(others)),
+        out_specs=[unread] * count + [pl.BlockSpec(memory_space=pltpu.VMEM)],
+        out_shape=[jax.ShapeDtypeStruct(array.shape, array.dtype) for array in arrays]
+        + [jax.ShapeDtypeStruct((8, 128), F32)],
+        input_output_aliases={place: place for place in range(count)},
+    )(*arrays, *others)
+    return list(outs[:count])
+
+
+def after(value, *arrays):
+    for array in arrays:
+        value = value + (array[(0,) * array.ndim].astype(F32) * 0.0).astype(value.dtype)
+    return value
 
 
 def split_pair(block):
@@ -446,7 +486,7 @@
     )
 
 
-def attend_forward(piece, ticket, triple, gathered, kept, segment, valid):
+def attend_forward(piece, ticket, triple, gathered, kept, waits, segment, valid):
     groups, part_pairs, all_pairs, part_at, all_at = piece
     images, rows, _ = triple.shape
     key_rows = gathered.shape[1]
@@ -463,7 +503,7 @@
                 pl.BlockSpec((None, rows, 3 * PAIR), narrow),
                 pl.BlockSpec((None, key_rows, 3 * PAIR), narrow),
             ]
-            + [unread] * len(kept),
+            + [unread] * (len(kept) + len(waits)),
             out_specs=[
                 pl.BlockSpec((None, rows, PAIR), wide),
                 pl.BlockSpec((None, rows, PAIR), wide),
@@ -477,10 +517,12 @@
         input_output_aliases={3 + place: place for place in range(len(kept))},
         cost_estimate=attend_cost(2, images, groups, rows, key_rows),
         compiler_params=pltpu.CompilerParams(vmem_limit_bytes=VMEM),
-    )(ticket, triple, gathered, *kept)
-
-
-def attend_backward(piece, ticket, triple, gathered, mixed, mixed_grad, logsum, kept, segment, valid):
+    )(ticket, triple, gathered, *kept, *waits)
+
+
+def attend_backward(
+    piece, ticket, triple, gathered, mixed, mixed_grad, logsum, kept, waits, segment, valid
+):
     groups, part_pairs, all_pairs, part_at, all_at = piece
     images, rows, width = triple.shape
     key_rows = gathered.shape[1]
@@ -514,7 +556,7 @@
                 wide_spec,
                 wide_spec,
             ]
-            + [pl.BlockSpec(memory_space=pl.ANY)] * len(kept),
+            + [pl.BlockSpec(memory_space=pl.ANY)] * (len(kept) + len(waits)),
             out_specs=out_specs,
             scratch_shapes=[pltpu.VMEM((PAIR, key_rows), F32)] * 2,
         ),
@@ -522,7 +564,7 @@
         input_output_aliases={6 + place: place for place in range(len(kept))},
         cost_estimate=attend_cost(5, images, groups, rows, key_rows),
         compiler_params=pltpu.CompilerParams(vmem_limit_bytes=VMEM),
-    )(ticket, triple, gathered, mixed, mixed_grad, logsum, *kept)
+    )(ticket, triple, gathered, mixed, mixed_grad, logsum, *kept, *waits)
 
 
 def join_grads(outs, pairs, shares, tensor):
@@ -748,20 +790,22 @@
         .transpose(0, 2, 1, 3)
         .reshape(shard_rows, 3 * local)
     )
-    first = tree.gather(jnp.concatenate([triple_shard, merge_weight], axis=1))
-    for _ in range(first.stages + 1):
-        first.step()
-    feed_chain = tree.gather(
-        after(jnp.concatenate([expand_weight, reduce_weight], axis=1), first)
-    )
-    feed_chain.step()
-    *triple_full, merge_full = first.finish(
-        tables, [part_width] * parts + [merge_weight.shape[1]]
-    )
-
     inputs = pad(tokens).astype(F32)
     normal_one, inverse_one = norm_parts(inputs)
     normed_one = (normal_one * gain_one + shift_one).astype(BF16)
+    first = tree.gather(jnp.concatenate([triple_shard, merge_weight], axis=1))
+    first.step()
+    feed_chain = tree.gather(
+        after(jnp.concatenate([expand_weight, reduce_weight], axis=1), *first.held)
+    )
+    feed_chain.step()
+    first.step()
+    while first.done < first.stages:
+        first.step()
+    first.step()
+    *triple_full, merge_full = first.finish(
+        tables, [part_width] * parts + [merge_weight.shape[1]]
+    )
     pairs = tree.tensor * local_pairs
     bias = jnp.stack(
         [
@@ -788,16 +832,17 @@
     kept = ()
     for number, (part, at) in enumerate(places):
         piece = (tree.tensor, part_pairs, local_pairs, at, part * part_pairs + at)
-        passed = ticket
-        if number in (1, 2):
-            passed = after(ticket, feed_chain)
+        waits = []
+        if number in (0, 1, 3):
+            feed_chain.held = hold(feed_chain.held, *(kept or triples))
+            waits = held_by(feed_chain)
             feed_chain.step()
         kept = attend_forward(
-            piece, passed, triples[part], pair_rows[part], kept, padded, segment_rows
+            piece, ticket, triples[part], pair_rows[part], kept, waits, padded, segment_rows
         )
     mixed, logsum = kept
     mixed_rows = mixed.reshape(rows, width)
-    branch_one = dot(mixed_rows, merge_full, 1, 1) + after(merge_shift, feed_chain)
+    branch_one = dot(mixed_rows, merge_full, 1, 1) + merge_shift
     middle = inputs + scale_one * branch_one
     normal_two, inverse_two = norm_parts(middle)
     normed_two = (normal_two * gain_two + shift_two).astype(BF16)
@@ -820,21 +865,26 @@
     mixed_grad = dot(back_one, merge_full, 1, 0).astype(BF16).reshape(images, padded, width)
     merge_grad = dot(back_one, mixed_rows, 0, 0).astype(BF16)
     chains, part_grads, kept = [feed_chain], [], ()
+    early, normed_one_grad = [], None
     for number, (part, at) in enumerate(places):
         piece = (tree.tensor, part_pairs, local_pairs, at, part * part_pairs + at)
         kept = attend_backward(
             piece,
-            after(ticket, *chains),
+            ticket,
             triples[part],
             pair_rows[part],
             mixed,
             mixed_grad,
             logsum,
             kept,
+            held_by(*chains) + early,
             padded,
             segment_rows,
         )
-        for chain in chains:
+        waiting = [chain for chain in chains if not chain.issued()]
+        held = hold([array for chain in waiting for array in chain.held], *kept)
+        for chain in waiting:
+            chain.held = [held.pop(0) for _ in chain.held]
             chain.step()
         if at == part_pairs - 1:
             grad = join_grads(kept, tree.tensor * part_pairs, shares, tree.tensor)
@@ -845,15 +895,13 @@
             if part == 0:
                 sent.append(merge_grad)
             chains.append(tree.scatter(sent, tables))
-            if part + 1 < parts:
-                chains[-1].step()
-    normed_one_grad = None
-    for grad, full_part in zip(part_grads, triple_full):
-        term = dot(grad, after(full_part, *chains[1:]), 1, 1)
-        normed_one_grad = term if normed_one_grad is None else normed_one_grad + term
-        for chain in chains:
-            chain.step()
-    late_gain = after(gain_one, *chains[1:])
+            term = dot(grad, triple_full[part], 1, 1)
+            normed_one_grad = term if normed_one_grad is None else normed_one_grad + term
+            early = [normed_one_grad]
+    for chain in chains:
+        chain.step()
+    late_gain = after(gain_one, *held_by(chains[-1]))
+    chains[-1].step()
     tokens_grad = middle_grad + norm_backward(normed_one_grad, late_gain, normal_one, inverse_one)
     tokens_grad = unpad(tokens_grad.astype(BF16))
     expand_out, reduce_out = chains[0].finish()

time: 1050 us -> 1010 us (0.962)
  starting transfers between devices: 86.4 us -> 58.7 us
  waiting for transfers between devices: 87.8 us -> 64.9 us
  other arithmetic: 96.9 us -> 116 us
  local copies, waits for them, and re-layouts: 81.8 us -> 67.8 us
    ppermute x73 -> x58, starting transfers between devices: 86.4 us -> 58.7 us  [swap(): return lax.ppermute(value, axis, [(i, i ^ mask) for i in range(size)])]
    ppermute x73 -> x58, waiting for transfers between devices: 87.8 us -> 64.9 us  [swap(): return lax.ppermute(value, axis, [(i, i ^ mask) for i in range(size)])]
    unnamed x149 -> x162, local copies, waits for them, and re-layouts: 20.8 us -> 5.96 us
    concatenate x5 -> x11, other arithmetic: 0.4 us -> 11.5 us  [spread(): jnp.concatenate([held] + [self.swap(held, stage[0], mask) for mask in sel...]
    convert_element_type x18 -> x12, other arithmetic: 23.7 us -> 22.3 us  [step(): total = total.astype(BF16)]
  transfers between devices with their start and end apart: 73 -> 58, of which waited for: 21 -> 17; matrix products, arithmetic and copies ran while one was open for 28% -> 26% of each run, Pallas kernels for 28% -> 29%
where the time goes in v3:
time: 1010 us; the launch traced here: 999 us
  Pallas kernels  557 us (55%)
  matrix products  128 us (13%)
  other arithmetic  116 us (11%)
  local copies, waits for them, and re-layouts  67.8 us (7%)
  waiting for transfers between devices  64.9 us (6%)
  starting transfers between devices  58.7 us (6%)
    pallas_call x1, Pallas kernels, feed_forward(): pl.pallas_call(functools.partial(feed_kernel, tile), grid=(hidden // bloc...  227 us
    pallas_call x4, Pallas kernels, attend_backward(): pl.pallas_call(functools.partial(attend_backward_kernel, segment, valid,...  163 us
    dot_general x9, matrix products, dot(): return lax.dot_general(left, right, dims, preferred_element_type=F32)  128 us
    pallas_call x4, Pallas kernels, attend_forward(): pl.pallas_call(functools.partial(attend_forward_kernel, segment, valid),...  111 us
    ppermute x58, waiting for transfers between devices, swap(): return lax.ppermute(value, axis, [(i, i ^ mask) for i in range(size)])  64.9 us
    ppermute x58, starting transfers between devices, swap(): return lax.ppermute(value, axis, [(i, i ^ mask) for i in range(size)])  58.7 us
    convert_element_type x12, other arithmetic, step(): total = total.astype(BF16)  22.3 us
  transfers between devices with their start and end apart: 58, of which 17 were waited for; matrix products, arithmetic and copies ran while one was open for 26% of the time, Pallas kernels for 29%

profile of v3, /device:TPU:0, one launch (start us, length us, event | category | flops | bytes accessed | tf_op | source)
XLA Modules:
  0.0 999.0 jit_solution(6185997233533192951)
XLA Ops:
  10.8 3.9 collective-permute-start.8
  15.2 6.1 reshape.539
  21.3 3.6 convert_reduce_fusion.4
  28.6 6.1 reshape.546
  41.1 3.7 collective-permute-start.17
  50.1 3.5 collective-permute-done.5
  54.9 11.7 %collective-permute-done.6 = bf16[1,64,2048]{2,1,0:T(8,128)(2,1)S(1)} collective-permute-done((bf16[1,64,2048]{2,1,0:T(8,128)(2,1)S(1)}, bf16[1,64,2048]{2,1,0:T(8,128)(2,1)S(1)}, u32[]{:S(2)}, u32[]{:S(2)}) %collective-permute-start.6) | collective-permute-done | bytes 262176 | tf_op jit(solution)/shard_map/ppermute | solution.py:50
  73.4 4.7 collective-permute-done.9
  82.1 8.0 fusion.22
  90.1 12.0 %collective-permute-done.10 = bf16[8,32,2048]{2,1,0:T(8,128)(2,1)S(1)} collective-permute-done((bf16[8,32,2048]{2,1,0:T(8,128)(2,1)S(1)}, bf16[8,32,2048]{2,1,0:T(8,128)(2,1)S(1)}, u32[]{:S(2)}, u32[]{:S(2)}) %collective-permute-start.10) | collective-permute-done | bytes 1048608 | tf_op jit(solution)/shard_map/ppermute | solution.py:50
  104.3 4.1 fusion.8.refs_1_
  112.9 7.4 shard_map.296
  120.3 14.7 %add_convert_fusion.1 = bf16[2816,1536]{1,0:T(8,128)(2,1)} fusion(bf16[2816,1024]{1,0:T(8,128)(2,1)} %fusion.22, bf16[1024,1536]{1,0:T(8,128)(2,1)} %get-tuple-element.62, f32[1536]{0:T(1024)S(1)} %add.453), kind=kOutput, calls=%fused_computation.5 | convolution fusion | flops 8867020800 | bytes 17569792 | tf_op jit(solution)/shard_map/dot_general | solution.py:22
  135.1 11.2 %add_convert_fusion = bf16[2816,1536]{1,0:T(8,128)(2,1)} fusion(bf16[2816,1024]{1,0:T(8,128)(2,1)S(1)} %bitcast.173, bf16[1024,1536]{1,0:T(8,128)(2,1)S(1)} %copy-done.65, f32[1536]{0:T(1024)S(1)} %add.456), kind=kOutput, calls=%fused_computation.4 | convolution fusion | flops 8867020800 | bytes 17569792 | tf_op jit(solution)/shard_map/dot_general | solution.py:22
  148.9 27.6 %shard_map.298 = (bf16[2,1408,1024]{2,1,0:T(8,128)(2,1)}, f32[2,1408,1024]{2,1,0:T(8,128)}) custom-call(s32[1]{0:T(128)} %constant.71.clone.1.ticket_ref, bf16[2,1408,1536]{2,1,0:T(8,128)(2,1)} %bitcast.164, bf16[2,1408,1536]{2,1,0:T(8,128)(2,1)} %bitcast.165, bf16[4,32,4096]{2,1,0:T(8,128)(2,1)} %get-tuple-element.64.rest_0_, ...), custom_call_target="tpu_custom_call" | custom-call | flops 16240345088 | bytes 11534336 | tf_op jit(solution)/shard_map/pallas_call | solution.py:497
  182.2 27.7 %shard_map.300 = (bf16[2,1408,1024]{2,1,0:T(8,128)(2,1)}, f32[2,1408,1024]{2,1,0:T(8,128)}) custom-call(s32[1]{0:T(128)} %constant.71.clone.1.ticket_ref, bf16[2,1408,1536]{2,1,0:T(8,128)(2,1)} %bitcast.166, bf16[2,1408,1536]{2,1,0:T(8,128)(2,1)} %bitcast.167, ...), custom_call_target="tpu_custom_call", output_to_operand_aliasing={{0}: (3, {}), {1}: (4, {})} | custom-call | flops 16240345088 | bytes 11534336 | tf_op jit(solution)/shard_map/pallas_call | solution.py:497
  209.9 27.9 %shard_map.301 = (bf16[2,1408,1024]{2,1,0:T(8,128)(2,1)}, f32[2,1408,1024]{2,1,0:T(8,128)}) custom-call(s32[1]{0:T(128)} %constant.71.clone.1.ticket_ref, bf16[2,1408,1536]{2,1,0:T(8,128)(2,1)} %bitcast.155, bf16[2,1408,1536]{2,1,0:T(8,128)(2,1)} %bitcast.156, ...), custom_call_target="tpu_custom_call", output_to_operand_aliasing={{0}: (3, {}), {1}: (4, {})} | custom-call | flops 16240345088 | bytes 11534336 | tf_op jit(solution)/shard_map/pallas_call | solution.py:497
  243.2 27.6 %shard_map.303 = (bf16[2,1408,1024]{2,1,0:T(8,128)(2,1)}, f32[2,1408,1024]{2,1,0:T(8,128)}) custom-call(s32[1]{0:T(128)} %constant.71.clone.1.ticket_ref, bf16[2,1408,1536]{2,1,0:T(8,128)(2,1)} %bitcast.157, bf16[2,1408,1536]{2,1,0:T(8,128)(2,1)} %bitcast.158, ...), custom_call_target="tpu_custom_call", output_to_operand_aliasing={{0}: (3, {}), {1}: (4, {})} | custom-call | flops 16240345088 | bytes 11534336 | tf_op jit(solution)/shard_map/pallas_call | solution.py:497
  271.3 18.8 %fusion.72 = (f32[2816]{0:T(1024)S(1)}, f32[2816,1024]{1,0:T(8,128)S(1)}, f32[2816,1024]{1,0:T(8,128)}) fusion(f32[1024]{0:T(1024)S(1)} %add.463, f32[1024]{0:T(1024)S(1)} %mul.187, bf16[2,1370,1024]{2,1,0:T(8,128)(2,1)} %reshape.539, bf16[2816,1024]{1,0:T(8,128)(2,1)} %bitcast.150, bf16[1024,1024]{1,0:T(8,128)(2,1)S(1)} %copy-done.66), kind=kOutput, calls=%fused_computation.217 | convolution fusion | flops 5919994880 | bytes 36563968 | tf_op jit(solution)/shard_map/dot_general | solution.py:22
  294.3 4.1 add_convert_fusion.3.refs_0_
  298.4 17.9 %shard_map.304 = (bf16[1024,4096]{1,0:T(8,128)(2,1)}, bf16[1024,4096]{1,0:T(8,128)(2,1)}) custom-call(s32[3,16]{1,0:T(4,128)} %add_add_fusion.1.tables_ref, bf16[16,32,4096]{2,1,0:T(8,128)(2,1)} %get-tuple-element.74.rest_2_.own_a, bf16[16,32,4096]{2,1,0:T(8,128)(2,1)} %collective-permute-done.22.far_a, ...), custom_call_target="tpu_custom_call" | custom-call | tf_op jit(solution)/shard_map/pallas_call | solution.py:115
  317.0 226.7 %shard_map.305 = (bf16[2816,1024]{1,0:T(8,128)(2,1)}, bf16[2816,1024]{1,0:T(8,128)(2,1)}, bf16[1024,4096]{1,0:T(8,128)(2,1)}, bf16[1024,4096]{1,0:T(8,128)(2,1)}, f32[8,4096]{1,0:T(8,128)}) custom-call(bf16[2816,1024]{1,0:T(8,128)(2,1)} %add_convert_fusion.3.refs_0_, bf16[2816,1024]{1,0:T(8,128)(2,1)} %fusion.8.refs_1_, ...), custom_call_target="tpu_custom_call" | custom-call | flops 141733920768 | bytes 56623104 | tf_op jit(solution)/shard_map/pallas_call | solution.py:685
  543.7 9.8 fusion.7
  553.6 18.5 %shard_map.306 = (bf16[16,32,4096]{2,1,0:T(8,128)(2,1)}, bf16[16,32,4096]{2,1,0:T(8,128)(2,1)}, bf16[16,32,4096]{2,1,0:T(8,128)(2,1)}, bf16[16,32,4096]{2,1,0:T(8,128)(2,1)}) custom-call(s32[3,16]{1,0:T(4,128)} %add_add_fusion.1.tables_ref, bf16[1024,4096]{1,0:T(8,128)(2,1)} %get-tuple-element.83.refs_0_, bf16[1024,4096]{1,0:T(8,128)(2,1)} %get-tuple-element.84.refs_1_), custom_call_target="tpu_custom_call" | custom-call | tf_op jit(solution)/shard_map/pallas_call | solution.py:232
  572.1 17.9 %multiply_reduce_fusion = (f32[1024]{0:T(1024)S(1)}, f32[1024]{0:T(1024)S(1)}, f32[2816,1024]{1,0:T(8,128)}, bf16[2816,1024]{1,0:T(8,128)(2,1)S(1)}, f32[1024]{0:T(1024)S(1)}) fusion(f32[2816,1024]{1,0:T(8,128)} %get-tuple-element.188, f32[1024]{0:T(1024)S(1)} %copy-done.60, f32[2816]{0:T(1024)S(1)} %broadcast_multiply_fusion.2, f32[2816,1024]{1,0:T(8,128)} %copy-done, ...), kind=kLoop, calls=%fused_computation.45 | loop fusion | flops 60552192 | bytes 57589760 | tf_op jit(solution)/shard_map/reduce_sum | solution.py:928
  593.0 6.3 reshape.548
  603.3 11.3 %convolution_convert_fusion = bf16[2816,1024]{1,0:T(8,128)(2,1)} fusion(bf16[1024,1024]{1,0:T(8,128)(2,1)} %get-tuple-element.77, f32[2816,1024]{1,0:T(8,128)} %get-tuple-element.127, f32[1024]{0:T(1024)S(1)} %copy-done.64), kind=kOutput, calls=%fused_computation.58 | convolution fusion | flops 5914230784 | bytes 19402752 | tf_op jit(solution)/shard_map/dot_general | solution.py:22
  616.2 9.5 fusion.32.refs_1_
  625.7 3.7 add_convert_fusion.4
  633.2 3.7 add_convert_fusion.5
  640.8 40.5 %shard_map.307.refs_2_.rest_0_ = bf16[2,1408,1536]{2,1,0:T(8,128)(2,1)} custom-call(s32[1]{0:T(128)} %constant.71.clone.1.ticket_ref, bf16[2,1408,1536]{2,1,0:T(8,128)(2,1)} %bitcast.168, bf16[2,1408,1536]{2,1,0:T(8,128)(2,1)} %bitcast.169, bf16[2,1408,1024]{2,1,0:T(8,128)(2,1)} %get-tuple-element.76.mixed_ref, bf16[2,1408,1024]{2,1,0:T(8,128)(2,1)} %bitcast.190, ...), custom_call_target="tpu_custom_call" | custom-call | flops 40600862720 | bytes 11534336 | tf_op jit(solution)/shard_map/pallas_call | solution.py:547
  691.5 40.7 %shard_map.309.refs_2_ = bf16[2,1408,1536]{2,1,0:T(8,128)(2,1)} custom-call(s32[1]{0:T(128)} %constant.71.clone.1.ticket_ref, bf16[2,1408,1536]{2,1,0:T(8,128)(2,1)} %bitcast.170, bf16[2,1408,1536]{2,1,0:T(8,128)(2,1)} %bitcast.171, bf16[2,1408,1024]{2,1,0:T(8,128)(2,1)} %get-tuple-element.76.mixed_ref, ...), custom_call_target="tpu_custom_call", output_to_operand_aliasing={{}: (6, {})} | custom-call | flops 40600862720 | bytes 11534336 | tf_op jit(solution)/shard_map/pallas_call | solution.py:547
  732.8 15.6 %fusion.89.rest_8_.rest_6_ = f32[2816,1024]{1,0:T(8,128)} fusion(bf16[2816,1536]{1,0:T(8,128)(2,1)} %bitcast.147, bf16[1024,1536]{1,0:T(8,128)(2,1)} %get-tuple-element.63), kind=kOutput, calls=%fused_computation.234 | convolution fusion | flops 8858370048 | bytes 23330816 | tf_op jit(solution)/shard_map/dot_general | solution.py:22
  748.5 11.0 %bitcast_convert_fusion.1.refs_0_ = bf16[1024,1536]{1,0:T(8,128)(2,1)} fusion(bf16[2,1408,1536]{2,1,0:T(8,128)(2,1)S(1)} %copy-done.4, f32[1024]{0:T(1024)S(1)} %copy-done.58, f32[1024]{0:T(1024)S(1)} %copy-done.49, f32[2,1408]{1,0:T(2,128)S(1)} %copy-done.45, f32[2,1408]{1,0:T(2,128)S(1)} %copy-done.40, bf16[2,1370,1024]{2,1,0:T(8,128)(2,1)S(1)} %bitcast.141), kind=kOutput, calls=%fused_computation.56 | convolution fusion | flops 8877244416 | bytes 17438720 | tf_op jit(solution)/shard_map/dot_general | solution.py:22
  759.4 5.4 shard_map.311
  765.4 4.7 convert_reduce_fusion.1
  774.3 4.3 collective-permute-start.32
  779.1 40.6 %shard_map.312.refs_3_.rest_0_ = bf16[2,1408,1536]{2,1,0:T(8,128)(2,1)} custom-call(s32[1]{0:T(128)} %constant.71.clone.1.ticket_ref, bf16[2,1408,1536]{2,1,0:T(8,128)(2,1)} %bitcast.159, bf16[2,1408,1536]{2,1,0:T(8,128)(2,1)} %bitcast.160, bf16[2,1408,1024]{2,1,0:T(8,128)(2,1)} %get-tuple-element.76.mixed_ref, bf16[2,1408,1024]{2,1,0:T(8,128)(2,1)} %bitcast.192, ...), custom_call_target="tpu_custom_call" | custom-call | flops 40600862720 | bytes 11534336 | tf_op jit(solution)/shard_map/pallas_call | solution.py:547
  829.1 40.7 %shard_map.314.refs_2_ = bf16[2,1408,1536]{2,1,0:T(8,128)(2,1)} custom-call(s32[1]{0:T(128)} %constant.71.clone.1.ticket_ref, bf16[2,1408,1536]{2,1,0:T(8,128)(2,1)} %bitcast.161, bf16[2,1408,1536]{2,1,0:T(8,128)(2,1)} %bitcast.162, bf16[2,1408,1024]{2,1,0:T(8,128)(2,1)} %get-tuple-element.76.mixed_ref, ...), custom_call_target="tpu_custom_call", output_to_operand_aliasing={{}: (6, {})} | custom-call | flops 40600862720 | bytes 11534336 | tf_op jit(solution)/shard_map/pallas_call | solution.py:547
  869.9 15.0 %bitcast_convert_fusion.refs_0_ = bf16[1024,1536]{1,0:T(8,128)(2,1)} fusion(bf16[2,1408,1536]{2,1,0:T(8,128)(2,1)} %shard_map.314.refs_2_, f32[1024]{0:T(1024)S(1)} %copy-done.58, f32[1024]{0:T(1024)S(1)} %copy-done.49, f32[2,1408]{1,0:T(2,128)S(1)} %copy-done.45, f32[2,1408]{1,0:T(2,128)S(1)} %copy-done.40, bf16[2,1370,1024]{2,1,0:T(8,128)(2,1)S(1)} %bitcast.143), kind=kOutput, calls=%fused_computation.55 | convolution fusion | flops 8877244416 | bytes 17438720 | tf_op jit(solution)/shard_map/dot_general | solution.py:22
  886.8 3.9 shard_map.315
  896.7 6.8 collective-permute-done.45
  905.9 3.7 collective-permute-start.50
  916.1 21.0 %fusion.28 = (f32[1024]{0:T(1024)S(1)}, f32[2816]{0:T(1024)S(1)}, f32[2816]{0:T(1024)S(1)}, f32[1024]{0:T(1024)S(1)}, f32[2816,1024]{1,0:T(8,128)}) fusion(f32[2816]{0:T(1024)S(1)} %copy-done.38, f32[2816]{0:T(1024)S(1)} %copy-done.36, bf16[2,1370,1024]{2,1,0:T(8,128)(2,1)} %reshape.539, f32[1024]{0:T(1024)S(1)} %add_add_fusion, ...), kind=kOutput, calls=%fused_computation.44 | convolution fusion | flops 8890081280 | bytes 40534016 | tf_op jit(solution)/shard_map/dot_general | solution.py:22
  939.4 3.8 collective-permute-done.37
  945.2 10.6 %fusion.27 = bf16[2816,1024]{1,0:T(8,128)(2,1)S(1)} fusion(f32[2816,1024]{1,0:T(8,128)} %get-tuple-element.127, f32[2816,1024]{1,0:T(8,128)} %get-tuple-element.189, f32[2816]{0:T(1024)S(1)} %broadcast_multiply_fusion, f32[2816]{0:T(1024)S(1)} %broadcast_multiply_fusion.1, f32[1024]{0:T(1024)S(1)} %add_add_fusion, f32[2816]{0:T(1024)S(1)} %copy-done.38, ...), kind=kLoop, calls=%fused_computation.43 | loop fusion | flops 28835840 | bytes 34496512 | tf_op jit(solution)/shard_map/convert_element_type | solution.py:906
  959.0 6.2 reshape.553
  971.3 4.9 collective-permute-done.48
  (423 shorter events, 153.5 us)
Async XLA Ops:
  2.9 37.6 %collective-permute-start = (f32[1,16,128]{2,1,0:T(8,128)S(1)}, f32[1,16,128]{2,1,0:T(8,128)S(1)}, u32[]{:S(2)}, u32[]{:S(2)}) collective-permute-start(f32[1,16,128]{2,1,0:T(8,128)S(1)} %bitcast_convert_fusion.2), channel_id=1, source_target_pairs={{0,8},{2,10},{4,12},{6,14},{8,0},{10,2},{12,4},{14,6},{16,24},{18,... | collective-permute-start | bytes 24584 | tf_op jit(solution)/shard_map/ppermute | solution.py:50
  6.0 35.1 %collective-permute-start.1 = (f32[1,16,128]{2,1,0:T(8,128)S(1)}, f32[1,16,128]{2,1,0:T(8,128)S(1)}, u32[]{:S(2)}, u32[]{:S(2)}) collective-permute-start(f32[1,16,128]{2,1,0:T(8,128)S(1)} %bitcast_convert_fusion.2), channel_id=1, source_target_pairs={{0,16},{2,18},{4,20},{6,22},{8,24},{10,26},{12,28},{14,30},{16,0},... | collective-permute-start | bytes 24584 | tf_op jit(solution)/shard_map/ppermute | solution.py:50
  8.6 36.3 %collective-permute-start.2 = (f32[1,16,128]{2,1,0:T(8,128)S(1)}, f32[1,16,128]{2,1,0:T(8,128)S(1)}, u32[]{:S(2)}, u32[]{:S(2)}) collective-permute-start(f32[1,16,128]{2,1,0:T(8,128)S(1)} %bitcast_convert_fusion.2), channel_id=1, source_target_pairs={{0,24},{2,26},{4,28},{6,30},{8,16},{10,18},{12,20},{14,22},{16,8},... | collective-permute-start | bytes 24584 | tf_op jit(solution)/shard_map/ppermute | solution.py:50
  10.8 43.5 %collective-permute-start.8 = (bf16[1,64,2048]{2,1,0:T(8,128)(2,1)S(1)}, bf16[1,64,2048]{2,1,0:T(8,128)(2,1)S(1)}, u32[]{:S(2)}, u32[]{:S(2)}) collective-permute-start(bf16[1,64,2048]{2,1,0:T(8,128)(2,1)S(1)} %maximum_bitcast_fusion.1), channel_id=1, source_target_pairs={{0,24},{2,26},{4,28},{6,30},{8,16},{10,18},{12,20},{14,22},{16,8},... | collective-permute-start | bytes 786440 | tf_op jit(solution)/shard_map/ppermute | solution.py:50
  14.6 40.2 %collective-permute-start.7 = (bf16[1,64,2048]{2,1,0:T(8,128)(2,1)S(1)}, bf16[1,64,2048]{2,1,0:T(8,128)(2,1)S(1)}, u32[]{:S(2)}, u32[]{:S(2)}) collective-permute-start(bf16[1,64,2048]{2,1,0:T(8,128)(2,1)S(1)} %maximum_bitcast_fusion.1), channel_id=1, source_target_pairs={{0,8},{2,10},{4,12},{6,14},{8,0},{10,2},{12,4},{14,6},{16,24},{18,... | collective-permute-start | bytes 786440 | tf_op jit(solution)/shard_map/ppermute | solution.py:50
  40.5 26.1 %collective-permute-start.6 = (bf16[1,64,2048]{2,1,0:T(8,128)(2,1)S(1)}, bf16[1,64,2048]{2,1,0:T(8,128)(2,1)S(1)}, u32[]{:S(2)}, u32[]{:S(2)}) collective-permute-start(bf16[1,64,2048]{2,1,0:T(8,128)(2,1)S(1)} %maximum_bitcast_fusion.1), channel_id=1, source_target_pairs={{0,16},{2,18},{4,20},{6,22},{8,24},{10,26},{12,28},{14,30},{16,0},... | collective-permute-start | bytes 786440 | tf_op jit(solution)/shard_map/ppermute | solution.py:50
  41.1 67.4 %collective-permute-start.17 = (bf16[1,64,4096]{2,1,0:T(8,128)(2,1)S(1)}, bf16[1,64,4096]{2,1,0:T(8,128)(2,1)}, u32[]{:S(2)}, u32[]{:S(2)}) collective-permute-start(bf16[1,64,4096]{2,1,0:T(8,128)(2,1)S(1)} %fusion.38), channel_id=1, source_target_pairs={{0,24},{2,26},{4,28},{6,30},{8,16},{10,18},{12,20},{14,22},{16,8},... | collective-permute-start | bytes 1572872 | tf_op jit(solution)/shard_map/ppermute | solution.py:50
  53.6 54.8 %collective-permute-start.16 = (bf16[1,64,4096]{2,1,0:T(8,128)(2,1)S(1)}, bf16[1,64,4096]{2,1,0:T(8,128)(2,1)}, u32[]{:S(2)}, u32[]{:S(2)}) collective-permute-start(bf16[1,64,4096]{2,1,0:T(8,128)(2,1)S(1)} %fusion.38), channel_id=1, source_target_pairs={{0,8},{2,10},{4,12},{6,14},{8,0},{10,2},{12,4},{14,6},{16,24},{18,... | collective-permute-start | bytes 1572872 | tf_op jit(solution)/shard_map/ppermute | solution.py:50
  54.2 54.2 %collective-permute-start.15 = (bf16[1,64,4096]{2,1,0:T(8,128)(2,1)S(1)}, bf16[1,64,4096]{2,1,0:T(8,128)(2,1)}, u32[]{:S(2)}, u32[]{:S(2)}) collective-permute-start(bf16[1,64,4096]{2,1,0:T(8,128)(2,1)S(1)} %fusion.38), channel_id=1, source_target_pairs={{0,16},{2,18},{4,20},{6,22},{8,24},{10,26},{12,28},{14,30},{16,0},... | collective-permute-start | bytes 1572872 | tf_op jit(solution)/shard_map/ppermute | solution.py:50
  66.8 11.3 %collective-permute-start.9 = (bf16[4,32,2048]{2,1,0:T(8,128)(2,1)S(1)}, bf16[4,32,2048]{2,1,0:T(8,128)(2,1)S(1)}, u32[]{:S(2)}, u32[]{:S(2)}) collective-permute-start(bf16[4,32,2048]{2,1,0:T(8,128)(2,1)S(1)} %get-tuple-element.153), channel_id=1, source_target_pairs={{0,4},{2,6},{4,0},{6,2},{8,12},{10,14},{12,8},{14,10},{16,20},{18,... | collective-permute-start | bytes 1572872 | tf_op jit(solution)/shard_map/ppermute | solution.py:50
  68.7 13.1 %collective-permute-start.12 = (bf16[4,32,2048]{2,1,0:T(8,128)(2,1)S(1)}, bf16[4,32,2048]{2,1,0:T(8,128)(2,1)S(1)}, u32[]{:S(2)}, u32[]{:S(2)}) collective-permute-start(bf16[4,32,2048]{2,1,0:T(8,128)(2,1)S(1)} %get-tuple-element.152), channel_id=1, source_target_pairs={{0,1},{1,0},{2,3},{3,2},{4,5},{5,4},{6,7},{7,6},{8,9},{9,8},{10,11... | collective-permute-start | bytes 1572872 | tf_op jit(solution)/shard_map/ppermute | solution.py:50
  78.2 24.0 %collective-permute-start.10 = (bf16[8,32,2048]{2,1,0:T(8,128)(2,1)S(1)}, bf16[8,32,2048]{2,1,0:T(8,128)(2,1)S(1)}, u32[]{:S(2)}, u32[]{:S(2)}) collective-permute-start(bf16[8,32,2048]{2,1,0:T(8,128)(2,1)S(1)} %pad_maximum_fusion.8), channel_id=1, source_target_pairs={{0,1},{1,0},{2,3},{3,2},{4,5},{5,4},{6,7},{7,6},{8,9},{9,8},{10,11... | collective-permute-start | bytes 3145736 | tf_op jit(solution)/shard_map/ppermute | solution.py:50
  82.0 20.5 %collective-permute-start.13 = (bf16[8,32,2048]{2,1,0:T(8,128)(2,1)S(1)}, bf16[8,32,2048]{2,1,0:T(8,128)(2,1)S(1)}, u32[]{:S(2)}, u32[]{:S(2)}) collective-permute-start(bf16[8,32,2048]{2,1,0:T(8,128)(2,1)S(1)} %pad_maximum_fusion.9), channel_id=1, source_target_pairs={{0,4},{2,6},{4,0},{6,2},{8,12},{10,14},{12,8},{14,10},{16,20},{18,... | collective-permute-start | bytes 3145736 | tf_op jit(solution)/shard_map/ppermute | solution.py:50
  102.4 9.2 collective-permute-start.11
  104.2 7.4 collective-permute-start.14
  146.8 29.7 %collective-permute-start.18 = (bf16[4,32,4096]{2,1,0:T(8,128)(2,1)}, bf16[4,32,4096]{2,1,0:T(8,128)(2,1)S(1)}, u32[]{:S(2)}, u32[]{:S(2)}) collective-permute-start(bf16[4,32,4096]{2,1,0:T(8,128)(2,1)} %get-tuple-element.64.rest_0_), channel_id=1, source_target_pairs={{0,4},{2,6},{4,0},{6,2},{8,12},{10,14},{12,8},{14,10},{16,20},{18,... | collective-permute-start | bytes 3145736 | tf_op jit(solution)/shard_map/ppermute | solution.py:50
  147.4 30.7 %collective-permute-start.19 = (bf16[4,32,4096]{2,1,0:T(8,128)(2,1)}, bf16[4,32,4096]{2,1,0:T(8,128)(2,1)S(1)}, u32[]{:S(2)}, u32[]{:S(2)}) collective-permute-start(bf16[4,32,4096]{2,1,0:T(8,128)(2,1)} %get-tuple-element.65.rest_1_), channel_id=1, source_target_pairs={{0,1},{1,0},{2,3},{3,2},{4,5},{5,4},{6,7},{7,6},{8,9},{9,8},{10,11... | collective-permute-start | bytes 3145736 | tf_op jit(solution)/shard_map/ppermute | solution.py:50
  180.1 57.7 %collective-permute-start.20 = (bf16[8,32,4096]{2,1,0:T(8,128)(2,1)}, bf16[8,32,4096]{2,1,0:T(8,128)(2,1)S(1)}, u32[]{:S(2)}, u32[]{:S(2)}) collective-permute-start(bf16[8,32,4096]{2,1,0:T(8,128)(2,1)} %get-tuple-element.68.rest_2_), channel_id=1, source_target_pairs={{0,1},{1,0},{2,3},{3,2},{4,5},{5,4},{6,7},{7,6},{8,9},{9,8},{10,11... | collective-permute-start | bytes 6291464 | tf_op jit(solution)/shard_map/ppermute | solution.py:50
  180.7 59.6 %collective-permute-start.21 = (bf16[8,32,4096]{2,1,0:T(8,128)(2,1)}, bf16[8,32,4096]{2,1,0:T(8,128)(2,1)S(1)}, u32[]{:S(2)}, u32[]{:S(2)}) collective-permute-start(bf16[8,32,4096]{2,1,0:T(8,128)(2,1)} %get-tuple-element.69.rest_3_), channel_id=1, source_target_pairs={{0,4},{2,6},{4,0},{6,2},{8,12},{10,14},{12,8},{14,10},{16,20},{18,... | collective-permute-start | bytes 6291464 | tf_op jit(solution)/shard_map/ppermute | solution.py:50
  243.2 55.2 %collective-permute-start.22 = (bf16[16,32,4096]{2,1,0:T(8,128)(2,1)}, bf16[16,32,4096]{2,1,0:T(8,128)(2,1)}, u32[]{:S(2)}, u32[]{:S(2)}) collective-permute-start(bf16[16,32,4096]{2,1,0:T(8,128)(2,1)} %get-tuple-element.74.rest_2_.own_a), channel_id=1, source_target_pairs={{0,2},{2,0},{4,6},{6,4},{8,10},{10,8},{12,14},{14,12},{16,18},{18,... | collective-permute-start | bytes 12582920 | tf_op jit(solution)/shard_map/ppermute | solution.py:50
  270.8 27.6 %collective-permute-start.23 = (bf16[16,32,4096]{2,1,0:T(8,128)(2,1)}, bf16[16,32,4096]{2,1,0:T(8,128)(2,1)}, u32[]{:S(2)}, u32[]{:S(2)}) collective-permute-start(bf16[16,32,4096]{2,1,0:T(8,128)(2,1)} %get-tuple-element.75.rest_3_.own_b), channel_id=1, source_target_pairs={{0,2},{2,0},{4,6},{6,4},{8,10},{10,8},{12,14},{14,12},{16,18},{18,... | collective-permute-start | bytes 12582920 | tf_op jit(solution)/shard_map/ppermute | solution.py:50
  572.1 53.7 %collective-permute-start.25 = (bf16[16,32,4096]{2,1,0:T(8,128)(2,1)}, bf16[16,32,4096]{2,1,0:T(8,128)(2,1)}, u32[]{:S(2)}, u32[]{:S(2)}) collective-permute-start(bf16[16,32,4096]{2,1,0:T(8,128)(2,1)} %get-tuple-element.88), channel_id=1, source_target_pairs={{0,2},{2,0},{4,6},{6,4},{8,10},{10,8},{12,14},{14,12},{16,18},{18,... | collective-permute-start | bytes 12582920 | tf_op jit(solution)/shard_map/ppermute | solution.py:50
  599.4 33.1 %collective-permute-start.24 = (bf16[16,32,4096]{2,1,0:T(8,128)(2,1)}, bf16[16,32,4096]{2,1,0:T(8,128)(2,1)}, u32[]{:S(2)}, u32[]{:S(2)}) collective-permute-start(bf16[16,32,4096]{2,1,0:T(8,128)(2,1)} %get-tuple-element.86), channel_id=1, source_target_pairs={{0,2},{2,0},{4,6},{6,4},{8,10},{10,8},{12,14},{14,12},{16,18},{18,... | collective-permute-start | bytes 12582920 | tf_op jit(solution)/shard_map/ppermute | solution.py:50
  631.9 49.9 %collective-permute-start.27 = (bf16[8,32,4096]{2,1,0:T(8,128)(2,1)}, bf16[8,32,4096]{2,1,0:T(8,128)(2,1)S(1)}, u32[]{:S(2)}, u32[]{:S(2)}) collective-permute-start(bf16[8,32,4096]{2,1,0:T(8,128)(2,1)} %get-tuple-element.132.rest_3_), channel_id=1, source_target_pairs={{0,4},{2,6},{4,0},{6,2},{8,12},{10,14},{12,8},{14,10},{16,20},{18,... | collective-permute-start | bytes 6291464 | tf_op jit(solution)/shard_map/ppermute | solution.py:50
  639.2 47.9 %collective-permute-start.26 = (bf16[8,32,4096]{2,1,0:T(8,128)(2,1)}, bf16[8,32,4096]{2,1,0:T(8,128)(2,1)}, u32[]{:S(2)}, u32[]{:S(2)}) collective-permute-start(bf16[8,32,4096]{2,1,0:T(8,128)(2,1)} %get-tuple-element.134.rest_2_), channel_id=1, source_target_pairs={{0,1},{1,0},{2,3},{3,2},{4,5},{5,4},{6,7},{7,6},{8,9},{9,8},{10,11... | collective-permute-start | bytes 6291464 | tf_op jit(solution)/shard_map/ppermute | solution.py:50
  685.8 84.3 %collective-permute-start.29 = (bf16[4,32,4096]{2,1,0:T(8,128)(2,1)}, bf16[4,32,4096]{2,1,0:T(8,128)(2,1)}, u32[]{:S(2)}, u32[]{:S(2)}) collective-permute-start(bf16[4,32,4096]{2,1,0:T(8,128)(2,1)} %get-tuple-element.140.rest_4_), channel_id=1, source_target_pairs={{0,1},{1,0},{2,3},{3,2},{4,5},{5,4},{6,7},{7,6},{8,9},{9,8},{10,11... | collective-permute-start | bytes 3145736 | tf_op jit(solution)/shard_map/ppermute | solution.py:50
  690.9 80.7 %collective-permute-start.28 = (bf16[4,32,4096]{2,1,0:T(8,128)(2,1)}, bf16[4,32,4096]{2,1,0:T(8,128)(2,1)}, u32[]{:S(2)}, u32[]{:S(2)}) collective-permute-start(bf16[4,32,4096]{2,1,0:T(8,128)(2,1)} %get-tuple-element.142.rest_3_), channel_id=1, source_target_pairs={{0,4},{2,6},{4,0},{6,2},{8,12},{10,14},{12,8},{14,10},{16,20},{18,... | collective-permute-start | bytes 3145736 | tf_op jit(solution)/shard_map/ppermute | solution.py:50
  764.9 55.5 %collective-permute-start.33 = (bf16[16,32,1280]{2,1,0:T(8,128)(2,1)}, bf16[16,32,1280]{2,1,0:T(8,128)(2,1)}, u32[]{:S(2)}, u32[]{:S(2)}) collective-permute-start(bf16[16,32,1280]{2,1,0:T(8,128)(2,1)} %get-tuple-element.95.rest_6_), channel_id=1, source_target_pairs={{0,2},{2,0},{4,6},{6,4},{8,10},{10,8},{12,14},{14,12},{16,18},{18,... | collective-permute-start | bytes 3932168 | tf_op jit(solution)/shard_map/ppermute | solution.py:50
  764.9 59.9 %collective-permute-start.34 = (bf16[16,32,1280]{2,1,0:T(8,128)(2,1)}, bf16[16,32,1280]{2,1,0:T(8,128)(2,1)S(1)}, u32[]{:S(2)}, u32[]{:S(2)}) collective-permute-start(bf16[16,32,1280]{2,1,0:T(8,128)(2,1)} %get-tuple-element.96.rest_7_), channel_id=1, source_target_pairs={{0,2},{2,0},{4,6},{6,4},{8,10},{10,8},{12,14},{14,12},{16,18},{18,... | collective-permute-start | bytes 3932168 | tf_op jit(solution)/shard_map/ppermute | solution.py:50
  774.3 53.6 %collective-permute-start.32 = (bf16[1,64,4096]{2,1,0:T(8,128)(2,1)}, bf16[1,64,4096]{2,1,0:T(8,128)(2,1)S(1)}, u32[]{:S(2)}, u32[]{:S(2)}) collective-permute-start(bf16[1,64,4096]{2,1,0:T(8,128)(2,1)} %get-tuple-element.136.rest_3_), channel_id=1, source_target_pairs={{0,24},{2,26},{4,28},{6,30},{8,16},{10,18},{12,20},{14,22},{16,8},... | collective-permute-start | bytes 1572872 | tf_op jit(solution)/shard_map/ppermute | solution.py:50
  778.6 49.3 %collective-permute-start.31 = (bf16[1,64,4096]{2,1,0:T(8,128)(2,1)}, bf16[1,64,4096]{2,1,0:T(8,128)(2,1)S(1)}, u32[]{:S(2)}, u32[]{:S(2)}) collective-permute-start(bf16[1,64,4096]{2,1,0:T(8,128)(2,1)} %get-tuple-element.139.rest_2_), channel_id=1, source_target_pairs={{0,8},{2,10},{4,12},{6,14},{8,0},{10,2},{12,4},{14,6},{16,24},{18,... | collective-permute-start | bytes 1572872 | tf_op jit(solution)/shard_map/ppermute | solution.py:50
  778.6 49.3 %collective-permute-start.30 = (bf16[1,64,4096]{2,1,0:T(8,128)(2,1)S(1)}, bf16[1,64,4096]{2,1,0:T(8,128)(2,1)S(1)}, u32[]{:S(2)}, u32[]{:S(2)}) collective-permute-start(bf16[1,64,4096]{2,1,0:T(8,128)(2,1)S(1)} %get-tuple-element.138.rest_1_), channel_id=1, source_target_pairs={{0,16},{2,18},{4,20},{6,22},{8,24},{10,26},{12,28},{14,30},{16,0},... | collective-permute-start | bytes 1572872 | tf_op jit(solution)/shard_map/ppermute | solution.py:50
  823.7 68.8 %collective-permute-start.44 = (bf16[8,32,1280]{2,1,0:T(8,128)(2,1)}, bf16[8,32,1280]{2,1,0:T(8,128)(2,1)}, u32[]{:S(2)}, u32[]{:S(2)}) collective-permute-start(bf16[8,32,1280]{2,1,0:T(8,128)(2,1)} %get-tuple-element.148.rest_4_), channel_id=1, source_target_pairs={{0,1},{1,0},{2,3},{3,2},{4,5},{5,4},{6,7},{7,6},{8,9},{9,8},{10,11... | collective-permute-start | bytes 1966088 | tf_op jit(solution)/shard_map/ppermute | solution.py:50
  826.3 68.1 %collective-permute-start.46 = (bf16[8,32,1280]{2,1,0:T(8,128)(2,1)}, bf16[8,32,1280]{2,1,0:T(8,128)(2,1)}, u32[]{:S(2)}, u32[]{:S(2)}) collective-permute-start(bf16[8,32,1280]{2,1,0:T(8,128)(2,1)} %get-tuple-element.146.rest_5_), channel_id=1, source_target_pairs={{0,4},{2,6},{4,0},{6,2},{8,12},{10,14},{12,8},{14,10},{16,20},{18,... | collective-permute-start | bytes 1966088 | tf_op jit(solution)/shard_map/ppermute | solution.py:50
  890.7 18.9 %collective-permute-start.36 = (bf16[16,32,768]{2,1,0:T(8,128)(2,1)}, bf16[16,32,768]{2,1,0:T(8,128)(2,1)}, u32[]{:S(2)}, u32[]{:S(2)}) collective-permute-start(bf16[16,32,768]{2,1,0:T(8,128)(2,1)} %get-tuple-element.103), channel_id=1, source_target_pairs={{0,2},{2,0},{4,6},{6,4},{8,10},{10,8},{12,14},{14,12},{16,18},{18,... | collective-permute-start | bytes 2359304 | tf_op jit(solution)/shard_map/ppermute | solution.py:50
  890.7 21.4 %collective-permute-start.35 = (bf16[16,32,768]{2,1,0:T(8,128)(2,1)}, bf16[16,32,768]{2,1,0:T(8,128)(2,1)}, u32[]{:S(2)}, u32[]{:S(2)}) collective-permute-start(bf16[16,32,768]{2,1,0:T(8,128)(2,1)} %get-tuple-element.101), channel_id=1, source_target_pairs={{0,2},{2,0},{4,6},{6,4},{8,10},{10,8},{12,14},{14,12},{16,18},{18,... | collective-permute-start | bytes 2359304 | tf_op jit(solution)/shard_map/ppermute | solution.py:50
  893.9 9.7 collective-permute-start.45
  895.7 9.4 collective-permute-start.47
  905.9 62.0 %collective-permute-start.50 = (bf16[1,64,1280]{2,1,0:T(8,128)(2,1)}, bf16[1,64,1280]{2,1,0:T(8,128)(2,1)}, u32[]{:S(2)}, u32[]{:S(2)}) collective-permute-start(bf16[1,64,1280]{2,1,0:T(8,128)(2,1)} %get-tuple-element.159), channel_id=1, source_target_pairs={{0,24},{2,26},{4,28},{6,30},{8,16},{10,18},{12,20},{14,22},{16,8},... | collective-permute-start | bytes 491528 | tf_op jit(solution)/shard_map/ppermute | solution.py:50
  909.6 61.7 %collective-permute-start.49 = (bf16[1,64,1280]{2,1,0:T(8,128)(2,1)}, bf16[1,64,1280]{2,1,0:T(8,128)(2,1)}, u32[]{:S(2)}, u32[]{:S(2)}) collective-permute-start(bf16[1,64,1280]{2,1,0:T(8,128)(2,1)} %get-tuple-element.160), channel_id=1, source_target_pairs={{0,8},{2,10},{4,12},{6,14},{8,0},{10,2},{12,4},{14,6},{16,24},{18,... | collective-permute-start | bytes 491528 | tf_op jit(solution)/shard_map/ppermute | solution.py:50
  943.3 21.9 %collective-permute-start.40 = (f32[4,16,128]{2,1,0:T(8,128)S(1)}, f32[4,16,128]{2,1,0:T(8,128)S(1)}, u32[]{:S(2)}, u32[]{:S(2)}) collective-permute-start(f32[4,16,128]{2,1,0:T(8,128)S(1)} %get-tuple-element.167), channel_id=1, source_target_pairs={{0,6},{2,4},{4,2},{6,0},{8,14},{10,12},{12,10},{14,8},{16,22},{18,... | collective-permute-start | bytes 98312 | tf_op jit(solution)/shard_map/ppermute | solution.py:50
  943.3 22.5 %collective-permute-start.39 = (f32[4,16,128]{2,1,0:T(8,128)S(1)}, f32[4,16,128]{2,1,0:T(8,128)S(1)}, u32[]{:S(2)}, u32[]{:S(2)}) collective-permute-start(f32[4,16,128]{2,1,0:T(8,128)S(1)} %get-tuple-element.168), channel_id=1, source_target_pairs={{0,4},{2,6},{4,0},{6,2},{8,12},{10,14},{12,8},{14,10},{16,20},{18,... | collective-permute-start | bytes 98312 | tf_op jit(solution)/shard_map/ppermute | solution.py:50
  944.5 22.4 %collective-permute-start.38 = (f32[4,16,128]{2,1,0:T(8,128)S(1)}, f32[4,16,128]{2,1,0:T(8,128)S(1)}, u32[]{:S(2)}, u32[]{:S(2)}) collective-permute-start(f32[4,16,128]{2,1,0:T(8,128)S(1)} %get-tuple-element.166), channel_id=1, source_target_pairs={{0,2},{2,0},{4,6},{6,4},{8,10},{10,8},{12,14},{14,12},{16,18},{18,... | collective-permute-start | bytes 98312 | tf_op jit(solution)/shard_map/ppermute | solution.py:50
  965.1 11.0 %collective-permute-start.48 = (bf16[1,64,1280]{2,1,0:T(8,128)(2,1)S(1)}, bf16[1,64,1280]{2,1,0:T(8,128)(2,1)S(1)}, u32[]{:S(2)}, u32[]{:S(2)}) collective-permute-start(bf16[1,64,1280]{2,1,0:T(8,128)(2,1)S(1)} %get-tuple-element.158), channel_id=1, source_target_pairs={{0,16},{2,18},{4,20},{6,22},{8,24},{10,26},{12,28},{14,30},{16,0},... | collective-permute-start | bytes 491528 | tf_op jit(solution)/shard_map/ppermute | solution.py:50
  965.8 14.0 %collective-permute-start.51 = (bf16[8,32,768]{2,1,0:T(8,128)(2,1)S(1)}, bf16[8,32,768]{2,1,0:T(8,128)(2,1)}, u32[]{:S(2)}, u32[]{:S(2)}) collective-permute-start(bf16[8,32,768]{2,1,0:T(8,128)(2,1)S(1)} %slice.423), channel_id=1, source_target_pairs={{0,1},{1,0},{2,3},{3,2},{4,5},{5,4},{6,7},{7,6},{8,9},{9,8},{10,11... | collective-permute-start | bytes 1179656 | tf_op jit(solution)/shard_map/ppermute | solution.py:50
  966.8 15.2 %collective-permute-start.53 = (bf16[8,32,768]{2,1,0:T(8,128)(2,1)S(1)}, bf16[8,32,768]{2,1,0:T(8,128)(2,1)}, u32[]{:S(2)}, u32[]{:S(2)}) collective-permute-start(bf16[8,32,768]{2,1,0:T(8,128)(2,1)S(1)} %slice.427), channel_id=1, source_target_pairs={{0,4},{2,6},{4,0},{6,2},{8,12},{10,14},{12,8},{14,10},{16,20},{18,... | collective-permute-start | bytes 1179656 | tf_op jit(solution)/shard_map/ppermute | solution.py:50
  967.9 10.1 %collective-permute-start.43 = (f32[1,16,128]{2,1,0:T(8,128)S(1)}, f32[1,16,128]{2,1,0:T(8,128)S(1)}, u32[]{:S(2)}, u32[]{:S(2)}) collective-permute-start(f32[1,16,128]{2,1,0:T(8,128)S(1)} %get-tuple-element.172), channel_id=1, source_target_pairs={{0,24},{2,26},{4,28},{6,30},{8,16},{10,18},{12,20},{14,22},{16,8},... | collective-permute-start | bytes 24584 | tf_op jit(solution)/shard_map/ppermute | solution.py:50
  971.3 6.8 collective-permute-start.42
  (88 other events, 2331.3 us)

commit v4 on v3

--- a/solution.py
+++ b/solution.py
@@ -628,11 +628,20 @@
 
     def tiles(first):
         total = None
+        here = pl.ds(0, tile)
+        ahead = (dot(normed_ref[here, :], expand, 1, 0), dot(back_ref[here, :], reduce, 1, 0))
         for base in range(0, rows, tile):
             here = pl.ds(base, tile)
-            active, slope = gelu_parts(dot(normed_ref[here, :], expand, 1, 0) + bias)
+            forward, backward = ahead
+            if base + tile < rows:
+                coming = pl.ds(base + tile, tile)
+                ahead = (
+                    dot(normed_ref[coming, :], expand, 1, 0),
+                    dot(back_ref[coming, :], reduce, 1, 0),
+                )
+            active, slope = gelu_parts(forward + bias)
             active = active.astype(BF16)
-            gate = dot(back_ref[here, :], reduce, 1, 0) * slope
+            gate = backward * slope
             part = jnp.sum(gate.reshape(tile // 8, 8, gate.shape[1]), axis=0)
             total = part if total is None else total + part
             gate = gate.astype(BF16)

time: 1010 us -> 1030 us (1.020)
  Pallas kernels: 557 us -> 578 us
    pallas_call x1, Pallas kernels: 227 us -> 247 us  [feed_forward(): pl.pallas_call(functools.partial(feed_kernel, tile), grid=(hidden // bloc...]
  transfers between devices with their start and end apart: 58 -> 58, of which waited for: 17 -> 17; matrix products, arithmetic and copies ran while one was open for 26% -> 26% of each run, Pallas kernels for 29% -> 28%
where the time goes in v4:
time: 1030 us; the launch traced here: 1020 us
  Pallas kernels  578 us (56%)
  matrix products  128 us (12%)
  other arithmetic  116 us (11%)
  local copies, waits for them, and re-layouts  67.8 us (7%)
  waiting for transfers between devices  64.9 us (6%)
  starting transfers between devices  58.7 us (6%)
    pallas_call x1, Pallas kernels, feed_forward(): pl.pallas_call(functools.partial(feed_kernel, tile), grid=(hidden // bloc...  247 us
    pallas_call x4, Pallas kernels, attend_backward(): pl.pallas_call(functools.partial(attend_backward_kernel, segment, valid,...  163 us
    dot_general x9, matrix products, dot(): return lax.dot_general(left, right, dims, preferred_element_type=F32)  128 us
    pallas_call x4, Pallas kernels, attend_forward(): pl.pallas_call(functools.partial(attend_forward_kernel, segment, valid),...  111 us
    ppermute x58, waiting for transfers between devices, swap(): return lax.ppermute(value, axis, [(i, i ^ mask) for i in range(size)])  64.9 us
    ppermute x58, starting transfers between devices, swap(): return lax.ppermute(value, axis, [(i, i ^ mask) for i in range(size)])  58.7 us
    convert_element_type x12, other arithmetic, step(): total = total.astype(BF16)  22.3 us
  transfers between devices with their start and end apart: 58, of which 17 were waited for; matrix products, arithmetic and copies ran while one was open for 26% of the time, Pallas kernels for 28%

profile of v4, /device:TPU:0, one launch (start us, length us, event | category | flops | bytes accessed | tf_op | source)
XLA Modules:
  0.0 1019.3 jit_solution(5782850277139503121)
XLA Ops:
  10.8 3.9 collective-permute-start.8
  15.2 6.1 reshape.539
  21.3 3.6 convert_reduce_fusion.4
  28.6 6.1 reshape.546
  41.1 3.7 collective-permute-start.17
  50.1 3.5 collective-permute-done.5
  54.9 11.7 %collective-permute-done.6 = bf16[1,64,2048]{2,1,0:T(8,128)(2,1)S(1)} collective-permute-done((bf16[1,64,2048]{2,1,0:T(8,128)(2,1)S(1)}, bf16[1,64,2048]{2,1,0:T(8,128)(2,1)S(1)}, u32[]{:S(2)}, u32[]{:S(2)}) %collective-permute-start.6) | collective-permute-done | bytes 262176 | tf_op jit(solution)/shard_map/ppermute | solution.py:50
  73.4 4.7 collective-permute-done.9
  82.1 8.0 fusion.22
  90.1 12.0 %collective-permute-done.10 = bf16[8,32,2048]{2,1,0:T(8,128)(2,1)S(1)} collective-permute-done((bf16[8,32,2048]{2,1,0:T(8,128)(2,1)S(1)}, bf16[8,32,2048]{2,1,0:T(8,128)(2,1)S(1)}, u32[]{:S(2)}, u32[]{:S(2)}) %collective-permute-start.10) | collective-permute-done | bytes 1048608 | tf_op jit(solution)/shard_map/ppermute | solution.py:50
  104.3 4.1 fusion.8.refs_1_
  112.9 7.4 shard_map.296
  120.3 14.7 %add_convert_fusion.1 = bf16[2816,1536]{1,0:T(8,128)(2,1)} fusion(bf16[2816,1024]{1,0:T(8,128)(2,1)} %fusion.22, bf16[1024,1536]{1,0:T(8,128)(2,1)} %get-tuple-element.62, f32[1536]{0:T(1024)S(1)} %add.453), kind=kOutput, calls=%fused_computation.5 | convolution fusion | flops 8867020800 | bytes 17569792 | tf_op jit(solution)/shard_map/dot_general | solution.py:22
  135.1 11.2 %add_convert_fusion = bf16[2816,1536]{1,0:T(8,128)(2,1)} fusion(bf16[2816,1024]{1,0:T(8,128)(2,1)S(1)} %bitcast.173, bf16[1024,1536]{1,0:T(8,128)(2,1)S(1)} %copy-done.65, f32[1536]{0:T(1024)S(1)} %add.456), kind=kOutput, calls=%fused_computation.4 | convolution fusion | flops 8867020800 | bytes 17569792 | tf_op jit(solution)/shard_map/dot_general | solution.py:22
  148.9 27.6 %shard_map.298 = (bf16[2,1408,1024]{2,1,0:T(8,128)(2,1)}, f32[2,1408,1024]{2,1,0:T(8,128)}) custom-call(s32[1]{0:T(128)} %constant.71.clone.1.ticket_ref, bf16[2,1408,1536]{2,1,0:T(8,128)(2,1)} %bitcast.164, bf16[2,1408,1536]{2,1,0:T(8,128)(2,1)} %bitcast.165, bf16[4,32,4096]{2,1,0:T(8,128)(2,1)} %get-tuple-element.64.rest_0_, ...), custom_call_target="tpu_custom_call" | custom-call | flops 16240345088 | bytes 11534336 | tf_op jit(solution)/shard_map/pallas_call | solution.py:497
  182.2 27.7 %shard_map.300 = (bf16[2,1408,1024]{2,1,0:T(8,128)(2,1)}, f32[2,1408,1024]{2,1,0:T(8,128)}) custom-call(s32[1]{0:T(128)} %constant.71.clone.1.ticket_ref, bf16[2,1408,1536]{2,1,0:T(8,128)(2,1)} %bitcast.166, bf16[2,1408,1536]{2,1,0:T(8,128)(2,1)} %bitcast.167, ...), custom_call_target="tpu_custom_call", output_to_operand_aliasing={{0}: (3, {}), {1}: (4, {})} | custom-call | flops 16240345088 | bytes 11534336 | tf_op jit(solution)/shard_map/pallas_call | solution.py:497
  209.9 27.9 %shard_map.301 = (bf16[2,1408,1024]{2,1,0:T(8,128)(2,1)}, f32[2,1408,1024]{2,1,0:T(8,128)}) custom-call(s32[1]{0:T(128)} %constant.71.clone.1.ticket_ref, bf16[2,1408,1536]{2,1,0:T(8,128)(2,1)} %bitcast.155, bf16[2,1408,1536]{2,1,0:T(8,128)(2,1)} %bitcast.156, ...), custom_call_target="tpu_custom_call", output_to_operand_aliasing={{0}: (3, {}), {1}: (4, {})} | custom-call | flops 16240345088 | bytes 11534336 | tf_op jit(solution)/shard_map/pallas_call | solution.py:497
  243.2 27.6 %shard_map.303 = (bf16[2,1408,1024]{2,1,0:T(8,128)(2,1)}, f32[2,1408,1024]{2,1,0:T(8,128)}) custom-call(s32[1]{0:T(128)} %constant.71.clone.1.ticket_ref, bf16[2,1408,1536]{2,1,0:T(8,128)(2,1)} %bitcast.157, bf16[2,1408,1536]{2,1,0:T(8,128)(2,1)} %bitcast.158, ...), custom_call_target="tpu_custom_call", output_to_operand_aliasing={{0}: (3, {}), {1}: (4, {})} | custom-call | flops 16240345088 | bytes 11534336 | tf_op jit(solution)/shard_map/pallas_call | solution.py:497
  271.3 18.8 %fusion.72 = (f32[2816]{0:T(1024)S(1)}, f32[2816,1024]{1,0:T(8,128)S(1)}, f32[2816,1024]{1,0:T(8,128)}) fusion(f32[1024]{0:T(1024)S(1)} %add.463, f32[1024]{0:T(1024)S(1)} %mul.187, bf16[2,1370,1024]{2,1,0:T(8,128)(2,1)} %reshape.539, bf16[2816,1024]{1,0:T(8,128)(2,1)} %bitcast.150, bf16[1024,1024]{1,0:T(8,128)(2,1)S(1)} %copy-done.66), kind=kOutput, calls=%fused_computation.217 | convolution fusion | flops 5919994880 | bytes 36563968 | tf_op jit(solution)/shard_map/dot_general | solution.py:22
  294.3 4.1 add_convert_fusion.3.refs_0_
  298.4 17.9 %shard_map.304 = (bf16[1024,4096]{1,0:T(8,128)(2,1)}, bf16[1024,4096]{1,0:T(8,128)(2,1)}) custom-call(s32[3,16]{1,0:T(4,128)} %add_add_fusion.1.tables_ref, bf16[16,32,4096]{2,1,0:T(8,128)(2,1)} %get-tuple-element.74.rest_2_.own_a, bf16[16,32,4096]{2,1,0:T(8,128)(2,1)} %collective-permute-done.22.far_a, ...), custom_call_target="tpu_custom_call" | custom-call | tf_op jit(solution)/shard_map/pallas_call | solution.py:115
  317.0 246.9 %shard_map.305 = (bf16[2816,1024]{1,0:T(8,128)(2,1)}, bf16[2816,1024]{1,0:T(8,128)(2,1)}, bf16[1024,4096]{1,0:T(8,128)(2,1)}, bf16[1024,4096]{1,0:T(8,128)(2,1)}, f32[8,4096]{1,0:T(8,128)}) custom-call(bf16[2816,1024]{1,0:T(8,128)(2,1)} %add_convert_fusion.3.refs_0_, bf16[2816,1024]{1,0:T(8,128)(2,1)} %fusion.8.refs_1_, ...), custom_call_target="tpu_custom_call" | custom-call | flops 141733920768 | bytes 56623104 | tf_op jit(solution)/shard_map/pallas_call | solution.py:694
  564.0 9.8 fusion.7
  573.8 18.5 %shard_map.306 = (bf16[16,32,4096]{2,1,0:T(8,128)(2,1)}, bf16[16,32,4096]{2,1,0:T(8,128)(2,1)}, bf16[16,32,4096]{2,1,0:T(8,128)(2,1)}, bf16[16,32,4096]{2,1,0:T(8,128)(2,1)}) custom-call(s32[3,16]{1,0:T(4,128)} %add_add_fusion.1.tables_ref, bf16[1024,4096]{1,0:T(8,128)(2,1)} %get-tuple-element.83.refs_0_, bf16[1024,4096]{1,0:T(8,128)(2,1)} %get-tuple-element.84.refs_1_), custom_call_target="tpu_custom_call" | custom-call | tf_op jit(solution)/shard_map/pallas_call | solution.py:232
  592.3 17.9 %multiply_reduce_fusion = (f32[1024]{0:T(1024)S(1)}, f32[1024]{0:T(1024)S(1)}, f32[2816,1024]{1,0:T(8,128)}, bf16[2816,1024]{1,0:T(8,128)(2,1)S(1)}, f32[1024]{0:T(1024)S(1)}) fusion(f32[2816,1024]{1,0:T(8,128)} %get-tuple-element.188, f32[1024]{0:T(1024)S(1)} %copy-done.60, f32[2816]{0:T(1024)S(1)} %broadcast_multiply_fusion.2, f32[2816,1024]{1,0:T(8,128)} %copy-done, ...), kind=kLoop, calls=%fused_computation.45 | loop fusion | flops 60552192 | bytes 57589760 | tf_op jit(solution)/shard_map/reduce_sum | solution.py:937
  613.3 6.3 reshape.548
  623.6 11.3 %convolution_convert_fusion = bf16[2816,1024]{1,0:T(8,128)(2,1)} fusion(bf16[1024,1024]{1,0:T(8,128)(2,1)} %get-tuple-element.77, f32[2816,1024]{1,0:T(8,128)} %get-tuple-element.127, f32[1024]{0:T(1024)S(1)} %copy-done.64), kind=kOutput, calls=%fused_computation.58 | convolution fusion | flops 5914230784 | bytes 19402752 | tf_op jit(solution)/shard_map/dot_general | solution.py:22
  636.4 9.5 fusion.32.refs_1_
  646.0 3.7 add_convert_fusion.4
  653.4 3.7 add_convert_fusion.5
  661.0 40.5 %shard_map.307.refs_2_.rest_0_ = bf16[2,1408,1536]{2,1,0:T(8,128)(2,1)} custom-call(s32[1]{0:T(128)} %constant.71.clone.1.ticket_ref, bf16[2,1408,1536]{2,1,0:T(8,128)(2,1)} %bitcast.168, bf16[2,1408,1536]{2,1,0:T(8,128)(2,1)} %bitcast.169, bf16[2,1408,1024]{2,1,0:T(8,128)(2,1)} %get-tuple-element.76.mixed_ref, bf16[2,1408,1024]{2,1,0:T(8,128)(2,1)} %bitcast.190, ...), custom_call_target="tpu_custom_call" | custom-call | flops 40600862720 | bytes 11534336 | tf_op jit(solution)/shard_map/pallas_call | solution.py:547
  711.7 40.7 %shard_map.309.refs_2_ = bf16[2,1408,1536]{2,1,0:T(8,128)(2,1)} custom-call(s32[1]{0:T(128)} %constant.71.clone.1.ticket_ref, bf16[2,1408,1536]{2,1,0:T(8,128)(2,1)} %bitcast.170, bf16[2,1408,1536]{2,1,0:T(8,128)(2,1)} %bitcast.171, bf16[2,1408,1024]{2,1,0:T(8,128)(2,1)} %get-tuple-element.76.mixed_ref, ...), custom_call_target="tpu_custom_call", output_to_operand_aliasing={{}: (6, {})} | custom-call | flops 40600862720 | bytes 11534336 | tf_op jit(solution)/shard_map/pallas_call | solution.py:547
  753.1 15.6 %fusion.89.rest_8_.rest_6_ = f32[2816,1024]{1,0:T(8,128)} fusion(bf16[2816,1536]{1,0:T(8,128)(2,1)} %bitcast.147, bf16[1024,1536]{1,0:T(8,128)(2,1)} %get-tuple-element.63), kind=kOutput, calls=%fused_computation.234 | convolution fusion | flops 8858370048 | bytes 23330816 | tf_op jit(solution)/shard_map/dot_general | solution.py:22
  768.7 11.0 %bitcast_convert_fusion.1.refs_0_ = bf16[1024,1536]{1,0:T(8,128)(2,1)} fusion(bf16[2,1408,1536]{2,1,0:T(8,128)(2,1)S(1)} %copy-done.4, f32[1024]{0:T(1024)S(1)} %copy-done.58, f32[1024]{0:T(1024)S(1)} %copy-done.49, f32[2,1408]{1,0:T(2,128)S(1)} %copy-done.45, f32[2,1408]{1,0:T(2,128)S(1)} %copy-done.40, bf16[2,1370,1024]{2,1,0:T(8,128)(2,1)S(1)} %bitcast.141), kind=kOutput, calls=%fused_computation.56 | convolution fusion | flops 8877244416 | bytes 17438720 | tf_op jit(solution)/shard_map/dot_general | solution.py:22
  779.7 5.4 shard_map.311
  785.6 4.7 convert_reduce_fusion.1
  794.5 4.3 collective-permute-start.32
  799.4 40.6 %shard_map.312.refs_3_.rest_0_ = bf16[2,1408,1536]{2,1,0:T(8,128)(2,1)} custom-call(s32[1]{0:T(128)} %constant.71.clone.1.ticket_ref, bf16[2,1408,1536]{2,1,0:T(8,128)(2,1)} %bitcast.159, bf16[2,1408,1536]{2,1,0:T(8,128)(2,1)} %bitcast.160, bf16[2,1408,1024]{2,1,0:T(8,128)(2,1)} %get-tuple-element.76.mixed_ref, bf16[2,1408,1024]{2,1,0:T(8,128)(2,1)} %bitcast.192, ...), custom_call_target="tpu_custom_call" | custom-call | flops 40600862720 | bytes 11534336 | tf_op jit(solution)/shard_map/pallas_call | solution.py:547
  849.4 40.7 %shard_map.314.refs_2_ = bf16[2,1408,1536]{2,1,0:T(8,128)(2,1)} custom-call(s32[1]{0:T(128)} %constant.71.clone.1.ticket_ref, bf16[2,1408,1536]{2,1,0:T(8,128)(2,1)} %bitcast.161, bf16[2,1408,1536]{2,1,0:T(8,128)(2,1)} %bitcast.162, bf16[2,1408,1024]{2,1,0:T(8,128)(2,1)} %get-tuple-element.76.mixed_ref, ...), custom_call_target="tpu_custom_call", output_to_operand_aliasing={{}: (6, {})} | custom-call | flops 40600862720 | bytes 11534336 | tf_op jit(solution)/shard_map/pallas_call | solution.py:547
  890.1 15.0 %bitcast_convert_fusion.refs_0_ = bf16[1024,1536]{1,0:T(8,128)(2,1)} fusion(bf16[2,1408,1536]{2,1,0:T(8,128)(2,1)} %shard_map.314.refs_2_, f32[1024]{0:T(1024)S(1)} %copy-done.58, f32[1024]{0:T(1024)S(1)} %copy-done.49, f32[2,1408]{1,0:T(2,128)S(1)} %copy-done.45, f32[2,1408]{1,0:T(2,128)S(1)} %copy-done.40, bf16[2,1370,1024]{2,1,0:T(8,128)(2,1)S(1)} %bitcast.143), kind=kOutput, calls=%fused_computation.55 | convolution fusion | flops 8877244416 | bytes 17438720 | tf_op jit(solution)/shard_map/dot_general | solution.py:22
  907.0 3.9 shard_map.315
  917.0 6.8 collective-permute-done.45
  926.2 3.7 collective-permute-start.50
  936.3 21.0 %fusion.28 = (f32[1024]{0:T(1024)S(1)}, f32[2816]{0:T(1024)S(1)}, f32[2816]{0:T(1024)S(1)}, f32[1024]{0:T(1024)S(1)}, f32[2816,1024]{1,0:T(8,128)}) fusion(f32[2816]{0:T(1024)S(1)} %copy-done.38, f32[2816]{0:T(1024)S(1)} %copy-done.36, bf16[2,1370,1024]{2,1,0:T(8,128)(2,1)} %reshape.539, f32[1024]{0:T(1024)S(1)} %add_add_fusion, ...), kind=kOutput, calls=%fused_computation.44 | convolution fusion | flops 8890081280 | bytes 40534016 | tf_op jit(solution)/shard_map/dot_general | solution.py:22
  959.7 3.8 collective-permute-done.37
  965.4 10.6 %fusion.27 = bf16[2816,1024]{1,0:T(8,128)(2,1)S(1)} fusion(f32[2816,1024]{1,0:T(8,128)} %get-tuple-element.127, f32[2816,1024]{1,0:T(8,128)} %get-tuple-element.189, f32[2816]{0:T(1024)S(1)} %broadcast_multiply_fusion, f32[2816]{0:T(1024)S(1)} %broadcast_multiply_fusion.1, f32[1024]{0:T(1024)S(1)} %add_add_fusion, f32[2816]{0:T(1024)S(1)} %copy-done.38, ...), kind=kLoop, calls=%fused_computation.43 | loop fusion | flops 28835840 | bytes 34496512 | tf_op jit(solution)/shard_map/convert_element_type | solution.py:915
  979.2 6.2 reshape.553
  991.5 4.9 collective-permute-done.48
  (423 shorter events, 153.5 us)
Async XLA Ops:
  2.9 37.6 %collective-permute-start = (f32[1,16,128]{2,1,0:T(8,128)S(1)}, f32[1,16,128]{2,1,0:T(8,128)S(1)}, u32[]{:S(2)}, u32[]{:S(2)}) collective-permute-start(f32[1,16,128]{2,1,0:T(8,128)S(1)} %bitcast_convert_fusion.2), channel_id=1, source_target_pairs={{0,8},{2,10},{4,12},{6,14},{8,0},{10,2},{12,4},{14,6},{16,24},{18,... | collective-permute-start | bytes 24584 | tf_op jit(solution)/shard_map/ppermute | solution.py:50
  6.0 35.1 %collective-permute-start.1 = (f32[1,16,128]{2,1,0:T(8,128)S(1)}, f32[1,16,128]{2,1,0:T(8,128)S(1)}, u32[]{:S(2)}, u32[]{:S(2)}) collective-permute-start(f32[1,16,128]{2,1,0:T(8,128)S(1)} %bitcast_convert_fusion.2), channel_id=1, source_target_pairs={{0,16},{2,18},{4,20},{6,22},{8,24},{10,26},{12,28},{14,30},{16,0},... | collective-permute-start | bytes 24584 | tf_op jit(solution)/shard_map/ppermute | solution.py:50
  8.6 36.3 %collective-permute-start.2 = (f32[1,16,128]{2,1,0:T(8,128)S(1)}, f32[1,16,128]{2,1,0:T(8,128)S(1)}, u32[]{:S(2)}, u32[]{:S(2)}) collective-permute-start(f32[1,16,128]{2,1,0:T(8,128)S(1)} %bitcast_convert_fusion.2), channel_id=1, source_target_pairs={{0,24},{2,26},{4,28},{6,30},{8,16},{10,18},{12,20},{14,22},{16,8},... | collective-permute-start | bytes 24584 | tf_op jit(solution)/shard_map/ppermute | solution.py:50
  10.8 43.5 %collective-permute-start.8 = (bf16[1,64,2048]{2,1,0:T(8,128)(2,1)S(1)}, bf16[1,64,2048]{2,1,0:T(8,128)(2,1)S(1)}, u32[]{:S(2)}, u32[]{:S(2)}) collective-permute-start(bf16[1,64,2048]{2,1,0:T(8,128)(2,1)S(1)} %maximum_bitcast_fusion.1), channel_id=1, source_target_pairs={{0,24},{2,26},{4,28},{6,30},{8,16},{10,18},{12,20},{14,22},{16,8},... | collective-permute-start | bytes 786440 | tf_op jit(solution)/shard_map/ppermute | solution.py:50
  14.6 40.2 %collective-permute-start.7 = (bf16[1,64,2048]{2,1,0:T(8,128)(2,1)S(1)}, bf16[1,64,2048]{2,1,0:T(8,128)(2,1)S(1)}, u32[]{:S(2)}, u32[]{:S(2)}) collective-permute-start(bf16[1,64,2048]{2,1,0:T(8,128)(2,1)S(1)} %maximum_bitcast_fusion.1), channel_id=1, source_target_pairs={{0,8},{2,10},{4,12},{6,14},{8,0},{10,2},{12,4},{14,6},{16,24},{18,... | collective-permute-start | bytes 786440 | tf_op jit(solution)/shard_map/ppermute | solution.py:50
  40.5 26.1 %collective-permute-start.6 = (bf16[1,64,2048]{2,1,0:T(8,128)(2,1)S(1)}, bf16[1,64,2048]{2,1,0:T(8,128)(2,1)S(1)}, u32[]{:S(2)}, u32[]{:S(2)}) collective-permute-start(bf16[1,64,2048]{2,1,0:T(8,128)(2,1)S(1)} %maximum_bitcast_fusion.1), channel_id=1, source_target_pairs={{0,16},{2,18},{4,20},{6,22},{8,24},{10,26},{12,28},{14,30},{16,0},... | collective-permute-start | bytes 786440 | tf_op jit(solution)/shard_map/ppermute | solution.py:50
  41.1 67.4 %collective-permute-start.17 = (bf16[1,64,4096]{2,1,0:T(8,128)(2,1)S(1)}, bf16[1,64,4096]{2,1,0:T(8,128)(2,1)}, u32[]{:S(2)}, u32[]{:S(2)}) collective-permute-start(bf16[1,64,4096]{2,1,0:T(8,128)(2,1)S(1)} %fusion.38), channel_id=1, source_target_pairs={{0,24},{2,26},{4,28},{6,30},{8,16},{10,18},{12,20},{14,22},{16,8},... | collective-permute-start | bytes 1572872 | tf_op jit(solution)/shard_map/ppermute | solution.py:50
  53.6 54.8 %collective-permute-start.16 = (bf16[1,64,4096]{2,1,0:T(8,128)(2,1)S(1)}, bf16[1,64,4096]{2,1,0:T(8,128)(2,1)}, u32[]{:S(2)}, u32[]{:S(2)}) collective-permute-start(bf16[1,64,4096]{2,1,0:T(8,128)(2,1)S(1)} %fusion.38), channel_id=1, source_target_pairs={{0,8},{2,10},{4,12},{6,14},{8,0},{10,2},{12,4},{14,6},{16,24},{18,... | collective-permute-start | bytes 1572872 | tf_op jit(solution)/shard_map/ppermute | solution.py:50
  54.2 54.2 %collective-permute-start.15 = (bf16[1,64,4096]{2,1,0:T(8,128)(2,1)S(1)}, bf16[1,64,4096]{2,1,0:T(8,128)(2,1)}, u32[]{:S(2)}, u32[]{:S(2)}) collective-permute-start(bf16[1,64,4096]{2,1,0:T(8,128)(2,1)S(1)} %fusion.38), channel_id=1, source_target_pairs={{0,16},{2,18},{4,20},{6,22},{8,24},{10,26},{12,28},{14,30},{16,0},... | collective-permute-start | bytes 1572872 | tf_op jit(solution)/shard_map/ppermute | solution.py:50
  66.8 11.3 %collective-permute-start.9 = (bf16[4,32,2048]{2,1,0:T(8,128)(2,1)S(1)}, bf16[4,32,2048]{2,1,0:T(8,128)(2,1)S(1)}, u32[]{:S(2)}, u32[]{:S(2)}) collective-permute-start(bf16[4,32,2048]{2,1,0:T(8,128)(2,1)S(1)} %get-tuple-element.153), channel_id=1, source_target_pairs={{0,4},{2,6},{4,0},{6,2},{8,12},{10,14},{12,8},{14,10},{16,20},{18,... | collective-permute-start | bytes 1572872 | tf_op jit(solution)/shard_map/ppermute | solution.py:50
  68.7 13.1 %collective-permute-start.12 = (bf16[4,32,2048]{2,1,0:T(8,128)(2,1)S(1)}, bf16[4,32,2048]{2,1,0:T(8,128)(2,1)S(1)}, u32[]{:S(2)}, u32[]{:S(2)}) collective-permute-start(bf16[4,32,2048]{2,1,0:T(8,128)(2,1)S(1)} %get-tuple-element.152), channel_id=1, source_target_pairs={{0,1},{1,0},{2,3},{3,2},{4,5},{5,4},{6,7},{7,6},{8,9},{9,8},{10,11... | collective-permute-start | bytes 1572872 | tf_op jit(solution)/shard_map/ppermute | solution.py:50
  78.2 24.0 %collective-permute-start.10 = (bf16[8,32,2048]{2,1,0:T(8,128)(2,1)S(1)}, bf16[8,32,2048]{2,1,0:T(8,128)(2,1)S(1)}, u32[]{:S(2)}, u32[]{:S(2)}) collective-permute-start(bf16[8,32,2048]{2,1,0:T(8,128)(2,1)S(1)} %pad_maximum_fusion.8), channel_id=1, source_target_pairs={{0,1},{1,0},{2,3},{3,2},{4,5},{5,4},{6,7},{7,6},{8,9},{9,8},{10,11... | collective-permute-start | bytes 3145736 | tf_op jit(solution)/shard_map/ppermute | solution.py:50
  82.0 20.5 %collective-permute-start.13 = (bf16[8,32,2048]{2,1,0:T(8,128)(2,1)S(1)}, bf16[8,32,2048]{2,1,0:T(8,128)(2,1)S(1)}, u32[]{:S(2)}, u32[]{:S(2)}) collective-permute-start(bf16[8,32,2048]{2,1,0:T(8,128)(2,1)S(1)} %pad_maximum_fusion.9), channel_id=1, source_target_pairs={{0,4},{2,6},{4,0},{6,2},{8,12},{10,14},{12,8},{14,10},{16,20},{18,... | collective-permute-start | bytes 3145736 | tf_op jit(solution)/shard_map/ppermute | solution.py:50
  102.4 9.2 collective-permute-start.11
  104.2 7.4 collective-permute-start.14
  146.8 29.7 %collective-permute-start.18 = (bf16[4,32,4096]{2,1,0:T(8,128)(2,1)}, bf16[4,32,4096]{2,1,0:T(8,128)(2,1)S(1)}, u32[]{:S(2)}, u32[]{:S(2)}) collective-permute-start(bf16[4,32,4096]{2,1,0:T(8,128)(2,1)} %get-tuple-element.64.rest_0_), channel_id=1, source_target_pairs={{0,4},{2,6},{4,0},{6,2},{8,12},{10,14},{12,8},{14,10},{16,20},{18,... | collective-permute-start | bytes 3145736 | tf_op jit(solution)/shard_map/ppermute | solution.py:50
  147.4 30.7 %collective-permute-start.19 = (bf16[4,32,4096]{2,1,0:T(8,128)(2,1)}, bf16[4,32,4096]{2,1,0:T(8,128)(2,1)S(1)}, u32[]{:S(2)}, u32[]{:S(2)}) collective-permute-start(bf16[4,32,4096]{2,1,0:T(8,128)(2,1)} %get-tuple-element.65.rest_1_), channel_id=1, source_target_pairs={{0,1},{1,0},{2,3},{3,2},{4,5},{5,4},{6,7},{7,6},{8,9},{9,8},{10,11... | collective-permute-start | bytes 3145736 | tf_op jit(solution)/shard_map/ppermute | solution.py:50
  180.1 57.7 %collective-permute-start.20 = (bf16[8,32,4096]{2,1,0:T(8,128)(2,1)}, bf16[8,32,4096]{2,1,0:T(8,128)(2,1)S(1)}, u32[]{:S(2)}, u32[]{:S(2)}) collective-permute-start(bf16[8,32,4096]{2,1,0:T(8,128)(2,1)} %get-tuple-element.68.rest_2_), channel_id=1, source_target_pairs={{0,1},{1,0},{2,3},{3,2},{4,5},{5,4},{6,7},{7,6},{8,9},{9,8},{10,11... | collective-permute-start | bytes 6291464 | tf_op jit(solution)/shard_map/ppermute | solution.py:50
  180.7 59.6 %collective-permute-start.21 = (bf16[8,32,4096]{2,1,0:T(8,128)(2,1)}, bf16[8,32,4096]{2,1,0:T(8,128)(2,1)S(1)}, u32[]{:S(2)}, u32[]{:S(2)}) collective-permute-start(bf16[8,32,4096]{2,1,0:T(8,128)(2,1)} %get-tuple-element.69.rest_3_), channel_id=1, source_target_pairs={{0,4},{2,6},{4,0},{6,2},{8,12},{10,14},{12,8},{14,10},{16,20},{18,... | collective-permute-start | bytes 6291464 | tf_op jit(solution)/shard_map/ppermute | solution.py:50
  243.2 55.2 %collective-permute-start.22 = (bf16[16,32,4096]{2,1,0:T(8,128)(2,1)}, bf16[16,32,4096]{2,1,0:T(8,128)(2,1)}, u32[]{:S(2)}, u32[]{:S(2)}) collective-permute-start(bf16[16,32,4096]{2,1,0:T(8,128)(2,1)} %get-tuple-element.74.rest_2_.own_a), channel_id=1, source_target_pairs={{0,2},{2,0},{4,6},{6,4},{8,10},{10,8},{12,14},{14,12},{16,18},{18,... | collective-permute-start | bytes 12582920 | tf_op jit(solution)/shard_map/ppermute | solution.py:50
  270.8 27.6 %collective-permute-start.23 = (bf16[16,32,4096]{2,1,0:T(8,128)(2,1)}, bf16[16,32,4096]{2,1,0:T(8,128)(2,1)}, u32[]{:S(2)}, u32[]{:S(2)}) collective-permute-start(bf16[16,32,4096]{2,1,0:T(8,128)(2,1)} %get-tuple-element.75.rest_3_.own_b), channel_id=1, source_target_pairs={{0,2},{2,0},{4,6},{6,4},{8,10},{10,8},{12,14},{14,12},{16,18},{18,... | collective-permute-start | bytes 12582920 | tf_op jit(solution)/shard_map/ppermute | solution.py:50
  592.3 53.7 %collective-permute-start.25 = (bf16[16,32,4096]{2,1,0:T(8,128)(2,1)}, bf16[16,32,4096]{2,1,0:T(8,128)(2,1)}, u32[]{:S(2)}, u32[]{:S(2)}) collective-permute-start(bf16[16,32,4096]{2,1,0:T(8,128)(2,1)} %get-tuple-element.88), channel_id=1, source_target_pairs={{0,2},{2,0},{4,6},{6,4},{8,10},{10,8},{12,14},{14,12},{16,18},{18,... | collective-permute-start | bytes 12582920 | tf_op jit(solution)/shard_map/ppermute | solution.py:50
  619.6 33.0 %collective-permute-start.24 = (bf16[16,32,4096]{2,1,0:T(8,128)(2,1)}, bf16[16,32,4096]{2,1,0:T(8,128)(2,1)}, u32[]{:S(2)}, u32[]{:S(2)}) collective-permute-start(bf16[16,32,4096]{2,1,0:T(8,128)(2,1)} %get-tuple-element.86), channel_id=1, source_target_pairs={{0,2},{2,0},{4,6},{6,4},{8,10},{10,8},{12,14},{14,12},{16,18},{18,... | collective-permute-start | bytes 12582920 | tf_op jit(solution)/shard_map/ppermute | solution.py:50
  652.1 49.9 %collective-permute-start.27 = (bf16[8,32,4096]{2,1,0:T(8,128)(2,1)}, bf16[8,32,4096]{2,1,0:T(8,128)(2,1)S(1)}, u32[]{:S(2)}, u32[]{:S(2)}) collective-permute-start(bf16[8,32,4096]{2,1,0:T(8,128)(2,1)} %get-tuple-element.132.rest_3_), channel_id=1, source_target_pairs={{0,4},{2,6},{4,0},{6,2},{8,12},{10,14},{12,8},{14,10},{16,20},{18,... | collective-permute-start | bytes 6291464 | tf_op jit(solution)/shard_map/ppermute | solution.py:50
  659.4 47.9 %collective-permute-start.26 = (bf16[8,32,4096]{2,1,0:T(8,128)(2,1)}, bf16[8,32,4096]{2,1,0:T(8,128)(2,1)}, u32[]{:S(2)}, u32[]{:S(2)}) collective-permute-start(bf16[8,32,4096]{2,1,0:T(8,128)(2,1)} %get-tuple-element.134.rest_2_), channel_id=1, source_target_pairs={{0,1},{1,0},{2,3},{3,2},{4,5},{5,4},{6,7},{7,6},{8,9},{9,8},{10,11... | collective-permute-start | bytes 6291464 | tf_op jit(solution)/shard_map/ppermute | solution.py:50
  706.1 84.3 %collective-permute-start.29 = (bf16[4,32,4096]{2,1,0:T(8,128)(2,1)}, bf16[4,32,4096]{2,1,0:T(8,128)(2,1)}, u32[]{:S(2)}, u32[]{:S(2)}) collective-permute-start(bf16[4,32,4096]{2,1,0:T(8,128)(2,1)} %get-tuple-element.140.rest_4_), channel_id=1, source_target_pairs={{0,1},{1,0},{2,3},{3,2},{4,5},{5,4},{6,7},{7,6},{8,9},{9,8},{10,11... | collective-permute-start | bytes 3145736 | tf_op jit(solution)/shard_map/ppermute | solution.py:50
  711.2 80.7 %collective-permute-start.28 = (bf16[4,32,4096]{2,1,0:T(8,128)(2,1)}, bf16[4,32,4096]{2,1,0:T(8,128)(2,1)}, u32[]{:S(2)}, u32[]{:S(2)}) collective-permute-start(bf16[4,32,4096]{2,1,0:T(8,128)(2,1)} %get-tuple-element.142.rest_3_), channel_id=1, source_target_pairs={{0,4},{2,6},{4,0},{6,2},{8,12},{10,14},{12,8},{14,10},{16,20},{18,... | collective-permute-start | bytes 3145736 | tf_op jit(solution)/shard_map/ppermute | solution.py:50
  785.1 55.5 %collective-permute-start.33 = (bf16[16,32,1280]{2,1,0:T(8,128)(2,1)}, bf16[16,32,1280]{2,1,0:T(8,128)(2,1)}, u32[]{:S(2)}, u32[]{:S(2)}) collective-permute-start(bf16[16,32,1280]{2,1,0:T(8,128)(2,1)} %get-tuple-element.95.rest_6_), channel_id=1, source_target_pairs={{0,2},{2,0},{4,6},{6,4},{8,10},{10,8},{12,14},{14,12},{16,18},{18,... | collective-permute-start | bytes 3932168 | tf_op jit(solution)/shard_map/ppermute | solution.py:50
  785.1 59.9 %collective-permute-start.34 = (bf16[16,32,1280]{2,1,0:T(8,128)(2,1)}, bf16[16,32,1280]{2,1,0:T(8,128)(2,1)S(1)}, u32[]{:S(2)}, u32[]{:S(2)}) collective-permute-start(bf16[16,32,1280]{2,1,0:T(8,128)(2,1)} %get-tuple-element.96.rest_7_), channel_id=1, source_target_pairs={{0,2},{2,0},{4,6},{6,4},{8,10},{10,8},{12,14},{14,12},{16,18},{18,... | collective-permute-start | bytes 3932168 | tf_op jit(solution)/shard_map/ppermute | solution.py:50
  794.5 53.6 %collective-permute-start.32 = (bf16[1,64,4096]{2,1,0:T(8,128)(2,1)}, bf16[1,64,4096]{2,1,0:T(8,128)(2,1)S(1)}, u32[]{:S(2)}, u32[]{:S(2)}) collective-permute-start(bf16[1,64,4096]{2,1,0:T(8,128)(2,1)} %get-tuple-element.136.rest_3_), channel_id=1, source_target_pairs={{0,24},{2,26},{4,28},{6,30},{8,16},{10,18},{12,20},{14,22},{16,8},... | collective-permute-start | bytes 1572872 | tf_op jit(solution)/shard_map/ppermute | solution.py:50
  798.8 49.3 %collective-permute-start.31 = (bf16[1,64,4096]{2,1,0:T(8,128)(2,1)}, bf16[1,64,4096]{2,1,0:T(8,128)(2,1)S(1)}, u32[]{:S(2)}, u32[]{:S(2)}) collective-permute-start(bf16[1,64,4096]{2,1,0:T(8,128)(2,1)} %get-tuple-element.139.rest_2_), channel_id=1, source_target_pairs={{0,8},{2,10},{4,12},{6,14},{8,0},{10,2},{12,4},{14,6},{16,24},{18,... | collective-permute-start | bytes 1572872 | tf_op jit(solution)/shard_map/ppermute | solution.py:50
  798.8 49.3 %collective-permute-start.30 = (bf16[1,64,4096]{2,1,0:T(8,128)(2,1)S(1)}, bf16[1,64,4096]{2,1,0:T(8,128)(2,1)S(1)}, u32[]{:S(2)}, u32[]{:S(2)}) collective-permute-start(bf16[1,64,4096]{2,1,0:T(8,128)(2,1)S(1)} %get-tuple-element.138.rest_1_), channel_id=1, source_target_pairs={{0,16},{2,18},{4,20},{6,22},{8,24},{10,26},{12,28},{14,30},{16,0},... | collective-permute-start | bytes 1572872 | tf_op jit(solution)/shard_map/ppermute | solution.py:50
  844.0 68.8 %collective-permute-start.44 = (bf16[8,32,1280]{2,1,0:T(8,128)(2,1)}, bf16[8,32,1280]{2,1,0:T(8,128)(2,1)}, u32[]{:S(2)}, u32[]{:S(2)}) collective-permute-start(bf16[8,32,1280]{2,1,0:T(8,128)(2,1)} %get-tuple-element.148.rest_4_), channel_id=1, source_target_pairs={{0,1},{1,0},{2,3},{3,2},{4,5},{5,4},{6,7},{7,6},{8,9},{9,8},{10,11... | collective-permute-start | bytes 1966088 | tf_op jit(solution)/shard_map/ppermute | solution.py:50
  846.6 68.1 %collective-permute-start.46 = (bf16[8,32,1280]{2,1,0:T(8,128)(2,1)}, bf16[8,32,1280]{2,1,0:T(8,128)(2,1)}, u32[]{:S(2)}, u32[]{:S(2)}) collective-permute-start(bf16[8,32,1280]{2,1,0:T(8,128)(2,1)} %get-tuple-element.146.rest_5_), channel_id=1, source_target_pairs={{0,4},{2,6},{4,0},{6,2},{8,12},{10,14},{12,8},{14,10},{16,20},{18,... | collective-permute-start | bytes 1966088 | tf_op jit(solution)/shard_map/ppermute | solution.py:50
  911.0 18.9 %collective-permute-start.36 = (bf16[16,32,768]{2,1,0:T(8,128)(2,1)}, bf16[16,32,768]{2,1,0:T(8,128)(2,1)}, u32[]{:S(2)}, u32[]{:S(2)}) collective-permute-start(bf16[16,32,768]{2,1,0:T(8,128)(2,1)} %get-tuple-element.103), channel_id=1, source_target_pairs={{0,2},{2,0},{4,6},{6,4},{8,10},{10,8},{12,14},{14,12},{16,18},{18,... | collective-permute-start | bytes 2359304 | tf_op jit(solution)/shard_map/ppermute | solution.py:50
  911.0 21.4 %collective-permute-start.35 = (bf16[16,32,768]{2,1,0:T(8,128)(2,1)}, bf16[16,32,768]{2,1,0:T(8,128)(2,1)}, u32[]{:S(2)}, u32[]{:S(2)}) collective-permute-start(bf16[16,32,768]{2,1,0:T(8,128)(2,1)} %get-tuple-element.101), channel_id=1, source_target_pairs={{0,2},{2,0},{4,6},{6,4},{8,10},{10,8},{12,14},{14,12},{16,18},{18,... | collective-permute-start | bytes 2359304 | tf_op jit(solution)/shard_map/ppermute | solution.py:50
  914.1 9.7 collective-permute-start.45
  915.9 9.4 collective-permute-start.47
  926.2 62.0 %collective-permute-start.50 = (bf16[1,64,1280]{2,1,0:T(8,128)(2,1)}, bf16[1,64,1280]{2,1,0:T(8,128)(2,1)}, u32[]{:S(2)}, u32[]{:S(2)}) collective-permute-start(bf16[1,64,1280]{2,1,0:T(8,128)(2,1)} %get-tuple-element.159), channel_id=1, source_target_pairs={{0,24},{2,26},{4,28},{6,30},{8,16},{10,18},{12,20},{14,22},{16,8},... | collective-permute-start | bytes 491528 | tf_op jit(solution)/shard_map/ppermute | solution.py:50
  929.9 61.7 %collective-permute-start.49 = (bf16[1,64,1280]{2,1,0:T(8,128)(2,1)}, bf16[1,64,1280]{2,1,0:T(8,128)(2,1)}, u32[]{:S(2)}, u32[]{:S(2)}) collective-permute-start(bf16[1,64,1280]{2,1,0:T(8,128)(2,1)} %get-tuple-element.160), channel_id=1, source_target_pairs={{0,8},{2,10},{4,12},{6,14},{8,0},{10,2},{12,4},{14,6},{16,24},{18,... | collective-permute-start | bytes 491528 | tf_op jit(solution)/shard_map/ppermute | solution.py:50
  963.5 21.9 %collective-permute-start.40 = (f32[4,16,128]{2,1,0:T(8,128)S(1)}, f32[4,16,128]{2,1,0:T(8,128)S(1)}, u32[]{:S(2)}, u32[]{:S(2)}) collective-permute-start(f32[4,16,128]{2,1,0:T(8,128)S(1)} %get-tuple-element.167), channel_id=1, source_target_pairs={{0,6},{2,4},{4,2},{6,0},{8,14},{10,12},{12,10},{14,8},{16,22},{18,... | collective-permute-start | bytes 98312 | tf_op jit(solution)/shard_map/ppermute | solution.py:50
  963.6 22.5 %collective-permute-start.39 = (f32[4,16,128]{2,1,0:T(8,128)S(1)}, f32[4,16,128]{2,1,0:T(8,128)S(1)}, u32[]{:S(2)}, u32[]{:S(2)}) collective-permute-start(f32[4,16,128]{2,1,0:T(8,128)S(1)} %get-tuple-element.168), channel_id=1, source_target_pairs={{0,4},{2,6},{4,0},{6,2},{8,12},{10,14},{12,8},{14,10},{16,20},{18,... | collective-permute-start | bytes 98312 | tf_op jit(solution)/shard_map/ppermute | solution.py:50
  964.7 22.4 %collective-permute-start.38 = (f32[4,16,128]{2,1,0:T(8,128)S(1)}, f32[4,16,128]{2,1,0:T(8,128)S(1)}, u32[]{:S(2)}, u32[]{:S(2)}) collective-permute-start(f32[4,16,128]{2,1,0:T(8,128)S(1)} %get-tuple-element.166), channel_id=1, source_target_pairs={{0,2},{2,0},{4,6},{6,4},{8,10},{10,8},{12,14},{14,12},{16,18},{18,... | collective-permute-start | bytes 98312 | tf_op jit(solution)/shard_map/ppermute | solution.py:50
  985.4 11.0 %collective-permute-start.48 = (bf16[1,64,1280]{2,1,0:T(8,128)(2,1)S(1)}, bf16[1,64,1280]{2,1,0:T(8,128)(2,1)S(1)}, u32[]{:S(2)}, u32[]{:S(2)}) collective-permute-start(bf16[1,64,1280]{2,1,0:T(8,128)(2,1)S(1)} %get-tuple-element.158), channel_id=1, source_target_pairs={{0,16},{2,18},{4,20},{6,22},{8,24},{10,26},{12,28},{14,30},{16,0},... | collective-permute-start | bytes 491528 | tf_op jit(solution)/shard_map/ppermute | solution.py:50
  986.1 14.0 %collective-permute-start.51 = (bf16[8,32,768]{2,1,0:T(8,128)(2,1)S(1)}, bf16[8,32,768]{2,1,0:T(8,128)(2,1)}, u32[]{:S(2)}, u32[]{:S(2)}) collective-permute-start(bf16[8,32,768]{2,1,0:T(8,128)(2,1)S(1)} %slice.423), channel_id=1, source_target_pairs={{0,1},{1,0},{2,3},{3,2},{4,5},{5,4},{6,7},{7,6},{8,9},{9,8},{10,11... | collective-permute-start | bytes 1179656 | tf_op jit(solution)/shard_map/ppermute | solution.py:50
  987.1 15.2 %collective-permute-start.53 = (bf16[8,32,768]{2,1,0:T(8,128)(2,1)S(1)}, bf16[8,32,768]{2,1,0:T(8,128)(2,1)}, u32[]{:S(2)}, u32[]{:S(2)}) collective-permute-start(bf16[8,32,768]{2,1,0:T(8,128)(2,1)S(1)} %slice.427), channel_id=1, source_target_pairs={{0,4},{2,6},{4,0},{6,2},{8,12},{10,14},{12,8},{14,10},{16,20},{18,... | collective-permute-start | bytes 1179656 | tf_op jit(solution)/shard_map/ppermute | solution.py:50
  988.2 10.1 collective-permute-start.43
  991.5 6.8 collective-permute-start.42
  (88 other events, 2392.1 us)
